TPU v7x, 32 devices: a whole 2x2x4 slice. The times are simulated.
32 devices in a mesh: req: 16 (over z, y, x), tp: 2 (over core).
Axes of the slice: x: 2, y: 2, z: 4, core: 2. Of those that a mesh axis runs over, the one named last changes fastest.
Arguments:
- tokens: bfloat16 [4096, 2048], P('req', 'tp'), may hold values from -1100 to 1100
- norm_gain: bfloat16 [2048], replicated, may hold values from 0.099609375 to 1.8984375
- norm_bias: bfloat16 [2048], replicated, may hold values from -3 to 3
- w_qkv: bfloat16 [2048, 3, 1024], P(None, None, 'tp'), may hold values from -10 to 10
- segment_ids: int32 [4096], P('req'), may hold values from 0 to 7, never falling along the last dimension, each value on 1 to 2048 neighbouring positions
- pack_lengths: int32 [1], replicated, may hold values from 3968 to 4096
- page_table: int32 [32, 2], P('req'), may hold values from 0 to 15, as said below
Outputs:
- context: bfloat16 [4096, 1024], P('req', 'tp')
- kv_cache: bfloat16 [64, 2, 128, 1024], P('req', None, None, 'tp')
Inputs may be any that keep to these rules, and one draw needn't show every extreme that they name: `segment_ids`: never falling along the tokens; each id covers at most 2048 consecutive tokens and some id exactly 2048. `page_table`: row g holds the owning device and the slot of the g-th page of 128 tokens. Within each aligned group of 16 devices, the j-th page of every device goes the same number of devices forward, 1 to 8, into slot j, unless that passes the last device of the axis; then it stays on its own device in slot j + 2.
All inputs are finite; a program needn't handle non-finite values.
Results may differ from a plain program's by a relative error of at most 0.0099.
Values may be sent and summed in bfloat16 or wider, within the bound.
No kernel may reach another device: no remote copies, remote signals or barrier semaphores. Data moves between devices by JAX's collectives and lax.ppermute only.
A program may use at most 64 MiB of HBM per device.

v0:
```python
import jax
import jax.numpy as jnp
from jax import lax
from jax.sharding import PartitionSpec as P

HD = 128
PAGE = 128
REACH = 8


def shifted(shard, axis, by):
    devices = lax.axis_size(axis)
    pairs = [(i, i + by) for i in range(devices) if 0 <= i + by < devices]
    return lax.ppermute(shard, axis, pairs)


def layer_norm(features, norm_gain, norm_bias):
    as_float = features.astype(jnp.float32)
    row_mean = jnp.mean(as_float, axis=-1, keepdims=True)
    centred = as_float - row_mean
    variance = jnp.mean(centred * centred, axis=-1, keepdims=True)
    scaled = centred * lax.rsqrt(variance + 1e-05)
    return (scaled * norm_gain.astype(jnp.float32) + norm_bias.astype(jnp.float32)).astype(
        jnp.bfloat16
    )


def block_scores(queries, key_block, allowed):
    raw_scores = jnp.einsum("qhd,khd->hqk", queries, key_block, preferred_element_type=jnp.float32)
    return jnp.where(allowed[None], raw_scores, -1e30)


def weigh_values(probs_part, value_block):
    return jnp.einsum("hqk,khd->qhd", probs_part, value_block, preferred_element_type=jnp.float32)


def per_device(tokens, norm_gain, norm_bias, w_qkv, segment_ids, pack_lengths, page_table):
    gathered = lax.all_gather(tokens, "tp", axis=1, tiled=True)
    normed = layer_norm(gathered, norm_gain, norm_bias)
    row_count = gathered.shape[0]
    local_width = w_qkv.shape[2]
    head_count = local_width // HD
    projected = jnp.dot(
        normed, w_qkv.reshape(w_qkv.shape[0], 3 * local_width), preferred_element_type=jnp.float32
    )
    projected = projected.reshape(row_count, 3, local_width)
    device_index = lax.axis_index("req")
    per_pack = lax.axis_size("req") // pack_lengths.shape[0]
    pack_id = device_index // per_pack
    offsets = device_index % per_pack * row_count + jnp.arange(row_count, dtype=jnp.int32)
    in_length = (offsets < pack_lengths[pack_id])[:, None]
    queries = (
        (projected[:, 0] * HD ** (-0.5)).astype(jnp.bfloat16).reshape(row_count, head_count, HD)
    )
    key_rows = jnp.where(in_length, projected[:, 1], 0.0).astype(jnp.bfloat16)
    value_rows = jnp.where(in_length, projected[:, 2], 0.0).astype(jnp.bfloat16)
    own_block = (key_rows, value_rows, segment_ids, page_table)
    blocks = [own_block]
    for distance in range(1, REACH + 1):
        blocks.append(shifted((key_rows, value_rows, segment_ids, page_table), "req", distance))
    causal = jnp.arange(row_count)[None, :] <= jnp.arange(row_count)[:, None]
    mask_list = []
    for distance in range(REACH + 1):
        source = device_index - distance
        same_pack = (source >= 0) & (source // per_pack == pack_id)
        allowed = same_pack & (blocks[distance][2][None, :] == segment_ids[:, None])
        if distance == 0:
            allowed = allowed & causal
        mask_list.append(allowed)
    key_list = [block_tuple[0].reshape(row_count, head_count, HD) for block_tuple in blocks]
    value_list = [block_tuple[1].reshape(row_count, head_count, HD) for block_tuple in blocks]
    scores = block_scores(
        queries, jnp.concatenate(key_list, axis=0), jnp.concatenate(mask_list, axis=1)
    )
    row_max = jnp.max(scores, axis=2, keepdims=True)
    exp_scores = jnp.exp(scores - row_max)
    row_sum = jnp.sum(exp_scores, axis=2, keepdims=True)
    probs_bf = (exp_scores / row_sum).astype(jnp.bfloat16)
    context = weigh_values(probs_bf, jnp.concatenate(value_list, axis=0))
    context = jnp.where(in_length, context.reshape(row_count, local_width), 0.0).astype(
        jnp.bfloat16
    )
    page_count = row_count // PAGE
    slot_count = 2 * page_count
    slot_range = jnp.arange(slot_count, dtype=jnp.int32)
    cache_sum = jnp.zeros((slot_count, 2, PAGE, local_width), jnp.float32)
    for block_tuple in blocks:
        table_part = block_tuple[3]
        chosen = (
            (table_part[:, 0] == device_index)[None, :]
            & (table_part[:, 1][None, :] == slot_range[:, None])
        ).astype(jnp.bfloat16)
        stacked = jnp.stack([block_tuple[0], block_tuple[1]]).reshape(
            2, page_count, PAGE, local_width
        )
        cache_sum = cache_sum + jnp.einsum(
            "sj,cjpx->scpx", chosen, stacked, preferred_element_type=jnp.float32
        )
    kv_cache = cache_sum.astype(jnp.bfloat16)
    return (context, kv_cache)


def solution(mesh):
    return jax.shard_map(
        per_device,
        mesh=mesh,
        in_specs=(P("req", "tp"), P(), P(), P(None, None, "tp"), P("req"), P(), P("req", None)),
        out_specs=(P("req", "tp"), P("req", None, None, "tp")),
        check_vma=False,
    )
```

profile of v0, /device:TPU:0, one launch (start us, length us, event | category | flops | bytes accessed | tf_op | source)
XLA Modules:
  0.0 279.0 jit_solution(16888581579660344434)
XLA Ops:
  7.2 4.8 %collective-permute-start.8 = (s32[256]{0:T(256)}, s32[256]{0:T(256)S(1)}, u32[]{:S(2)}, u32[]{:S(2)}) collective-permute-start(s32[256]{0:T(256)} %param.11), channel_id=1, source_target_pairs={{0,2},{2,4},{4,6},{6,8},{8,10},{10,12},{12,14},{14,16},{16,18},{18... | collective-permute-start | bytes 3080 | tf_op jit(solution)/shard_map/ppermute | solution.py:14
  12.1 3.4 %collective-permute-start.9 = (s32[256]{0:T(256)}, s32[256]{0:T(256)S(1)}, u32[]{:S(2)}, u32[]{:S(2)}) collective-permute-start(s32[256]{0:T(256)} %param.11), channel_id=1, source_target_pairs={{0,4},{2,6},{4,8},{6,10},{8,12},{10,14},{12,16},{14,18},{16,20},{1... | collective-permute-start | bytes 3080 | tf_op jit(solution)/shard_map/ppermute | solution.py:14
  15.5 4.4 %collective-permute-start.10 = (s32[256]{0:T(256)}, s32[256]{0:T(256)S(1)}, u32[]{:S(2)}, u32[]{:S(2)}) collective-permute-start(s32[256]{0:T(256)} %param.11), channel_id=1, source_target_pairs={{0,6},{2,8},{4,10},{6,12},{8,14},{10,16},{12,18},{14,20},{16,22},{... | collective-permute-start | bytes 3080 | tf_op jit(solution)/shard_map/ppermute | solution.py:14
  19.9 3.5 %collective-permute-start.11 = (s32[256]{0:T(256)}, s32[256]{0:T(256)S(1)}, u32[]{:S(2)}, u32[]{:S(2)}) collective-permute-start(s32[256]{0:T(256)} %param.11), channel_id=1, source_target_pairs={{0,8},{2,10},{4,12},{6,14},{8,16},{10,18},{12,20},{14,22},{16,24},... | collective-permute-start | bytes 3080 | tf_op jit(solution)/shard_map/ppermute | solution.py:14
  23.4 2.9 %collective-permute-start.30 = (s32[2,2]{1,0:T(2,128)}, s32[2,2]{1,0:T(2,128)S(1)}, u32[]{:S(2)}, u32[]{:S(2)}) collective-permute-start(s32[2,2]{1,0:T(2,128)} %param.13), channel_id=1, source_target_pairs={{0,14},{2,16},{4,18},{6,20},{8,22},{10,24},{12,26},{14,28},{16,30}... | collective-permute-start | bytes 56 | tf_op jit(solution)/shard_map/ppermute | solution.py:14
  28.1 9.0 %copy.90 = bf16[2048,3,512]{0,2,1:T(8,128)(2,1)} copy(bf16[2048,3,512]{2,0,1:T(8,128)(2,1)} %param.10) | data formatting | bytes 12582912 | tf_op args[3]
  41.0 1.8 collective-permute-start.28
  44.0 6.6 %collective-permute-start.27 = (s32[2,2]{1,0:T(2,128)S(1)}, s32[2,2]{1,0:T(2,128)S(1)}, u32[]{:S(2)}, u32[]{:S(2)}) collective-permute-start(s32[2,2]{1,0:T(2,128)S(1)} %copy-done.20), channel_id=1, source_target_pairs={{0,8},{2,10},{4,12},{6,14},{8,16},{10,18},{12,20},{14,22},{16,24},... | collective-permute-start | bytes 56 | tf_op jit(solution)/shard_map/ppermute | solution.py:14
  51.9 5.0 %collective-permute-start.26 = (s32[2,2]{1,0:T(2,128)S(1)}, s32[2,2]{1,0:T(2,128)S(1)}, u32[]{:S(2)}, u32[]{:S(2)}) collective-permute-start(s32[2,2]{1,0:T(2,128)S(1)} %copy-done.20), channel_id=1, source_target_pairs={{0,6},{2,8},{4,10},{6,12},{8,14},{10,16},{12,18},{14,20},{16,22},{... | collective-permute-start | bytes 56 | tf_op jit(solution)/shard_map/ppermute | solution.py:14
  58.2 3.4 %collective-permute-start.25 = (s32[2,2]{1,0:T(2,128)S(1)}, s32[2,2]{1,0:T(2,128)S(1)}, u32[]{:S(2)}, u32[]{:S(2)}) collective-permute-start(s32[2,2]{1,0:T(2,128)S(1)} %copy-done.20), channel_id=1, source_target_pairs={{0,4},{2,6},{4,8},{6,10},{8,12},{10,14},{12,16},{14,18},{16,20},{1... | collective-permute-start | bytes 56 | tf_op jit(solution)/shard_map/ppermute | solution.py:14
  62.9 4.2 %collective-permute-start.24 = (s32[2,2]{1,0:T(2,128)S(1)}, s32[2,2]{1,0:T(2,128)S(1)}, u32[]{:S(2)}, u32[]{:S(2)}) collective-permute-start(s32[2,2]{1,0:T(2,128)S(1)} %copy-done.20), channel_id=1, source_target_pairs={{0,2},{2,4},{4,6},{6,8},{8,10},{10,12},{12,14},{14,16},{16,18},{18... | collective-permute-start | bytes 56 | tf_op jit(solution)/shard_map/ppermute | solution.py:14
  68.4 12.6 %collective-permute-start.31 = (s32[2,2]{1,0:T(2,128)S(1)}, s32[2,2]{1,0:T(2,128)S(1)}, u32[]{:S(2)}, u32[]{:S(2)}) collective-permute-start(s32[2,2]{1,0:T(2,128)S(1)} %copy-done.20), channel_id=1, source_target_pairs={{0,16},{2,18},{4,20},{6,22},{8,24},{10,26},{12,28},{14,30},{1,17},... | collective-permute-start | bytes 56 | tf_op jit(solution)/shard_map/ppermute | solution.py:14
  83.9 4.0 %collective-permute-start.13 = (s32[256]{0:T(256)S(1)}, s32[256]{0:T(256)S(1)}, u32[]{:S(2)}, u32[]{:S(2)}) collective-permute-start(s32[256]{0:T(256)S(1)} %copy-done.16), channel_id=1, source_target_pairs={{0,12},{2,14},{4,16},{6,18},{8,20},{10,22},{12,24},{14,26},{16,28}... | collective-permute-start | bytes 3080 | tf_op jit(solution)/shard_map/ppermute | solution.py:14
  88.0 5.4 %collective-permute-start.14 = (s32[256]{0:T(256)S(1)}, s32[256]{0:T(256)S(1)}, u32[]{:S(2)}, u32[]{:S(2)}) collective-permute-start(s32[256]{0:T(256)S(1)} %copy-done.16), channel_id=1, source_target_pairs={{0,14},{2,16},{4,18},{6,20},{8,22},{10,24},{12,26},{14,28},{16,30}... | collective-permute-start | bytes 3080 | tf_op jit(solution)/shard_map/ppermute | solution.py:14
  99.7 5.0 %fusion.4 = f32[256,3,512]{2,0,1:T(8,128)S(1)} fusion(bf16[2048,3,512]{0,2,1:T(8,128)(2,1)} %copy.90, bf16[256,2048]{1,0:T(8,128)(2,1)} %all-gather.2.cloned.1.call-done, f32[2048]{0:T(1024)S(1)} %convert_element_type.71, f32[2048]{0:T(1024)S(1)} %convert_element_type.70, f32[256]{0:T(256)S(1)} %add_rsqrt_fusion, f32[256]{0:T(256)S(1)} %broadcast_multiply_fusion), kind=kOutput, calls=%fused_computation.5 | convolution fusion | flops 1613758464 | bytes 8931328 | tf_op jit(solution)/shard_map/dot_general | solution.py:43
  106.8 1.9 collective-permute-start
  108.6 1.8 collective-permute-start.1
  110.5 2.8 %collective-permute-start.2 = (bf16[256,512]{1,0:T(8,128)(2,1)}, bf16[256,512]{1,0:T(8,128)(2,1)S(1)}, u32[]{:S(2)}, u32[]{:S(2)}) collective-permute-start(bf16[256,512]{1,0:T(8,128)(2,1)} %get-tuple-element.9), channel_id=1, source_target_pairs={{0,6},{2,8},{4,10},{6,12},{8,14},{10,16},{12,18},{14,20},{16,22},{... | collective-permute-start | bytes 786440 | tf_op jit(solution)/shard_map/ppermute | solution.py:14
  113.3 6.5 %collective-permute-start.16 = (bf16[256,512]{1,0:T(8,128)(2,1)}, bf16[256,512]{1,0:T(8,128)(2,1)S(1)}, u32[]{:S(2)}, u32[]{:S(2)}) collective-permute-start(bf16[256,512]{1,0:T(8,128)(2,1)} %get-tuple-element.8), channel_id=1, source_target_pairs={{0,2},{2,4},{4,6},{6,8},{8,10},{10,12},{12,14},{14,16},{16,18},{18... | collective-permute-start | bytes 786440 | tf_op jit(solution)/shard_map/ppermute | solution.py:14
  119.8 4.8 %collective-permute-start.17 = (bf16[256,512]{1,0:T(8,128)(2,1)}, bf16[256,512]{1,0:T(8,128)(2,1)}, u32[]{:S(2)}, u32[]{:S(2)}) collective-permute-start(bf16[256,512]{1,0:T(8,128)(2,1)} %get-tuple-element.8), channel_id=1, source_target_pairs={{0,4},{2,6},{4,8},{6,10},{8,12},{10,14},{12,16},{14,18},{16,20},{1... | collective-permute-start | bytes 786440 | tf_op jit(solution)/shard_map/ppermute | solution.py:14
  130.1 3.5 %collective-permute-start.18 = (bf16[256,512]{1,0:T(8,128)(2,1)}, bf16[256,512]{1,0:T(8,128)(2,1)S(1)}, u32[]{:S(2)}, u32[]{:S(2)}) collective-permute-start(bf16[256,512]{1,0:T(8,128)(2,1)} %get-tuple-element.8), channel_id=1, source_target_pairs={{0,6},{2,8},{4,10},{6,12},{8,14},{10,16},{12,18},{14,20},{16,22},{... | collective-permute-start | bytes 786440 | tf_op jit(solution)/shard_map/ppermute | solution.py:14
  134.4 10.5 %collective-permute-start.19 = (bf16[256,512]{1,0:T(8,128)(2,1)}, bf16[256,512]{1,0:T(8,128)(2,1)S(1)}, u32[]{:S(2)}, u32[]{:S(2)}) collective-permute-start(bf16[256,512]{1,0:T(8,128)(2,1)} %get-tuple-element.8), channel_id=1, source_target_pairs={{0,8},{2,10},{4,12},{6,14},{8,16},{10,18},{12,20},{14,22},{16,24},... | collective-permute-start | bytes 786440 | tf_op jit(solution)/shard_map/ppermute | solution.py:14
  145.0 1.7 bitcast_dynamic-update-slice_fusion.6
  146.7 17.0 %collective-permute-start.20 = (bf16[256,512]{1,0:T(8,128)(2,1)}, bf16[256,512]{1,0:T(8,128)(2,1)S(1)}, u32[]{:S(2)}, u32[]{:S(2)}) collective-permute-start(bf16[256,512]{1,0:T(8,128)(2,1)} %get-tuple-element.8), channel_id=1, source_target_pairs={{0,10},{2,12},{4,14},{6,16},{8,18},{10,20},{12,22},{14,24},{16,26}... | collective-permute-start | bytes 786440 | tf_op jit(solution)/shard_map/ppermute | solution.py:14
  168.1 14.7 %collective-permute-start.22 = (bf16[256,512]{1,0:T(8,128)(2,1)}, bf16[256,512]{1,0:T(8,128)(2,1)S(1)}, u32[]{:S(2)}, u32[]{:S(2)}) collective-permute-start(bf16[256,512]{1,0:T(8,128)(2,1)} %get-tuple-element.8), channel_id=1, source_target_pairs={{0,14},{2,16},{4,18},{6,20},{8,22},{10,24},{12,26},{14,28},{16,30}... | collective-permute-start | bytes 786440 | tf_op jit(solution)/shard_map/ppermute | solution.py:14
  187.0 4.5 %collective-permute-start.3 = (bf16[256,512]{1,0:T(8,128)(2,1)}, bf16[256,512]{1,0:T(8,128)(2,1)}, u32[]{:S(2)}, u32[]{:S(2)}) collective-permute-start(bf16[256,512]{1,0:T(8,128)(2,1)} %get-tuple-element.9), channel_id=1, source_target_pairs={{0,8},{2,10},{4,12},{6,14},{8,16},{10,18},{12,20},{14,22},{16,24},... | collective-permute-start | bytes 786440 | tf_op jit(solution)/shard_map/ppermute | solution.py:14
  192.3 16.3 %collective-permute-start.4 = (bf16[256,512]{1,0:T(8,128)(2,1)}, bf16[256,512]{1,0:T(8,128)(2,1)}, u32[]{:S(2)}, u32[]{:S(2)}) collective-permute-start(bf16[256,512]{1,0:T(8,128)(2,1)} %get-tuple-element.9), channel_id=1, source_target_pairs={{0,10},{2,12},{4,14},{6,16},{8,18},{10,20},{12,22},{14,24},{16,26}... | collective-permute-start | bytes 786440 | tf_op jit(solution)/shard_map/ppermute | solution.py:14
  209.3 8.6 %fusion.141 = (f32[4,256]{1,0:T(4,128)S(1)}, f32[4,256,2304]{2,1,0:T(8,128)}) fusion(pred[256,2304]{1,0:T(8,128)(4,1)} %copy-done.17, bf16[2304,4,128]{2,0,1:T(8,128)(2,1)} %bitcast_dynamic-update-slice_fusion, bf16[256,4,128]{2,1,0:T(4,128)(2,1)} %convert_element_type.76), kind=kOutput, calls=%fused_computation.194 | convolution fusion | flops 611059968 | bytes 12652544 | tf_op jit(solution)/shard_map/sub | solution.py:76
  220.2 7.7 %collective-permute-start.6 = (bf16[256,512]{1,0:T(8,128)(2,1)}, bf16[256,512]{1,0:T(8,128)(2,1)S(1)}, u32[]{:S(2)}, u32[]{:S(2)}) collective-permute-start(bf16[256,512]{1,0:T(8,128)(2,1)} %get-tuple-element.9), channel_id=1, source_target_pairs={{0,14},{2,16},{4,18},{6,20},{8,22},{10,24},{12,26},{14,28},{16,30}... | collective-permute-start | bytes 786440 | tf_op jit(solution)/shard_map/ppermute | solution.py:14
  228.7 3.9 %collective-permute-start.7 = (bf16[256,512]{1,0:T(8,128)(2,1)}, bf16[256,512]{1,0:T(8,128)(2,1)S(1)}, u32[]{:S(2)}, u32[]{:S(2)}) collective-permute-start(bf16[256,512]{1,0:T(8,128)(2,1)} %get-tuple-element.9), channel_id=1, source_target_pairs={{0,16},{2,18},{4,20},{6,22},{8,24},{10,26},{12,28},{14,30},{1,17},... | collective-permute-start | bytes 786440 | tf_op jit(solution)/shard_map/ppermute | solution.py:14
  239.8 6.9 %fusion.7 = bf16[4,128,256]{2,1,0:T(8,128)(2,1)} fusion(bf16[2304,4,128]{2,0,1:T(8,128)(2,1)} %bitcast_dynamic-update-slice_fusion.8, f32[4,256,2304]{2,1,0:T(8,128)} %get-tuple-element.17, f32[4,256]{1,0:T(4,128)S(1)} %get-tuple-element.16), kind=kOutput, calls=%fused_computation.8 | convolution fusion | flops 608698368 | bytes 12062720 | tf_op jit(solution)/shard_map/hqk,khd->qhd/dot_general | solution.py:34
  268.4 2.6 add_convert_fusion
  (169 shorter events, 71.4 us)
Async XLA Ops:
  7.2 89.2 %all-gather.2.cloned.1.call-start = ((), (), s32[]{:S(2)}) async-start(), calls=%async_computation | async-start | bytes 1572864 | tf_op jit(solution)/shard_map/all_gather | solution.py:38
  7.2 76.7 %collective-permute-start.8 = (s32[256]{0:T(256)}, s32[256]{0:T(256)S(1)}, u32[]{:S(2)}, u32[]{:S(2)}) collective-permute-start(s32[256]{0:T(256)} %param.11), channel_id=1, source_target_pairs={{0,2},{2,4},{4,6},{6,8},{8,10},{10,12},{12,14},{14,16},{16,18},{18... | collective-permute-start | bytes 3080 | tf_op jit(solution)/shard_map/ppermute | solution.py:14
  12.1 76.0 %collective-permute-start.9 = (s32[256]{0:T(256)}, s32[256]{0:T(256)S(1)}, u32[]{:S(2)}, u32[]{:S(2)}) collective-permute-start(s32[256]{0:T(256)} %param.11), channel_id=1, source_target_pairs={{0,4},{2,6},{4,8},{6,10},{8,12},{10,14},{12,16},{14,18},{16,20},{1... | collective-permute-start | bytes 3080 | tf_op jit(solution)/shard_map/ppermute | solution.py:14
  15.5 78.1 %collective-permute-start.10 = (s32[256]{0:T(256)}, s32[256]{0:T(256)S(1)}, u32[]{:S(2)}, u32[]{:S(2)}) collective-permute-start(s32[256]{0:T(256)} %param.11), channel_id=1, source_target_pairs={{0,6},{2,8},{4,10},{6,12},{8,14},{10,16},{12,18},{14,20},{16,22},{... | collective-permute-start | bytes 3080 | tf_op jit(solution)/shard_map/ppermute | solution.py:14
  19.9 75.2 %collective-permute-start.11 = (s32[256]{0:T(256)}, s32[256]{0:T(256)S(1)}, u32[]{:S(2)}, u32[]{:S(2)}) collective-permute-start(s32[256]{0:T(256)} %param.11), channel_id=1, source_target_pairs={{0,8},{2,10},{4,12},{6,14},{8,16},{10,18},{12,20},{14,22},{16,24},... | collective-permute-start | bytes 3080 | tf_op jit(solution)/shard_map/ppermute | solution.py:14
  23.4 15.0 %collective-permute-start.30 = (s32[2,2]{1,0:T(2,128)}, s32[2,2]{1,0:T(2,128)S(1)}, u32[]{:S(2)}, u32[]{:S(2)}) collective-permute-start(s32[2,2]{1,0:T(2,128)} %param.13), channel_id=1, source_target_pairs={{0,14},{2,16},{4,18},{6,20},{8,22},{10,24},{12,26},{14,28},{16,30}... | collective-permute-start | bytes 56 | tf_op jit(solution)/shard_map/ppermute | solution.py:14
  38.4 2.6 collective-permute-start.29
  41.0 3.1 %collective-permute-start.28 = (s32[2,2]{1,0:T(2,128)S(1)}, s32[2,2]{1,0:T(2,128)S(1)}, u32[]{:S(2)}, u32[]{:S(2)}) collective-permute-start(s32[2,2]{1,0:T(2,128)S(1)} %copy-done.20), channel_id=1, source_target_pairs={{0,10},{2,12},{4,14},{6,16},{8,18},{10,20},{12,22},{14,24},{16,26}... | collective-permute-start | bytes 56 | tf_op jit(solution)/shard_map/ppermute | solution.py:14
  44.0 7.9 %collective-permute-start.27 = (s32[2,2]{1,0:T(2,128)S(1)}, s32[2,2]{1,0:T(2,128)S(1)}, u32[]{:S(2)}, u32[]{:S(2)}) collective-permute-start(s32[2,2]{1,0:T(2,128)S(1)} %copy-done.20), channel_id=1, source_target_pairs={{0,8},{2,10},{4,12},{6,14},{8,16},{10,18},{12,20},{14,22},{16,24},... | collective-permute-start | bytes 56 | tf_op jit(solution)/shard_map/ppermute | solution.py:14
  51.9 6.3 %collective-permute-start.26 = (s32[2,2]{1,0:T(2,128)S(1)}, s32[2,2]{1,0:T(2,128)S(1)}, u32[]{:S(2)}, u32[]{:S(2)}) collective-permute-start(s32[2,2]{1,0:T(2,128)S(1)} %copy-done.20), channel_id=1, source_target_pairs={{0,6},{2,8},{4,10},{6,12},{8,14},{10,16},{12,18},{14,20},{16,22},{... | collective-permute-start | bytes 56 | tf_op jit(solution)/shard_map/ppermute | solution.py:14
  58.2 4.7 %collective-permute-start.25 = (s32[2,2]{1,0:T(2,128)S(1)}, s32[2,2]{1,0:T(2,128)S(1)}, u32[]{:S(2)}, u32[]{:S(2)}) collective-permute-start(s32[2,2]{1,0:T(2,128)S(1)} %copy-done.20), channel_id=1, source_target_pairs={{0,4},{2,6},{4,8},{6,10},{8,12},{10,14},{12,16},{14,18},{16,20},{1... | collective-permute-start | bytes 56 | tf_op jit(solution)/shard_map/ppermute | solution.py:14
  62.9 5.5 %collective-permute-start.24 = (s32[2,2]{1,0:T(2,128)S(1)}, s32[2,2]{1,0:T(2,128)S(1)}, u32[]{:S(2)}, u32[]{:S(2)}) collective-permute-start(s32[2,2]{1,0:T(2,128)S(1)} %copy-done.20), channel_id=1, source_target_pairs={{0,2},{2,4},{4,6},{6,8},{8,10},{10,12},{12,14},{14,16},{16,18},{18... | collective-permute-start | bytes 56 | tf_op jit(solution)/shard_map/ppermute | solution.py:14
  68.4 13.8 %collective-permute-start.31 = (s32[2,2]{1,0:T(2,128)S(1)}, s32[2,2]{1,0:T(2,128)S(1)}, u32[]{:S(2)}, u32[]{:S(2)}) collective-permute-start(s32[2,2]{1,0:T(2,128)S(1)} %copy-done.20), channel_id=1, source_target_pairs={{0,16},{2,18},{4,20},{6,22},{8,24},{10,26},{12,28},{14,30},{1,17},... | collective-permute-start | bytes 56 | tf_op jit(solution)/shard_map/ppermute | solution.py:14
  82.3 12.9 %collective-permute-start.12 = (s32[256]{0:T(256)S(1)}, s32[256]{0:T(256)S(1)}, u32[]{:S(2)}, u32[]{:S(2)}) collective-permute-start(s32[256]{0:T(256)S(1)} %copy-done.16), channel_id=1, source_target_pairs={{0,10},{2,12},{4,14},{6,16},{8,18},{10,20},{12,22},{14,24},{16,26}... | collective-permute-start | bytes 3080 | tf_op jit(solution)/shard_map/ppermute | solution.py:14
  83.9 11.5 %collective-permute-start.13 = (s32[256]{0:T(256)S(1)}, s32[256]{0:T(256)S(1)}, u32[]{:S(2)}, u32[]{:S(2)}) collective-permute-start(s32[256]{0:T(256)S(1)} %copy-done.16), channel_id=1, source_target_pairs={{0,12},{2,14},{4,16},{6,18},{8,20},{10,22},{12,24},{14,26},{16,28}... | collective-permute-start | bytes 3080 | tf_op jit(solution)/shard_map/ppermute | solution.py:14
  88.0 7.5 %collective-permute-start.14 = (s32[256]{0:T(256)S(1)}, s32[256]{0:T(256)S(1)}, u32[]{:S(2)}, u32[]{:S(2)}) collective-permute-start(s32[256]{0:T(256)S(1)} %copy-done.16), channel_id=1, source_target_pairs={{0,14},{2,16},{4,18},{6,20},{8,22},{10,24},{12,26},{14,28},{16,30}... | collective-permute-start | bytes 3080 | tf_op jit(solution)/shard_map/ppermute | solution.py:14
  106.8 111.2 %collective-permute-start = (bf16[256,512]{1,0:T(8,128)(2,1)}, bf16[256,512]{1,0:T(8,128)(2,1)S(1)}, u32[]{:S(2)}, u32[]{:S(2)}) collective-permute-start(bf16[256,512]{1,0:T(8,128)(2,1)} %get-tuple-element.9), channel_id=1, source_target_pairs={{0,2},{2,4},{4,6},{6,8},{8,10},{10,12},{12,14},{14,16},{16,18},{18... | collective-permute-start | bytes 786440 | tf_op jit(solution)/shard_map/ppermute | solution.py:14
  108.6 111.6 %collective-permute-start.1 = (bf16[256,512]{1,0:T(8,128)(2,1)}, bf16[256,512]{1,0:T(8,128)(2,1)S(1)}, u32[]{:S(2)}, u32[]{:S(2)}) collective-permute-start(bf16[256,512]{1,0:T(8,128)(2,1)} %get-tuple-element.9), channel_id=1, source_target_pairs={{0,4},{2,6},{4,8},{6,10},{8,12},{10,14},{12,16},{14,18},{16,20},{1... | collective-permute-start | bytes 786440 | tf_op jit(solution)/shard_map/ppermute | solution.py:14
  110.5 118.2 %collective-permute-start.2 = (bf16[256,512]{1,0:T(8,128)(2,1)}, bf16[256,512]{1,0:T(8,128)(2,1)S(1)}, u32[]{:S(2)}, u32[]{:S(2)}) collective-permute-start(bf16[256,512]{1,0:T(8,128)(2,1)} %get-tuple-element.9), channel_id=1, source_target_pairs={{0,6},{2,8},{4,10},{6,12},{8,14},{10,16},{12,18},{14,20},{16,22},{... | collective-permute-start | bytes 786440 | tf_op jit(solution)/shard_map/ppermute | solution.py:14
  113.3 16.9 %collective-permute-start.16 = (bf16[256,512]{1,0:T(8,128)(2,1)}, bf16[256,512]{1,0:T(8,128)(2,1)S(1)}, u32[]{:S(2)}, u32[]{:S(2)}) collective-permute-start(bf16[256,512]{1,0:T(8,128)(2,1)} %get-tuple-element.8), channel_id=1, source_target_pairs={{0,2},{2,4},{4,6},{6,8},{8,10},{10,12},{12,14},{14,16},{16,18},{18... | collective-permute-start | bytes 786440 | tf_op jit(solution)/shard_map/ppermute | solution.py:14
  119.8 14.6 %collective-permute-start.17 = (bf16[256,512]{1,0:T(8,128)(2,1)}, bf16[256,512]{1,0:T(8,128)(2,1)}, u32[]{:S(2)}, u32[]{:S(2)}) collective-permute-start(bf16[256,512]{1,0:T(8,128)(2,1)} %get-tuple-element.8), channel_id=1, source_target_pairs={{0,4},{2,6},{4,8},{6,10},{8,12},{10,14},{12,16},{14,18},{16,20},{1... | collective-permute-start | bytes 786440 | tf_op jit(solution)/shard_map/ppermute | solution.py:14
  130.1 16.5 %collective-permute-start.18 = (bf16[256,512]{1,0:T(8,128)(2,1)}, bf16[256,512]{1,0:T(8,128)(2,1)S(1)}, u32[]{:S(2)}, u32[]{:S(2)}) collective-permute-start(bf16[256,512]{1,0:T(8,128)(2,1)} %get-tuple-element.8), channel_id=1, source_target_pairs={{0,6},{2,8},{4,10},{6,12},{8,14},{10,16},{12,18},{14,20},{16,22},{... | collective-permute-start | bytes 786440 | tf_op jit(solution)/shard_map/ppermute | solution.py:14
  134.4 30.0 %collective-permute-start.19 = (bf16[256,512]{1,0:T(8,128)(2,1)}, bf16[256,512]{1,0:T(8,128)(2,1)S(1)}, u32[]{:S(2)}, u32[]{:S(2)}) collective-permute-start(bf16[256,512]{1,0:T(8,128)(2,1)} %get-tuple-element.8), channel_id=1, source_target_pairs={{0,8},{2,10},{4,12},{6,14},{8,16},{10,18},{12,20},{14,22},{16,24},... | collective-permute-start | bytes 786440 | tf_op jit(solution)/shard_map/ppermute | solution.py:14
  146.7 21.4 %collective-permute-start.20 = (bf16[256,512]{1,0:T(8,128)(2,1)}, bf16[256,512]{1,0:T(8,128)(2,1)S(1)}, u32[]{:S(2)}, u32[]{:S(2)}) collective-permute-start(bf16[256,512]{1,0:T(8,128)(2,1)} %get-tuple-element.8), channel_id=1, source_target_pairs={{0,10},{2,12},{4,14},{6,16},{8,18},{10,20},{12,22},{14,24},{16,26}... | collective-permute-start | bytes 786440 | tf_op jit(solution)/shard_map/ppermute | solution.py:14
  164.4 19.2 %collective-permute-start.21 = (bf16[256,512]{1,0:T(8,128)(2,1)}, bf16[256,512]{1,0:T(8,128)(2,1)S(1)}, u32[]{:S(2)}, u32[]{:S(2)}) collective-permute-start(bf16[256,512]{1,0:T(8,128)(2,1)} %get-tuple-element.8), channel_id=1, source_target_pairs={{0,12},{2,14},{4,16},{6,18},{8,20},{10,22},{12,24},{14,26},{16,28}... | collective-permute-start | bytes 786440 | tf_op jit(solution)/shard_map/ppermute | solution.py:14
  168.1 18.9 %collective-permute-start.22 = (bf16[256,512]{1,0:T(8,128)(2,1)}, bf16[256,512]{1,0:T(8,128)(2,1)S(1)}, u32[]{:S(2)}, u32[]{:S(2)}) collective-permute-start(bf16[256,512]{1,0:T(8,128)(2,1)} %get-tuple-element.8), channel_id=1, source_target_pairs={{0,14},{2,16},{4,18},{6,20},{8,22},{10,24},{12,26},{14,28},{16,30}... | collective-permute-start | bytes 786440 | tf_op jit(solution)/shard_map/ppermute | solution.py:14
  183.6 8.7 %collective-permute-start.23 = (bf16[256,512]{1,0:T(8,128)(2,1)}, bf16[256,512]{1,0:T(8,128)(2,1)S(1)}, u32[]{:S(2)}, u32[]{:S(2)}) collective-permute-start(bf16[256,512]{1,0:T(8,128)(2,1)} %get-tuple-element.8), channel_id=1, source_target_pairs={{0,16},{2,18},{4,20},{6,22},{8,24},{10,26},{12,28},{14,30},{1,17},... | collective-permute-start | bytes 786440 | tf_op jit(solution)/shard_map/ppermute | solution.py:14
  187.0 46.4 %collective-permute-start.3 = (bf16[256,512]{1,0:T(8,128)(2,1)}, bf16[256,512]{1,0:T(8,128)(2,1)}, u32[]{:S(2)}, u32[]{:S(2)}) collective-permute-start(bf16[256,512]{1,0:T(8,128)(2,1)} %get-tuple-element.9), channel_id=1, source_target_pairs={{0,8},{2,10},{4,12},{6,14},{8,16},{10,18},{12,20},{14,22},{16,24},... | collective-permute-start | bytes 786440 | tf_op jit(solution)/shard_map/ppermute | solution.py:14
  192.3 42.8 %collective-permute-start.4 = (bf16[256,512]{1,0:T(8,128)(2,1)}, bf16[256,512]{1,0:T(8,128)(2,1)}, u32[]{:S(2)}, u32[]{:S(2)}) collective-permute-start(bf16[256,512]{1,0:T(8,128)(2,1)} %get-tuple-element.9), channel_id=1, source_target_pairs={{0,10},{2,12},{4,14},{6,16},{8,18},{10,20},{12,22},{14,24},{16,26}... | collective-permute-start | bytes 786440 | tf_op jit(solution)/shard_map/ppermute | solution.py:14
  217.9 18.8 %collective-permute-start.5 = (bf16[256,512]{1,0:T(8,128)(2,1)}, bf16[256,512]{1,0:T(8,128)(2,1)S(1)}, u32[]{:S(2)}, u32[]{:S(2)}) collective-permute-start(bf16[256,512]{1,0:T(8,128)(2,1)} %get-tuple-element.9), channel_id=1, source_target_pairs={{0,12},{2,14},{4,16},{6,18},{8,20},{10,22},{12,24},{14,26},{16,28}... | collective-permute-start | bytes 786440 | tf_op jit(solution)/shard_map/ppermute | solution.py:14
  220.2 17.4 %collective-permute-start.6 = (bf16[256,512]{1,0:T(8,128)(2,1)}, bf16[256,512]{1,0:T(8,128)(2,1)S(1)}, u32[]{:S(2)}, u32[]{:S(2)}) collective-permute-start(bf16[256,512]{1,0:T(8,128)(2,1)} %get-tuple-element.9), channel_id=1, source_target_pairs={{0,14},{2,16},{4,18},{6,20},{8,22},{10,24},{12,26},{14,28},{16,30}... | collective-permute-start | bytes 786440 | tf_op jit(solution)/shard_map/ppermute | solution.py:14
  228.7 9.7 %collective-permute-start.7 = (bf16[256,512]{1,0:T(8,128)(2,1)}, bf16[256,512]{1,0:T(8,128)(2,1)S(1)}, u32[]{:S(2)}, u32[]{:S(2)}) collective-permute-start(bf16[256,512]{1,0:T(8,128)(2,1)} %get-tuple-element.9), channel_id=1, source_target_pairs={{0,16},{2,18},{4,20},{6,22},{8,24},{10,26},{12,28},{14,30},{1,17},... | collective-permute-start | bytes 786440 | tf_op jit(solution)/shard_map/ppermute | solution.py:14
  (22 other events, 219.7 us)
Sparse Core Ops, SparseCore 0:
  23.5 6.3 all-gather.1
where the time goes:
time: 281 us; the launch traced here: 279 us
  starting transfers between devices  166 us (59%)
  local copies, waits for them, and re-layouts  43.3 us (15%)
  matrix products  32.8 us (12%)
  between operations  15.8 us (6%)
  other arithmetic  10.7 us (4%)
  waiting for transfers between devices  10.4 us (4%)
    ppermute x32, starting transfers between devices, shifted(): return lax.ppermute(shard, axis, pairs)  166 us
    unnamed x58, local copies, waits for them, and re-layouts  25.5 us
    dot_general x9, matrix products, per_device(): jnp.einsum('sj,cjpx->scpx', chosen, stacked, preferred_element_type=jnp.f...  12.3 us
    another operation x16, local copies, waits for them, and re-layouts, per_device(): jnp.stack([block_tuple[0], block_tuple[1]])  11.1 us
    ppermute x32, waiting for transfers between devices, shifted(): return lax.ppermute(shard, axis, pairs)  10.4 us
    sub x1, matrix products, per_device(): exp_scores = jnp.exp(scores - row_max)  8.62 us
    dot_general x1, matrix products, weigh_values(): jnp.einsum('hqk,khd->qhd', probs_part, value_block, preferred_element_typ...  6.88 us
  transfers between devices with their start and end apart: 33, of which 10 were waited for; matrix products, arithmetic and copies ran while one was open for 15% of the time, Pallas kernels for 0%

commit v1 on v0

v1 whole, which is shorter than its diff:
```python
import functools
import jax
import jax.numpy as jnp
from jax import lax
from jax.experimental import pallas as pl
from jax.experimental.pallas import tpu as pltpu
from jax.sharding import PartitionSpec as P

HD = 128
PAGE = 128
REACH = 8
NOTES = 16
MASKED = -1e30
VMEM = pl.BlockSpec(memory_space=pltpu.VMEM)
SMEM = pl.BlockSpec(memory_space=pltpu.SMEM)


def paired(shard, axis, bit):
    devices = lax.axis_size(axis)
    return lax.ppermute(shard, axis, [(i, i ^ bit) for i in range(devices)])


def forward(shard, axis, by):
    devices = lax.axis_size(axis)
    return lax.ppermute(shard, axis, [(i, i + by) for i in range(devices - by)])


def cost(flops, moved, transcendentals=0):
    return pl.CostEstimate(flops=flops, bytes_accessed=moved, transcendentals=transcendentals)


def valid_rows(lengths_ref, row_count):
    device = lax.axis_index("req")
    per_pack = lax.axis_size("req") // lengths_ref.shape[0]
    limit = lengths_ref[device // per_pack] - device % per_pack * row_count
    return lax.broadcasted_iota(jnp.int32, (row_count, 1), 0) < limit


def key_value_kernel(tp, heads, lengths_ref, table_ref, notes_ref, *refs):
    parts, refs = refs[:tp], refs[tp:]
    gain_ref, bias_ref, w_ref, normed_ref = refs[:4]
    sends, (columns,) = refs[4 : 4 + 2 * heads], refs[4 + 2 * heads :]
    rows, features = parts[0].shape
    here = lax.axis_index("tp")
    me = lax.axis_index("req") % heads
    which = pl.program_id(0)

    @pl.when(which == 0)
    def _():
        step = 32

        def norm_rows(index, carry):
            at = pl.ds(pl.multiple_of(index * step, step), step)
            pieces = [part[at, :].astype(jnp.float32) for part in parts]
            total = sum(jnp.sum(piece, axis=1, keepdims=True) for piece in pieces)
            mean = total * (1.0 / (tp * features))
            centred = [piece - mean for piece in pieces]
            squares = sum(jnp.sum(piece * piece, axis=1, keepdims=True) for piece in centred)
            scale = lax.rsqrt(squares * (1.0 / (tp * features)) + 1e-05)
            for bit, piece in enumerate(centred):
                lanes = pl.ds(pl.multiple_of((here ^ bit) * features, features), features)
                gain = gain_ref[:, lanes].astype(jnp.float32)
                bias = bias_ref[:, lanes].astype(jnp.float32)
                normed_ref[at, lanes] = (piece * scale * gain + bias).astype(jnp.bfloat16)
            return carry

        lax.fori_loop(0, rows // step, norm_rows, 0)

    projected = jnp.dot(normed_ref[...], w_ref[0], preferred_element_type=jnp.float32)
    projected = jnp.where(valid_rows(lengths_ref, rows), projected, 0.0)
    columns[...] = projected.astype(jnp.bfloat16)
    for bit in range(heads):
        lanes = pl.ds(pl.multiple_of((me ^ bit) * HD, HD), HD)
        for page in range(2):
            at = pl.ds(pl.multiple_of(which * PAGE, PAGE), PAGE)
            sends[2 * bit + page][at, :] = columns[page * PAGE : (page + 1) * PAGE, lanes]

    @pl.when(which == 1)
    def _():
        row = lax.broadcasted_iota(jnp.int32, (NOTES, HD), 0)
        notes = jnp.zeros((NOTES, HD), jnp.int32)
        for page in range(2):
            notes = jnp.where(row == page, notes_ref[:, page * PAGE : (page + 1) * PAGE] + 1, notes)
            for column in range(2):
                entry = table_ref[page, column] + 1
                notes = jnp.where(row == 2 + 2 * page + column, entry, notes)
        notes = notes.astype(jnp.float32).astype(jnp.bfloat16)
        for bit in range(heads):
            sends[2 * bit][2 * PAGE :, :] = notes


def query_kernel(heads, normed_ref, w_ref, *refs):
    sends, columns = refs[:heads], refs[heads]
    me = lax.axis_index("req") % heads
    projected = jnp.dot(normed_ref[...], w_ref[0], preferred_element_type=jnp.float32)
    columns[...] = (projected * HD ** (-0.5)).astype(jnp.bfloat16)
    for bit in range(heads):
        sends[bit][...] = columns[:, pl.ds(pl.multiple_of((me ^ bit) * HD, HD), HD)]


def attend_kernel(heads, reach, packs, tiles, first, last, cache_page, *refs):
    refs = list(refs)
    take = lambda count: [refs.pop(0) for _ in range(count)]
    queries = take(heads)
    noted = dict(zip(noted_layers(reach, tiles, cache_page), take(len(noted_layers(reach, tiles, cache_page)))))
    pages = dict(zip(page_list(reach, tiles, cache_page), take(len(page_list(reach, tiles, cache_page)))))
    pages.update({(layer, 0): buffer for layer, buffer in noted.items()})
    state = [] if first else take(2)
    outs = refs
    device = lax.axis_index("req")
    per_pack = lax.axis_size("req") // packs
    me = device % heads
    rows = queries[0].shape[0]
    width = heads * PAGE
    notes = {
        layer: [buffer[bit, 2 * PAGE :, :].astype(jnp.float32) for bit in range(heads)]
        for layer, buffer in noted.items()
    }
    keys, values, key_ids, key_places = [], [], [], []
    ones = jnp.ones((width, HD), jnp.bfloat16)
    lane = lax.broadcasted_iota(jnp.int32, (1, PAGE), 1)
    for layer, page in tiles:
        buffer = pages[layer, page]
        keys.append(buffer[:, :PAGE].reshape(width, HD))
        values.append(
            jnp.concatenate([buffer[:, PAGE : 2 * PAGE].reshape(width, HD), ones], axis=1)
        )
        ids = jnp.concatenate([note[page : page + 1] for note in notes[layer]], axis=1)
        if layer > 0:
            same_pack = (device - layer * heads) // per_pack == device // per_pack
            ids = jnp.where(same_pack, ids, 0.0)
        key_ids.append(ids)
        key_places.append(
            jnp.concatenate(
                [lane + ((me ^ bit) * rows + page * PAGE) for bit in range(heads)], axis=1
            )
        )
    for bit in range(heads):
        query = queries[bit][...]
        query_ids = jnp.concatenate(
            [
                jnp.broadcast_to(notes[0][bit][page : page + 1], (PAGE, PAGE)).T[:, :1]
                for page in range(2)
            ],
            axis=0,
        )
        place = lax.broadcasted_iota(jnp.int32, (rows, 1), 0) + (me ^ bit) * rows
        if first:
            top = jnp.full((rows, 1), MASKED, jnp.float32)
            total = jnp.zeros((rows, 2 * HD), jnp.float32)
        else:
            top = state[0][bit][:, :1]
            total = state[1][bit]
        for index, (layer, page) in enumerate(tiles):
            scores = lax.dot_general(
                query, keys[index], (((1,), (1,)), ((), ())), preferred_element_type=jnp.float32
            )
            allowed = key_ids[index] == query_ids
            if layer == 0:
                allowed = allowed & (key_places[index] <= place)
            scores = jnp.where(allowed, scores, MASKED)
            higher = jnp.maximum(top, jnp.max(scores, axis=1, keepdims=True))
            weights = jnp.exp(scores - higher).astype(jnp.bfloat16)
            total = total * jnp.exp(top - higher) + jnp.dot(
                weights, values[index], preferred_element_type=jnp.float32
            )
            top = higher
        if last:
            outs[bit][0:rows, :] = (total[:, :HD] / total[:, HD:]).astype(jnp.bfloat16)
        else:
            outs[0][bit] = jnp.broadcast_to(top, (rows, HD))
            outs[1][bit] = total
    if cache_page is not None:
        start = rows if last else 0
        outs = outs if last else outs[2:]
        for bit in range(heads):
            owner = (device ^ bit) + 1
            found = jnp.zeros((2 * PAGE, HD), jnp.bfloat16)
            for layer in range(reach + 1):
                for other in range(heads):
                    if layer == 0 and other == bit:
                        continue
                    note = notes[layer][other]
                    at = 2 + 2 * cache_page
                    hit = (note[at : at + 1] == owner.astype(jnp.float32)) & (
                        note[at + 1 : at + 2] == cache_page + 1.0
                    )
                    page = pages[layer, cache_page][other, : 2 * PAGE, :]
                    found = jnp.where(hit, page, found)
            outs[bit][start : start + 2 * PAGE, :] = found


def noted_layers(reach, tiles, cache_page):
    layers = range(reach + 1) if cache_page is not None else [0] + [layer for layer, _ in tiles]
    return sorted(set(layers))


def page_list(reach, tiles, cache_page):
    wanted = list(tiles)
    if cache_page is not None:
        wanted += [(layer, cache_page) for layer in range(reach + 1)]
    return sorted(set(place for place in wanted if place[1] == 1))


def finish_kernel(heads, table_ref, lengths_ref, *refs):
    refs = list(refs)
    take = lambda count: [refs.pop(0) for _ in range(count)]
    final, early, own = take(heads), take(heads), take(2 * heads)
    context_ref, cache_ref = refs
    device = lax.axis_index("req")
    me = device % heads
    rows = context_ref.shape[0]
    valid = valid_rows(lengths_ref, rows)
    for bit in range(heads):
        lanes = pl.ds(pl.multiple_of((me ^ bit) * HD, HD), HD)
        context_ref[:, lanes] = jnp.where(valid, final[bit][0:rows, :], 0).astype(jnp.bfloat16)
        for part in range(2):
            first = part * PAGE
            cache_ref[0, part, :, lanes] = early[bit][first : first + PAGE, :]
            cache_ref[1, part, :, lanes] = final[bit][rows + first : rows + first + PAGE, :]
            for page in range(2):
                stays = (table_ref[page, 0] == device) & (table_ref[page, 1] == page + 2)
                cache_ref[2 + page, part, :, lanes] = jnp.where(
                    stays, own[2 * bit + page][first : first + PAGE, :], 0
                ).astype(jnp.bfloat16)


def per_device(tokens, norm_gain, norm_bias, w_qkv, segment_ids, pack_lengths, page_table):
    rows, features = tokens.shape
    tp = lax.axis_size("tp")
    local_width = w_qkv.shape[2]
    heads = local_width // HD
    reach = REACH // heads
    width = w_qkv.shape[0]
    packs = pack_lengths.shape[0]
    bf16 = jnp.bfloat16

    parts = [tokens] + [paired(tokens, "tp", bit) for bit in range(1, tp)]
    weights = jnp.transpose(w_qkv, (1, 0, 2))
    gain, bias = norm_gain.reshape(1, -1), norm_bias.reshape(1, -1)

    page_shapes = [(2 * PAGE + NOTES, HD), (2 * PAGE, HD)] * heads
    whole = lambda shape: pl.BlockSpec(shape, lambda i: (0,) * len(shape))
    normed, *own = pl.pallas_call(
        functools.partial(key_value_kernel, tp, heads),
        grid=(2,),
        out_shape=[jax.ShapeDtypeStruct((rows, width), bf16)] + [jax.ShapeDtypeStruct(shape, bf16) for shape in page_shapes],
        in_specs=[SMEM, SMEM, whole((1, rows))]
        + [whole((rows, features))] * tp
        + [whole((1, width))] * 2
        + [pl.BlockSpec((1, width, local_width), lambda i: (i + 1, 0, 0))],
        out_specs=[whole((rows, width))] + [whole(shape) for shape in page_shapes],
        scratch_shapes=[pltpu.VMEM((rows, local_width), bf16)],
        compiler_params=pltpu.CompilerParams(vmem_limit_bytes=24 << 20),
        cost_estimate=cost(4 * rows * width * local_width, 4 * width * local_width),
        name="norm_keys_values",
    )(pack_lengths, page_table, segment_ids.reshape(1, rows), *parts, gain, bias, weights)

    received = [
        [own[page]] + [paired(own[2 * bit + page], "req", bit) for bit in range(1, heads)]
        for page in range(2)
    ]
    layers = [[jnp.stack(pieces) for pieces in received]]

    queries = pl.pallas_call(
        functools.partial(query_kernel, heads),
        grid=(1,),
        out_shape=[jax.ShapeDtypeStruct((rows, HD), bf16)] * heads,
        in_specs=[
            whole((rows, width)),
            pl.BlockSpec((1, width, local_width), lambda i: (0, 0, 0)),
        ],
        out_specs=[whole((rows, HD))] * heads,
        scratch_shapes=[pltpu.VMEM((rows, local_width), bf16)],
        compiler_params=pltpu.CompilerParams(vmem_limit_bytes=24 << 20),
        cost_estimate=cost(2 * rows * width * local_width, 2 * width * local_width),
        name="queries",
    )(normed, weights)
    queries = [queries[0]] + [paired(queries[bit], "req", bit) for bit in range(1, heads)]

    for _ in range(reach):
        layers.append([forward(buffer, "req", heads) for buffer in layers[-1]])

    state_shape = [
        jax.ShapeDtypeStruct((heads, rows, HD), jnp.float32),
        jax.ShapeDtypeStruct((heads, rows, 2 * HD), jnp.float32),
    ]

    def attend(tiles, state, last, cache_page):
        pairs = heads * rows * heads * PAGE * len(tiles)
        operands = (
            list(queries)
            + [layers[layer][0] for layer in noted_layers(reach, tiles, cache_page)]
            + [layers[layer][page] for layer, page in page_list(reach, tiles, cache_page)]
            + list(state)
        )
        if last:
            outs = [jax.ShapeDtypeStruct((rows + 2 * PAGE, HD), bf16)] * heads
        else:
            outs = state_shape + (
                [jax.ShapeDtypeStruct((2 * PAGE, HD), bf16)] * heads
                if cache_page is not None
                else []
            )
        return pl.pallas_call(
            functools.partial(
                attend_kernel, heads, reach, packs, tiles, not state, last, cache_page
            ),
            out_shape=outs,
            in_specs=[VMEM] * len(operands),
            out_specs=[VMEM] * len(outs),
            compiler_params=pltpu.CompilerParams(vmem_limit_bytes=32 << 20),
            cost_estimate=cost(6 * pairs * HD, 4 << 20, pairs),
            name="attend",
        )(*operands)

    state = attend([(0, 0), (0, 1)], [], False, None)
    for layer in range(1, reach):
        state = attend([(layer, 0), (layer, 1)], state, False, None)
    *state, = attend([(reach, 0)], state, False, 0)
    state, early = state[:2], state[2:]
    early = [early[0]] + [paired(early[bit], "req", bit) for bit in range(1, heads)]
    final = attend([(reach, 1)], state, True, 1)
    final = [final[0]] + [paired(final[bit], "req", bit) for bit in range(1, heads)]

    context, cache = pl.pallas_call(
        functools.partial(finish_kernel, heads),
        out_shape=[
            jax.ShapeDtypeStruct((rows, local_width), bf16),
            jax.ShapeDtypeStruct((4, 2, PAGE, local_width), bf16),
        ],
        in_specs=[SMEM, SMEM] + [VMEM] * (4 * heads),
        out_specs=[VMEM] * 2,
        compiler_params=pltpu.CompilerParams(vmem_limit_bytes=16 << 20),
        name="finish",
    )(page_table, pack_lengths, *final, *early, *own)
    return context, cache


def solution(mesh):
    return jax.shard_map(
        per_device,
        mesh=mesh,
        in_specs=(P("req", "tp"), P(), P(), P(None, None, "tp"), P("req"), P(), P("req", None)),
        out_specs=(P("req", "tp"), P("req", None, None, "tp")),
        check_vma=False,
    )
```

time: 281 us -> 74.4 us (0.26)
  starting transfers between devices: 166 us -> 35.1 us
  local copies, waits for them, and re-layouts: 43.3 us -> 6.57 us
  matrix products: 32.8 us -> 0 us
  Pallas kernels: 0 us -> 17.1 us
  between operations: 15.8 us -> 1.46 us
  other arithmetic: 10.7 us -> 0.07 us
  waiting for transfers between devices: 10.4 us -> 13.7 us
    ppermute x32 -> x20, starting transfers between devices: 166 us -> 35.1 us  [the longest x16 19.3 us: paired(): return lax.ppermute(shard, axis, [(i, i ^ bit) for i in range(devices)])]
    dot_general x11 -> x0, matrix products: 24.2 us -> none  [the longest x9 12.3 us: per_device(): jnp.einsum('sj,cjpx->scpx', chosen, stacked, preferred_element_type=jnp.f...]
    unnamed x58 -> x12, local copies, waits for them, and re-layouts: 25.5 us -> 5.19 us
    pallas_call x0 -> x7, Pallas kernels: none -> 17.1 us  [the longest x4 10.4 us: attend(): pl.pallas_call(functools.partial(attend_kernel, heads, reach, packs, tile...]
    another operation x16 -> x0, local copies, waits for them, and re-layouts: 11.1 us -> none  [per_device(): jnp.stack([block_tuple[0], block_tuple[1]])]
    sub x1 -> x0, matrix products: 8.62 us -> none  [per_device(): exp_scores = jnp.exp(scores - row_max)]
    convert_element_type x6 -> x0, other arithmetic: 3.48 us -> none  [the longest x2 1.57 us: per_device(): key_rows = jnp.where(in_length, projected[:, 1], 0.0).astype(jnp.bfloat16)]
    ppermute x32 -> x20, waiting for transfers between devices: 10.4 us -> 13.7 us  [the longest x16 8.96 us: paired(): return lax.ppermute(shard, axis, [(i, i ^ bit) for i in range(devices)])]
  transfers between devices with their start and end apart: 33 -> 20, of which waited for: 10 -> 8; matrix products, arithmetic and copies ran while one was open for 15% -> 2% of each run, Pallas kernels for 0% -> 15%
where the time goes in v1:
time: 74.4 us; the launch traced here: 74 us
  starting transfers between devices  35.1 us (47%)
  Pallas kernels  17.1 us (23%)
  waiting for transfers between devices  13.7 us (18%)
  local copies, waits for them, and re-layouts  6.57 us (9%)
  between operations  1.46 us (2%)
    ppermute x16, starting transfers between devices, paired(): return lax.ppermute(shard, axis, [(i, i ^ bit) for i in range(devices)])  19.3 us
    ppermute x4, starting transfers between devices, forward(): return lax.ppermute(shard, axis, [(i, i + by) for i in range(devices - by)])  15.8 us
    pallas_call x4, Pallas kernels, attend(): pl.pallas_call(functools.partial(attend_kernel, heads, reach, packs, tile...  10.4 us
    ppermute x16, waiting for transfers between devices, paired(): return lax.ppermute(shard, axis, [(i, i ^ bit) for i in range(devices)])  8.96 us
    unnamed x12, local copies, waits for them, and re-layouts  5.19 us
    ppermute x4, waiting for transfers between devices, forward(): return lax.ppermute(shard, axis, [(i, i + by) for i in range(devices - by)])  4.74 us
    pallas_call x1, Pallas kernels, per_device(): pl.pallas_call(functools.partial(key_value_kernel, tp, heads), grid=(2,),...  4.06 us
    pallas_call x1, Pallas kernels, per_device(): pl.pallas_call(functools.partial(finish_kernel, heads), out_shape=[jax.Sh...  1.96 us
  transfers between devices with their start and end apart: 20, of which 8 were waited for; matrix products, arithmetic and copies ran while one was open for 2% of the time, Pallas kernels for 15%

profile of v1, /device:TPU:0, one launch (start us, length us, event | category | flops | bytes accessed | tf_op | source)
XLA Modules:
  0.0 74.0 jit_solution(7375672733202195581)
XLA Ops:
  3.2 2.8 %copy-done = bf16[2048,3,512]{2,0,1:T(8,128)(2,1)S(1)} copy-done((bf16[2048,3,512]{2,0,1:T(8,128)(2,1)S(1)}, bf16[2048,3,512]{2,0,1:T(8,128)(2,1)}, u32[]{:S(2)}) %copy-start) | copy-done | bytes 6291480
  6.0 1.0 %copy-done.2 = bf16[256,1024]{1,0:T(8,128)(2,1)S(1)} copy-done((bf16[256,1024]{1,0:T(8,128)(2,1)S(1)}, bf16[256,1024]{1,0:T(8,128)(2,1)}, u32[]{:S(2)}) %copy-start.2) | copy-done | bytes 524312
  8.4 4.1 %norm_keys_values.1 = (bf16[256,2048]{1,0:T(8,128)(2,1)S(1)}, bf16[272,128]{1,0:T(8,128)(2,1)S(1)}, bf16[256,128]{1,0:T(8,128)(2,1)S(1)}, bf16[272,128]{1,0:T(8,...) custom-call(s32[1]{0:T(128)S(6)} %copy.9.lengths_ref, ...), custom_call_target="tpu_custom_call" | custom-call | flops 1073741824 | bytes 4194304 | tf_op jit(solution)/shard_map/norm_keys_values/pallas_call | solution.py:244
  12.5 2.6 %collective-permute-start.4 = (bf16[272,128]{1,0:T(8,128)(2,1)S(1)}, bf16[272,128]{1,0:T(8,128)(2,1)S(1)}, u32[]{:S(2)}, u32[]{:S(2)}) collective-permute-start(bf16[272,128]{1,0:T(8,128)(2,1)S(1)} %get-tuple-element.35.refs_10_), channel_id=1, source_target_pairs={{0,2},{2,0},{4,6},{6,4},{8,10},{10,8},{12,14},{14,12},{16,18},{18,... | collective-permute-start | bytes 208904 | tf_op jit(solution)/shard_map/ppermute | solution.py:20
  15.1 1.5 %collective-permute-start.5 = (bf16[272,128]{1,0:T(8,128)(2,1)S(1)}, bf16[272,128]{1,0:T(8,128)(2,1)S(1)}, u32[]{:S(2)}, u32[]{:S(2)}) collective-permute-start(bf16[272,128]{1,0:T(8,128)(2,1)S(1)} %get-tuple-element.36.refs_12_), channel_id=1, source_target_pairs={{0,4},{2,6},{4,0},{6,2},{8,12},{10,14},{12,8},{14,10},{16,20},{18,... | collective-permute-start | bytes 208904 | tf_op jit(solution)/shard_map/ppermute | solution.py:20
  16.6 1.9 %collective-permute-start.9 = (bf16[256,128]{1,0:T(8,128)(2,1)S(1)}, bf16[256,128]{1,0:T(8,128)(2,1)S(1)}, u32[]{:S(2)}, u32[]{:S(2)}) collective-permute-start(bf16[256,128]{1,0:T(8,128)(2,1)S(1)} %get-tuple-element.39.refs_11_), channel_id=1, source_target_pairs={{0,2},{2,0},{4,6},{6,4},{8,10},{10,8},{12,14},{14,12},{16,18},{18,... | collective-permute-start | bytes 196616 | tf_op jit(solution)/shard_map/ppermute | solution.py:20
  18.6 1.5 %collective-permute-start.10 = (bf16[256,128]{1,0:T(8,128)(2,1)S(1)}, bf16[256,128]{1,0:T(8,128)(2,1)S(1)}, u32[]{:S(2)}, u32[]{:S(2)}) collective-permute-start(bf16[256,128]{1,0:T(8,128)(2,1)S(1)} %get-tuple-element.40.refs_13_), channel_id=1, source_target_pairs={{0,4},{2,6},{4,0},{6,2},{8,12},{10,14},{12,8},{14,10},{16,20},{18,... | collective-permute-start | bytes 196616 | tf_op jit(solution)/shard_map/ppermute | solution.py:20
  20.6 1.5 %collective-permute-done.6 = bf16[272,128]{1,0:T(8,128)(2,1)S(1)} collective-permute-done((bf16[272,128]{1,0:T(8,128)(2,1)S(1)}, bf16[272,128]{1,0:T(8,128)(2,1)S(1)}, u32[]{:S(2)}, u32[]{:S(2)}) %collective-permute-start.6) | collective-permute-done | bytes 69664 | tf_op jit(solution)/shard_map/ppermute | solution.py:20
  22.2 3.5 %collective-permute-start.7 = (bf16[4,272,128]{2,1,0:T(8,128)(2,1)S(1)}, bf16[4,272,128]{2,1,0:T(8,128)(2,1)S(1)}, u32[]{:S(2)}, u32[]{:S(2)}) collective-permute-start(bf16[4,272,128]{2,1,0:T(8,128)(2,1)S(1)} %pad_maximum_fusion.refs_4_), channel_id=1, source_target_pairs={{0,8},{2,10},{4,12},{6,14},{8,16},{10,18},{12,20},{14,22},{16,24},... | collective-permute-start | bytes 835592 | tf_op jit(solution)/shard_map/ppermute | solution.py:25
  25.8 3.5 %collective-permute-start.12 = (bf16[4,256,128]{2,1,0:T(8,128)(2,1)S(1)}, bf16[4,256,128]{2,1,0:T(8,128)(2,1)S(1)}, u32[]{:S(2)}, u32[]{:S(2)}) collective-permute-start(bf16[4,256,128]{2,1,0:T(8,128)(2,1)S(1)} %pad_maximum_fusion.1.refs_5_.refs_7_), channel_id=1, source_target_pairs={{0,8},{2,10},{4,12},{6,14},{8,16},{10,18},{12,20},{14,22},{16,24},... | collective-permute-start | bytes 786440 | tf_op jit(solution)/shard_map/ppermute | solution.py:25
  29.3 3.5 %collective-permute-done.7.refs_5_ = bf16[4,272,128]{2,1,0:T(8,128)(2,1)S(1)} collective-permute-done((bf16[4,272,128]{2,1,0:T(8,128)(2,1)S(1)}, bf16[4,272,128]{2,1,0:T(8,128)(2,1)S(1)}, u32[]{:S(2)}, u32[]{:S(2)}) %collective-permute-start.7) | collective-permute-done | bytes 278560 | tf_op jit(solution)/shard_map/ppermute | solution.py:25
  32.8 4.4 %collective-permute-start.8 = (bf16[4,272,128]{2,1,0:T(8,128)(2,1)S(1)}, bf16[4,272,128]{2,1,0:T(8,128)(2,1)S(1)}, u32[]{:S(2)}, u32[]{:S(2)}) collective-permute-start(bf16[4,272,128]{2,1,0:T(8,128)(2,1)S(1)} %collective-permute-done.7.refs_5_), channel_id=1, source_target_pairs={{0,8},{2,10},{4,12},{6,14},{8,16},{10,18},{12,20},{14,22},{16,24},... | collective-permute-start | bytes 835592 | tf_op jit(solution)/shard_map/ppermute | solution.py:25
  37.2 1.2 %collective-permute-done.12.refs_6_.refs_8_ = bf16[4,256,128]{2,1,0:T(8,128)(2,1)S(1)} collective-permute-done((bf16[4,256,128]{2,1,0:T(8,128)(2,1)S(1)}, bf16[4,256,128]{2,1,0:T(8,128)(2,1)S(1)}, u32[]{:S(2)}, u32[]{:S(2)}) %collective-permute-start.12) | collective-permute-done | bytes 262176 | tf_op jit(solution)/shard_map/ppermute | solution.py:25
  38.4 4.4 %collective-permute-start.13 = (bf16[4,256,128]{2,1,0:T(8,128)(2,1)S(1)}, bf16[4,256,128]{2,1,0:T(8,128)(2,1)S(1)}, u32[]{:S(2)}, u32[]{:S(2)}) collective-permute-start(bf16[4,256,128]{2,1,0:T(8,128)(2,1)S(1)} %collective-permute-done.12.refs_6_.refs_8_), channel_id=1, source_target_pairs={{0,8},{2,10},{4,12},{6,14},{8,16},{10,18},{12,20},{14,22},{16,24},... | collective-permute-start | bytes 786440 | tf_op jit(solution)/shard_map/ppermute | solution.py:25
  42.8 0.8 %queries.1 = (bf16[256,128]{1,0:T(8,128)(2,1)S(1)}, bf16[256,128]{1,0:T(8,128)(2,1)S(1)}, bf16[256,128]{1,0:T(8,128)(2,1)S(1)}, bf16[256,128]{1,0:T(8,128)(2,1)S(1)}) custom-call(bf16[256,2048]{1,0:T(8,128)(2,1)S(1)} %get-tuple-element.29.normed_ref, bf16[3,2048,512]{2,1,0:T(8,128)(2,1)S(1)} %bitcast.11), custom_call_target="tpu_custom_call" | custom-call | flops 536870912 | bytes 2097152 | tf_op jit(solution)/shard_map/queries/pallas_call | solution.py:265
  44.3 0.8 %collective-permute-start.2 = (bf16[256,128]{1,0:T(8,128)(2,1)S(1)}, bf16[256,128]{1,0:T(8,128)(2,1)S(1)}, u32[]{:S(2)}, u32[]{:S(2)}) collective-permute-start(bf16[256,128]{1,0:T(8,128)(2,1)S(1)} %get-tuple-element.32), channel_id=1, source_target_pairs={{0,4},{2,6},{4,0},{6,2},{8,12},{10,14},{12,8},{14,10},{16,20},{18,... | collective-permute-start | bytes 196616 | tf_op jit(solution)/shard_map/ppermute | solution.py:20
  45.1 2.1 %collective-permute-start.3 = (bf16[256,128]{1,0:T(8,128)(2,1)S(1)}, bf16[256,128]{1,0:T(8,128)(2,1)S(1)}, u32[]{:S(2)}, u32[]{:S(2)}) collective-permute-start(bf16[256,128]{1,0:T(8,128)(2,1)S(1)} %get-tuple-element.33), channel_id=1, source_target_pairs={{0,6},{2,4},{4,2},{6,0},{8,14},{10,12},{12,10},{14,8},{16,22},{18,... | collective-permute-start | bytes 196616 | tf_op jit(solution)/shard_map/ppermute | solution.py:20
  47.1 0.8 %collective-permute-done.1.refs_1_ = bf16[256,128]{1,0:T(8,128)(2,1)S(1)} collective-permute-done((bf16[256,128]{1,0:T(8,128)(2,1)S(1)}, bf16[256,128]{1,0:T(8,128)(2,1)S(1)}, u32[]{:S(2)}, u32[]{:S(2)}) %collective-permute-start.1) | collective-permute-done | bytes 65568 | tf_op jit(solution)/shard_map/ppermute | solution.py:20
  48.6 1.7 %collective-permute-done.3.refs_3_ = bf16[256,128]{1,0:T(8,128)(2,1)S(1)} collective-permute-done((bf16[256,128]{1,0:T(8,128)(2,1)S(1)}, bf16[256,128]{1,0:T(8,128)(2,1)S(1)}, u32[]{:S(2)}, u32[]{:S(2)}) %collective-permute-start.3) | collective-permute-done | bytes 65568 | tf_op jit(solution)/shard_map/ppermute | solution.py:20
  50.2 2.4 %attend.4 = (f32[4,256,128]{2,1,0:T(8,128)S(1)}, f32[4,256,256]{2,1,0:T(8,128)S(1)}) custom-call(bf16[256,128]{1,0:T(8,128)(2,1)S(1)} %get-tuple-element.30.refs_0_, bf16[256,128]{1,0:T(8,128)(2,1)S(1)} %collective-permute-done.1.refs_1_, bf16[256,128]{1,0:T(8,128)(2,1)S(1)} %collective-permute-done.2.refs_2_, ...), custom_call_target="tpu_custom_call" | custom-call | flops 805306368 | bytes 4194304 | tf_op jit(solution)/shard_map/attend/pallas_call | solution.py:305
  52.6 3.1 %attend.5 = (f32[4,256,128]{2,1,0:T(8,128)S(1)}, f32[4,256,256]{2,1,0:T(8,128)S(1)}) custom-call(bf16[256,128]{1,0:T(8,128)(2,1)S(1)} %get-tuple-element.30.refs_0_, bf16[256,128]{1,0:T(8,128)(2,1)S(1)} %collective-permute-done.1.refs_1_, bf16[256,128]{1,0:T(8,128)(2,1)S(1)} %collective-permute-done.2.refs_2_, ...), custom_call_target="tpu_custom_call" | custom-call | flops 805306368 | bytes 4194304 | tf_op jit(solution)/shard_map/attend/pallas_call | solution.py:305
  55.8 2.4 %attend.6 = (f32[4,256,128]{2,1,0:T(8,128)S(1)}, f32[4,256,256]{2,1,0:T(8,128)S(1)}, bf16[256,128]{1,0:T(8,128)(2,1)S(1)}, bf16[256,128]{1,0:T(8,128)(2,1)S(1)},...) custom-call(bf16[256,128]{1,0:T(8,128)(2,1)S(1)} %get-tuple-element.30.refs_0_, ...), custom_call_target="tpu_custom_call" | custom-call | flops 402653184 | bytes 4194304 | tf_op jit(solution)/shard_map/attend/pallas_call | solution.py:305
  58.2 1.2 %collective-permute-start.17 = (bf16[256,128]{1,0:T(8,128)(2,1)S(1)}, bf16[256,128]{1,0:T(8,128)(2,1)S(1)}, u32[]{:S(2)}, u32[]{:S(2)}) collective-permute-start(bf16[256,128]{1,0:T(8,128)(2,1)S(1)} %get-tuple-element.53), channel_id=1, source_target_pairs={{0,2},{2,0},{4,6},{6,4},{8,10},{10,8},{12,14},{14,12},{16,18},{18,... | collective-permute-start | bytes 196616 | tf_op jit(solution)/shard_map/ppermute | solution.py:20
  59.4 2.5 %attend.7 = (bf16[512,128]{1,0:T(8,128)(2,1)S(1)}, bf16[512,128]{1,0:T(8,128)(2,1)S(1)}, bf16[512,128]{1,0:T(8,128)(2,1)S(1)}, bf16[512,128]{1,0:T(8,128)(2,1)S(1)}) custom-call(bf16[256,128]{1,0:T(8,128)(2,1)S(1)} %get-tuple-element.30.refs_0_, bf16[256,128]{1,0:T(8,128)(2,1)S(1)} %collective-permute-done.1.refs_1_, ...), custom_call_target="tpu_custom_call" | custom-call | flops 402653184 | bytes 4194304 | tf_op jit(solution)/shard_map/attend/pallas_call | solution.py:305
  61.9 0.9 %collective-permute-start.14 = (bf16[512,128]{1,0:T(8,128)(2,1)S(1)}, bf16[512,128]{1,0:T(8,128)(2,1)S(1)}, u32[]{:S(2)}, u32[]{:S(2)}) collective-permute-start(bf16[512,128]{1,0:T(8,128)(2,1)S(1)} %get-tuple-element.49), channel_id=1, source_target_pairs={{0,2},{2,0},{4,6},{6,4},{8,10},{10,8},{12,14},{14,12},{16,18},{18,... | collective-permute-start | bytes 393224 | tf_op jit(solution)/shard_map/ppermute | solution.py:20
  62.8 1.2 %collective-permute-start.15 = (bf16[512,128]{1,0:T(8,128)(2,1)S(1)}, bf16[512,128]{1,0:T(8,128)(2,1)S(1)}, u32[]{:S(2)}, u32[]{:S(2)}) collective-permute-start(bf16[512,128]{1,0:T(8,128)(2,1)S(1)} %get-tuple-element.50), channel_id=1, source_target_pairs={{0,4},{2,6},{4,0},{6,2},{8,12},{10,14},{12,8},{14,10},{16,20},{18,... | collective-permute-start | bytes 393224 | tf_op jit(solution)/shard_map/ppermute | solution.py:20
  64.0 1.4 %collective-permute-start.16 = (bf16[512,128]{1,0:T(8,128)(2,1)S(1)}, bf16[512,128]{1,0:T(8,128)(2,1)S(1)}, u32[]{:S(2)}, u32[]{:S(2)}) collective-permute-start(bf16[512,128]{1,0:T(8,128)(2,1)S(1)} %get-tuple-element.51), channel_id=1, source_target_pairs={{0,6},{2,4},{4,2},{6,0},{8,14},{10,12},{12,10},{14,8},{16,22},{18,... | collective-permute-start | bytes 393224 | tf_op jit(solution)/shard_map/ppermute | solution.py:20
  65.4 1.5 %collective-permute-start.18 = (bf16[256,128]{1,0:T(8,128)(2,1)S(1)}, bf16[256,128]{1,0:T(8,128)(2,1)S(1)}, u32[]{:S(2)}, u32[]{:S(2)}) collective-permute-start(bf16[256,128]{1,0:T(8,128)(2,1)S(1)} %get-tuple-element.54), channel_id=1, source_target_pairs={{0,4},{2,6},{4,0},{6,2},{8,12},{10,14},{12,8},{14,10},{16,20},{18,... | collective-permute-start | bytes 196616 | tf_op jit(solution)/shard_map/ppermute | solution.py:20
  66.9 0.9 %collective-permute-start.19 = (bf16[256,128]{1,0:T(8,128)(2,1)S(1)}, bf16[256,128]{1,0:T(8,128)(2,1)S(1)}, u32[]{:S(2)}, u32[]{:S(2)}) collective-permute-start(bf16[256,128]{1,0:T(8,128)(2,1)S(1)} %get-tuple-element.55), channel_id=1, source_target_pairs={{0,6},{2,4},{4,2},{6,0},{8,14},{10,12},{12,10},{14,8},{16,22},{18,... | collective-permute-start | bytes 196616 | tf_op jit(solution)/shard_map/ppermute | solution.py:20
  67.8 2.8 %collective-permute-done.18.refs_6_ = bf16[256,128]{1,0:T(8,128)(2,1)S(1)} collective-permute-done((bf16[256,128]{1,0:T(8,128)(2,1)S(1)}, bf16[256,128]{1,0:T(8,128)(2,1)S(1)}, u32[]{:S(2)}, u32[]{:S(2)}) %collective-permute-start.18) | collective-permute-done | bytes 65568 | tf_op jit(solution)/shard_map/ppermute | solution.py:20
  70.6 1.4 %collective-permute-done.19.refs_7_ = bf16[256,128]{1,0:T(8,128)(2,1)S(1)} collective-permute-done((bf16[256,128]{1,0:T(8,128)(2,1)S(1)}, bf16[256,128]{1,0:T(8,128)(2,1)S(1)}, u32[]{:S(2)}, u32[]{:S(2)}) %collective-permute-start.19) | collective-permute-done | bytes 65568 | tf_op jit(solution)/shard_map/ppermute | solution.py:20
  72.1 2.0 %finish.1 = (bf16[256,512]{1,0:T(8,128)(2,1)}, bf16[4,2,128,512]{3,2,1,0:T(8,128)(2,1)}) custom-call(s32[2,2]{1,0:T(2,128)S(1)} %copy-done.4, s32[1]{0:T(128)S(6)} %copy.9.lengths_ref, bf16[512,128]{1,0:T(8,128)(2,1)S(1)} %get-tuple-element.48.refs_0_, bf16[512,128]{1,0:T(8,128)(2,1)S(1)} %collective-permute-done.14.refs_1_, ...), custom_call_target="tpu_custom_call" | custom-call | tf_op jit(solution)/shard_map/finish/pallas_call | solution.py:326
  (31 shorter events, 5.3 us)
Async XLA Ops:
  0.6 2.6 %collective-permute-start = (bf16[256,1024]{1,0:T(8,128)(2,1)}, bf16[256,1024]{1,0:T(8,128)(2,1)S(1)}, u32[]{:S(2)}, u32[]{:S(2)}) collective-permute-start(bf16[256,1024]{1,0:T(8,128)(2,1)} %refs_0_.1), channel_id=1, source_target_pairs={{0,1},{1,0},{2,3},{3,2},{4,5},{5,4},{6,7},{7,6},{8,9},{9,8},{10,11... | collective-permute-start | bytes 1572872 | tf_op jit(solution)/shard_map/ppermute | solution.py:20
  3.2 2.8 %copy-start = (bf16[2048,3,512]{2,0,1:T(8,128)(2,1)S(1)}, bf16[2048,3,512]{2,0,1:T(8,128)(2,1)}, u32[]{:S(2)}) copy-start(bf16[2048,3,512]{2,0,1:T(8,128)(2,1)} %param.10) | copy-start | bytes 18874372
  6.0 1.0 %copy-start.2 = (bf16[256,1024]{1,0:T(8,128)(2,1)S(1)}, bf16[256,1024]{1,0:T(8,128)(2,1)}, u32[]{:S(2)}) copy-start(bf16[256,1024]{1,0:T(8,128)(2,1)} %refs_0_.1) | copy-start | bytes 1572868
  7.0 0.7 copy-start.3
  7.7 0.7 copy-start.5
  8.4 34.4 %copy-start.1 = (bf16[2048,3,512]{2,0,1:T(8,128)(2,1)S(1)}, bf16[2048,3,512]{2,0,1:T(8,128)(2,1)}, u32[]{:S(2)}) copy-start(bf16[2048,3,512]{2,0,1:T(8,128)(2,1)} %param.10) | copy-start | bytes 18874372
  12.5 7.6 %collective-permute-start.4 = (bf16[272,128]{1,0:T(8,128)(2,1)S(1)}, bf16[272,128]{1,0:T(8,128)(2,1)S(1)}, u32[]{:S(2)}, u32[]{:S(2)}) collective-permute-start(bf16[272,128]{1,0:T(8,128)(2,1)S(1)} %get-tuple-element.35.refs_10_), channel_id=1, source_target_pairs={{0,2},{2,0},{4,6},{6,4},{8,10},{10,8},{12,14},{14,12},{16,18},{18,... | collective-permute-start | bytes 208904 | tf_op jit(solution)/shard_map/ppermute | solution.py:20
  15.1 5.5 %collective-permute-start.5 = (bf16[272,128]{1,0:T(8,128)(2,1)S(1)}, bf16[272,128]{1,0:T(8,128)(2,1)S(1)}, u32[]{:S(2)}, u32[]{:S(2)}) collective-permute-start(bf16[272,128]{1,0:T(8,128)(2,1)S(1)} %get-tuple-element.36.refs_12_), channel_id=1, source_target_pairs={{0,4},{2,6},{4,0},{6,2},{8,12},{10,14},{12,8},{14,10},{16,20},{18,... | collective-permute-start | bytes 208904 | tf_op jit(solution)/shard_map/ppermute | solution.py:20
  16.6 5.6 %collective-permute-start.6 = (bf16[272,128]{1,0:T(8,128)(2,1)S(1)}, bf16[272,128]{1,0:T(8,128)(2,1)S(1)}, u32[]{:S(2)}, u32[]{:S(2)}) collective-permute-start(bf16[272,128]{1,0:T(8,128)(2,1)S(1)} %get-tuple-element.37.refs_14_), channel_id=1, source_target_pairs={{0,6},{2,4},{4,2},{6,0},{8,14},{10,12},{12,10},{14,8},{16,22},{18,... | collective-permute-start | bytes 208904 | tf_op jit(solution)/shard_map/ppermute | solution.py:20
  16.6 9.1 %collective-permute-start.9 = (bf16[256,128]{1,0:T(8,128)(2,1)S(1)}, bf16[256,128]{1,0:T(8,128)(2,1)S(1)}, u32[]{:S(2)}, u32[]{:S(2)}) collective-permute-start(bf16[256,128]{1,0:T(8,128)(2,1)S(1)} %get-tuple-element.39.refs_11_), channel_id=1, source_target_pairs={{0,2},{2,0},{4,6},{6,4},{8,10},{10,8},{12,14},{14,12},{16,18},{18,... | collective-permute-start | bytes 196616 | tf_op jit(solution)/shard_map/ppermute | solution.py:20
  18.6 7.2 %collective-permute-start.10 = (bf16[256,128]{1,0:T(8,128)(2,1)S(1)}, bf16[256,128]{1,0:T(8,128)(2,1)S(1)}, u32[]{:S(2)}, u32[]{:S(2)}) collective-permute-start(bf16[256,128]{1,0:T(8,128)(2,1)S(1)} %get-tuple-element.40.refs_13_), channel_id=1, source_target_pairs={{0,4},{2,6},{4,0},{6,2},{8,12},{10,14},{12,8},{14,10},{16,20},{18,... | collective-permute-start | bytes 196616 | tf_op jit(solution)/shard_map/ppermute | solution.py:20
  20.1 5.6 %collective-permute-start.11 = (bf16[256,128]{1,0:T(8,128)(2,1)S(1)}, bf16[256,128]{1,0:T(8,128)(2,1)S(1)}, u32[]{:S(2)}, u32[]{:S(2)}) collective-permute-start(bf16[256,128]{1,0:T(8,128)(2,1)S(1)} %get-tuple-element.41.refs_15_), channel_id=1, source_target_pairs={{0,6},{2,4},{4,2},{6,0},{8,14},{10,12},{12,10},{14,8},{16,22},{18,... | collective-permute-start | bytes 196616 | tf_op jit(solution)/shard_map/ppermute | solution.py:20
  22.2 10.6 %collective-permute-start.7 = (bf16[4,272,128]{2,1,0:T(8,128)(2,1)S(1)}, bf16[4,272,128]{2,1,0:T(8,128)(2,1)S(1)}, u32[]{:S(2)}, u32[]{:S(2)}) collective-permute-start(bf16[4,272,128]{2,1,0:T(8,128)(2,1)S(1)} %pad_maximum_fusion.refs_4_), channel_id=1, source_target_pairs={{0,8},{2,10},{4,12},{6,14},{8,16},{10,18},{12,20},{14,22},{16,24},... | collective-permute-start | bytes 835592 | tf_op jit(solution)/shard_map/ppermute | solution.py:25
  25.8 12.6 %collective-permute-start.12 = (bf16[4,256,128]{2,1,0:T(8,128)(2,1)S(1)}, bf16[4,256,128]{2,1,0:T(8,128)(2,1)S(1)}, u32[]{:S(2)}, u32[]{:S(2)}) collective-permute-start(bf16[4,256,128]{2,1,0:T(8,128)(2,1)S(1)} %pad_maximum_fusion.1.refs_5_.refs_7_), channel_id=1, source_target_pairs={{0,8},{2,10},{4,12},{6,14},{8,16},{10,18},{12,20},{14,22},{16,24},... | collective-permute-start | bytes 786440 | tf_op jit(solution)/shard_map/ppermute | solution.py:25
  32.8 23.0 %collective-permute-start.8 = (bf16[4,272,128]{2,1,0:T(8,128)(2,1)S(1)}, bf16[4,272,128]{2,1,0:T(8,128)(2,1)S(1)}, u32[]{:S(2)}, u32[]{:S(2)}) collective-permute-start(bf16[4,272,128]{2,1,0:T(8,128)(2,1)S(1)} %collective-permute-done.7.refs_5_), channel_id=1, source_target_pairs={{0,8},{2,10},{4,12},{6,14},{8,16},{10,18},{12,20},{14,22},{16,24},... | collective-permute-start | bytes 835592 | tf_op jit(solution)/shard_map/ppermute | solution.py:25
  38.4 21.0 %collective-permute-start.13 = (bf16[4,256,128]{2,1,0:T(8,128)(2,1)S(1)}, bf16[4,256,128]{2,1,0:T(8,128)(2,1)S(1)}, u32[]{:S(2)}, u32[]{:S(2)}) collective-permute-start(bf16[4,256,128]{2,1,0:T(8,128)(2,1)S(1)} %collective-permute-done.12.refs_6_.refs_8_), channel_id=1, source_target_pairs={{0,8},{2,10},{4,12},{6,14},{8,16},{10,18},{12,20},{14,22},{16,24},... | collective-permute-start | bytes 786440 | tf_op jit(solution)/shard_map/ppermute | solution.py:25
  43.6 28.5 %copy-start.4 = (s32[2,2]{1,0:T(2,128)S(1)}, s32[2,2]{1,0:T(2,128)}, u32[]{:S(2)}) copy-start(s32[2,2]{1,0:T(2,128)} %table_ref.3) | copy-start | bytes 52
  43.6 4.3 %collective-permute-start.1 = (bf16[256,128]{1,0:T(8,128)(2,1)S(1)}, bf16[256,128]{1,0:T(8,128)(2,1)S(1)}, u32[]{:S(2)}, u32[]{:S(2)}) collective-permute-start(bf16[256,128]{1,0:T(8,128)(2,1)S(1)} %get-tuple-element.31), channel_id=1, source_target_pairs={{0,2},{2,0},{4,6},{6,4},{8,10},{10,8},{12,14},{14,12},{16,18},{18,... | collective-permute-start | bytes 196616 | tf_op jit(solution)/shard_map/ppermute | solution.py:20
  44.3 4.3 %collective-permute-start.2 = (bf16[256,128]{1,0:T(8,128)(2,1)S(1)}, bf16[256,128]{1,0:T(8,128)(2,1)S(1)}, u32[]{:S(2)}, u32[]{:S(2)}) collective-permute-start(bf16[256,128]{1,0:T(8,128)(2,1)S(1)} %get-tuple-element.32), channel_id=1, source_target_pairs={{0,4},{2,6},{4,0},{6,2},{8,12},{10,14},{12,8},{14,10},{16,20},{18,... | collective-permute-start | bytes 196616 | tf_op jit(solution)/shard_map/ppermute | solution.py:20
  45.1 5.2 %collective-permute-start.3 = (bf16[256,128]{1,0:T(8,128)(2,1)S(1)}, bf16[256,128]{1,0:T(8,128)(2,1)S(1)}, u32[]{:S(2)}, u32[]{:S(2)}) collective-permute-start(bf16[256,128]{1,0:T(8,128)(2,1)S(1)} %get-tuple-element.33), channel_id=1, source_target_pairs={{0,6},{2,4},{4,2},{6,0},{8,14},{10,12},{12,10},{14,8},{16,22},{18,... | collective-permute-start | bytes 196616 | tf_op jit(solution)/shard_map/ppermute | solution.py:20
  58.2 8.7 %collective-permute-start.17 = (bf16[256,128]{1,0:T(8,128)(2,1)S(1)}, bf16[256,128]{1,0:T(8,128)(2,1)S(1)}, u32[]{:S(2)}, u32[]{:S(2)}) collective-permute-start(bf16[256,128]{1,0:T(8,128)(2,1)S(1)} %get-tuple-element.53), channel_id=1, source_target_pairs={{0,2},{2,0},{4,6},{6,4},{8,10},{10,8},{12,14},{14,12},{16,18},{18,... | collective-permute-start | bytes 196616 | tf_op jit(solution)/shard_map/ppermute | solution.py:20
  61.9 10.2 %collective-permute-start.14 = (bf16[512,128]{1,0:T(8,128)(2,1)S(1)}, bf16[512,128]{1,0:T(8,128)(2,1)S(1)}, u32[]{:S(2)}, u32[]{:S(2)}) collective-permute-start(bf16[512,128]{1,0:T(8,128)(2,1)S(1)} %get-tuple-element.49), channel_id=1, source_target_pairs={{0,2},{2,0},{4,6},{6,4},{8,10},{10,8},{12,14},{14,12},{16,18},{18,... | collective-permute-start | bytes 393224 | tf_op jit(solution)/shard_map/ppermute | solution.py:20
  62.8 9.3 %collective-permute-start.15 = (bf16[512,128]{1,0:T(8,128)(2,1)S(1)}, bf16[512,128]{1,0:T(8,128)(2,1)S(1)}, u32[]{:S(2)}, u32[]{:S(2)}) collective-permute-start(bf16[512,128]{1,0:T(8,128)(2,1)S(1)} %get-tuple-element.50), channel_id=1, source_target_pairs={{0,4},{2,6},{4,0},{6,2},{8,12},{10,14},{12,8},{14,10},{16,20},{18,... | collective-permute-start | bytes 393224 | tf_op jit(solution)/shard_map/ppermute | solution.py:20
  64.0 8.0 %collective-permute-start.16 = (bf16[512,128]{1,0:T(8,128)(2,1)S(1)}, bf16[512,128]{1,0:T(8,128)(2,1)S(1)}, u32[]{:S(2)}, u32[]{:S(2)}) collective-permute-start(bf16[512,128]{1,0:T(8,128)(2,1)S(1)} %get-tuple-element.51), channel_id=1, source_target_pairs={{0,6},{2,4},{4,2},{6,0},{8,14},{10,12},{12,10},{14,8},{16,22},{18,... | collective-permute-start | bytes 393224 | tf_op jit(solution)/shard_map/ppermute | solution.py:20
  65.4 5.2 %collective-permute-start.18 = (bf16[256,128]{1,0:T(8,128)(2,1)S(1)}, bf16[256,128]{1,0:T(8,128)(2,1)S(1)}, u32[]{:S(2)}, u32[]{:S(2)}) collective-permute-start(bf16[256,128]{1,0:T(8,128)(2,1)S(1)} %get-tuple-element.54), channel_id=1, source_target_pairs={{0,4},{2,6},{4,0},{6,2},{8,12},{10,14},{12,8},{14,10},{16,20},{18,... | collective-permute-start | bytes 196616 | tf_op jit(solution)/shard_map/ppermute | solution.py:20
  66.9 5.2 %collective-permute-start.19 = (bf16[256,128]{1,0:T(8,128)(2,1)S(1)}, bf16[256,128]{1,0:T(8,128)(2,1)S(1)}, u32[]{:S(2)}, u32[]{:S(2)}) collective-permute-start(bf16[256,128]{1,0:T(8,128)(2,1)S(1)} %get-tuple-element.55), channel_id=1, source_target_pairs={{0,6},{2,4},{4,2},{6,0},{8,14},{10,12},{12,10},{14,8},{16,22},{18,... | collective-permute-start | bytes 196616 | tf_op jit(solution)/shard_map/ppermute | solution.py:20

commit v2 on v1

v2 whole, which is shorter than its diff:
```python
import functools
import jax
import jax.numpy as jnp
from jax import lax
from jax.experimental import pallas as pl
from jax.experimental.pallas import tpu as pltpu
from jax.sharding import PartitionSpec as P

HD = 128
PAGE = 128
REACH = 8
NOTES = 16
MASKED = -1e30
PROJECT_VMEM = 48 << 20
VMEM = pl.BlockSpec(memory_space=pltpu.VMEM)
SMEM = pl.BlockSpec(memory_space=pltpu.SMEM)
HBM = pl.BlockSpec(memory_space=pltpu.HBM)


def paired(shard, axis, bit):
    devices = lax.axis_size(axis)
    return lax.ppermute(shard, axis, [(i, i ^ bit) for i in range(devices)])


def forward(shard, axis, by):
    devices = lax.axis_size(axis)
    return lax.ppermute(shard, axis, [(i, i + by) for i in range(devices - by)])


def cost(flops, moved, transcendentals=0):
    return pl.CostEstimate(flops=flops, bytes_accessed=moved, transcendentals=transcendentals)


def valid_rows(lengths_ref, row_count):
    device = lax.axis_index("req")
    per_pack = lax.axis_size("req") // lengths_ref.shape[0]
    limit = lengths_ref[device // per_pack] - device % per_pack * row_count
    return lax.broadcasted_iota(jnp.int32, (row_count, 1), 0) < limit


def project_kernel(tp, heads, *refs):
    refs = list(refs)
    take = lambda count: [refs.pop(0) for _ in range(count)]
    lengths_ref, tokens_hbm, w_hbm, affine_ref, notes_ref = take(5)
    received, (normed_ref,), pieces = take(tp - 1), take(1), take(2 * heads)
    tokens_ref, w_ref, spread_ref, columns, sems = refs
    rows, features = tokens_ref.shape
    here = lax.axis_index("tp")
    me = lax.axis_index("req") % heads
    loads = [
        pltpu.make_async_copy(tokens_hbm, tokens_ref, sems.at[0]),
        pltpu.make_async_copy(w_hbm.at[1], w_ref.at[0], sems.at[1]),
        pltpu.make_async_copy(w_hbm.at[2], w_ref.at[1], sems.at[2]),
    ]
    for load in loads:
        load.start()
    lines = affine_ref.shape[0] // 2
    affine = affine_ref[...].astype(jnp.float32)
    for row in range(2):
        for line in range(lines):
            spread_ref[row : row + 1, line * HD : (line + 1) * HD] = affine[
                row * lines + line : row * lines + line + 1
            ]
    loads[0].wait()
    parts = [tokens_ref] + received
    step = 32

    def norm_rows(index, carry):
        at = pl.ds(pl.multiple_of(index * step, step), step)
        shares = [part[at, :].astype(jnp.float32) for part in parts]
        total = sum(jnp.sum(share, axis=1, keepdims=True) for share in shares)
        mean = total * (1.0 / (tp * features))
        centred = [share - mean for share in shares]
        squares = sum(jnp.sum(share * share, axis=1, keepdims=True) for share in centred)
        scale = lax.rsqrt(squares * (1.0 / (tp * features)) + 1e-05)
        for bit, share in enumerate(centred):
            lanes = pl.ds(pl.multiple_of((here ^ bit) * features, features), features)
            gain = spread_ref[0:1, lanes]
            bias = spread_ref[1:2, lanes]
            normed_ref[at, lanes] = (share * scale * gain + bias).astype(jnp.bfloat16)
        return carry

    lax.fori_loop(0, rows // step, norm_rows, 0)

    valid = valid_rows(lengths_ref, rows)
    for which in range(2):
        loads[1 + which].wait()
        projected = jnp.dot(normed_ref[...], w_ref[which], preferred_element_type=jnp.float32)
        columns[...] = jnp.where(valid, projected, 0.0).astype(jnp.bfloat16)
        for bit in range(heads):
            lanes = pl.ds(pl.multiple_of((me ^ bit) * HD, HD), HD)
            for page in range(2):
                pieces[2 * bit + page][which * PAGE : (which + 1) * PAGE, :] = columns[
                    page * PAGE : (page + 1) * PAGE, lanes
                ]

    for bit in range(heads):
        pieces[2 * bit][2 * PAGE :, :] = notes_ref[...]


def query_kernel(heads, normed_ref, w_hbm, *refs):
    pieces, (columns, w_ref, sem) = refs[:heads], refs[heads:]
    load = pltpu.make_async_copy(w_hbm.at[0], w_ref, sem)
    load.start()
    load.wait()
    me = lax.axis_index("req") % heads
    projected = jnp.dot(normed_ref[...], w_ref[...], preferred_element_type=jnp.float32)
    columns[...] = (projected * HD ** (-0.5)).astype(jnp.bfloat16)
    for bit in range(heads):
        pieces[bit][...] = columns[:, pl.ds(pl.multiple_of((me ^ bit) * HD, HD), HD)]


def attend_kernel(heads, reach, packs, tiles, first, last, cache_page, *refs):
    refs = list(refs)
    take = lambda count: [refs.pop(0) for _ in range(count)]
    queries = take(heads)
    noted = dict(zip(noted_layers(reach, tiles, cache_page), take(len(noted_layers(reach, tiles, cache_page)))))
    pages = dict(zip(page_list(reach, tiles, cache_page), take(len(page_list(reach, tiles, cache_page)))))
    pages.update({(layer, 0): buffer for layer, buffer in noted.items()})
    ids_ref, top_ref, total_ref = (None,) * 3 if first else take(3)
    if first:
        ids_ref = take(1)[0]
    top_out, total_out = (None,) * 2 if last else take(2)
    outs = refs
    device = lax.axis_index("req")
    per_pack = lax.axis_size("req") // packs
    me = device % heads
    rows = 2 * PAGE
    width = heads * PAGE
    notes = {
        layer: [buffer[bit, 2 * PAGE :, :].astype(jnp.float32) for bit in range(heads)]
        for layer, buffer in noted.items()
    }
    keys, values, key_ids, key_places = [], [], [], []
    ones = jnp.ones((width, HD), jnp.bfloat16)
    lane = lax.broadcasted_iota(jnp.int32, (1, PAGE), 1)
    for layer, page in tiles:
        buffer = pages[layer, page]
        keys.append(buffer[:, :PAGE].reshape(width, HD))
        values.append(
            jnp.concatenate([buffer[:, PAGE : 2 * PAGE].reshape(width, HD), ones], axis=1)
        )
        ids = jnp.concatenate([note[page : page + 1] for note in notes[layer]], axis=1)
        if layer > 0:
            same_pack = (device - layer * heads) // per_pack == device // per_pack
            ids = jnp.where(same_pack, ids, 0.0)
        key_ids.append(ids)
        key_places.append(
            jnp.concatenate(
                [lane + ((me ^ bit) * rows + page * PAGE) for bit in range(heads)], axis=1
            )
        )
    wide = (PAGE, HD)
    for bit in range(heads):
        for page in range(2):
            at = pl.ds(page * PAGE, PAGE)
            query = queries[bit][at, :]
            if first:
                query_ids = jnp.broadcast_to(notes[0][bit][page : page + 1], wide).T
                ids_ref[bit, at] = query_ids
                place = lax.broadcasted_iota(jnp.int32, wide, 0) + ((me ^ bit) * rows + page * PAGE)
                top = jnp.full(wide, MASKED, jnp.float32)
                total = [jnp.zeros(wide, jnp.float32)] * 2
            else:
                query_ids = ids_ref[bit, at]
                top = top_ref[bit, at]
                total = [total_ref[bit, at, half * HD : (half + 1) * HD] for half in range(2)]
            for index, (layer, _) in enumerate(tiles):
                scores = lax.dot_general(
                    query, keys[index], (((1,), (1,)), ((), ())), preferred_element_type=jnp.float32
                )
                chunks = []
                for other in range(heads):
                    lanes = slice(other * PAGE, (other + 1) * PAGE)
                    allowed = key_ids[index][:, lanes] == query_ids
                    if layer == 0:
                        allowed = allowed & (key_places[index][:, lanes] <= place)
                    chunks.append(jnp.where(allowed, scores[:, lanes], MASKED))
                highest = jnp.max(functools.reduce(jnp.maximum, chunks), axis=1, keepdims=True)
                higher = jnp.maximum(top, jnp.broadcast_to(highest, wide))
                weights = jnp.concatenate(
                    [jnp.exp(chunk - higher).astype(jnp.bfloat16) for chunk in chunks], axis=1
                )
                shrink = jnp.exp(top - higher)
                added = jnp.dot(weights, values[index], preferred_element_type=jnp.float32)
                total = [total[half] * shrink + added[:, half * HD : (half + 1) * HD] for half in range(2)]
                top = higher
            if last:
                outs[bit][at, :] = (total[0] / total[1]).astype(jnp.bfloat16)
            else:
                top_out[bit, at] = top
                for half in range(2):
                    total_out[bit, at, half * HD : (half + 1) * HD] = total[half]
    if cache_page is not None:
        select_pages(heads, reach, cache_page, device, notes, pages, outs, rows)


def select_pages(heads, reach, page, device, notes, pages, outs, start):
    me = device % heads
    sought = jnp.zeros((1, HD), jnp.int32)
    for bit in range(heads):
        owner = ((device ^ bit) + 1).astype(jnp.float32)
        for layer in range(reach + 1):
            for other in range(heads):
                if layer == 0 and other == bit:
                    continue
                note = notes[layer][other]
                at = 2 + 2 * page
                hit = (note[at : at + 1] == owner) & (note[at + 1 : at + 2] == page + 1.0)
                place = (layer * heads + other + 1) << (6 * bit)
                sought = sought | jnp.where(hit, place, 0)
    sought = jnp.max(sought)
    for bit in range(heads):
        found = ((sought >> (6 * bit)) & 63) - 1
        for layer in range(reach + 1):

            @pl.when((found >= layer * heads) & (found < (layer + 1) * heads))
            def _():
                outs[bit][start : start + 2 * PAGE, :] = pages[layer, page][
                    found - layer * heads, : 2 * PAGE, :
                ]

        @pl.when(found < 0)
        def _():
            outs[bit][start : start + 2 * PAGE, :] = jnp.zeros((2 * PAGE, HD), jnp.bfloat16)


def select_kernel(heads, reach, *refs):
    buffers, outs = refs[: reach + 1], refs[reach + 1 :]
    notes = [
        [buffer[bit, 2 * PAGE :, :].astype(jnp.float32) for bit in range(heads)]
        for buffer in buffers
    ]
    pages = {(layer, 0): buffer for layer, buffer in enumerate(buffers)}
    select_pages(heads, reach, 0, lax.axis_index("req"), notes, pages, outs, 0)


def noted_layers(reach, tiles, cache_page):
    layers = range(reach + 1) if cache_page is not None else [0] + [layer for layer, _ in tiles]
    return sorted(set(layers))


def page_list(reach, tiles, cache_page):
    wanted = list(tiles)
    if cache_page is not None:
        wanted += [(layer, cache_page) for layer in range(reach + 1)]
    return sorted(set(place for place in wanted if place[1] == 1))


def finish_kernel(heads, table_hbm, lengths_ref, *refs):
    refs = list(refs)
    take = lambda count: [refs.pop(0) for _ in range(count)]
    final, early, own = take(heads), take(heads), take(2 * heads)
    context_ref, cache_ref, table_ref, sem = refs
    load = pltpu.make_async_copy(table_hbm, table_ref, sem)
    load.start()
    load.wait()
    device = lax.axis_index("req")
    me = device % heads
    rows = context_ref.shape[0]
    valid = valid_rows(lengths_ref, rows)
    for bit in range(heads):
        lanes = pl.ds(pl.multiple_of((me ^ bit) * HD, HD), HD)
        context_ref[:, lanes] = jnp.where(valid, final[bit][0:rows, :], 0).astype(jnp.bfloat16)
        for part in range(2):
            first = part * PAGE
            cache_ref[0, part, :, lanes] = early[bit][first : first + PAGE, :]
            cache_ref[1, part, :, lanes] = final[bit][rows + first : rows + first + PAGE, :]
            for page in range(2):
                stays = (table_ref[page, 0] == device) & (table_ref[page, 1] == page + 2)
                cache_ref[2 + page, part, :, lanes] = jnp.where(
                    stays, own[2 * bit + page][first : first + PAGE, :], 0
                ).astype(jnp.bfloat16)


def per_device(tokens, norm_gain, norm_bias, w_qkv, segment_ids, pack_lengths, page_table):
    rows, features = tokens.shape
    tp = lax.axis_size("tp")
    local_width = w_qkv.shape[2]
    heads = local_width // HD
    reach = REACH // heads
    width = w_qkv.shape[0]
    packs = pack_lengths.shape[0]
    bf16 = jnp.bfloat16

    received = [paired(tokens, "tp", bit) for bit in range(1, tp)]
    weights = jnp.transpose(w_qkv, (1, 0, 2))
    affine = jnp.concatenate([norm_gain.reshape(-1, HD), norm_bias.reshape(-1, HD)])
    entries = jnp.broadcast_to(page_table.reshape(-1, 1), (page_table.size, HD))
    notes = jnp.concatenate([segment_ids.reshape(2, HD), entries]) + 1
    notes = jnp.pad(notes, ((0, NOTES - notes.shape[0]), (0, 0))).astype(bf16)

    piece_shapes = [(2 * PAGE + NOTES, HD), (2 * PAGE, HD)] * heads
    normed, *own = pl.pallas_call(
        functools.partial(project_kernel, tp, heads),
        out_shape=[jax.ShapeDtypeStruct((rows, width), bf16)]
        + [jax.ShapeDtypeStruct(shape, bf16) for shape in piece_shapes],
        in_specs=[SMEM] + [HBM] * 2 + [VMEM] * (1 + tp),
        out_specs=[VMEM] * (1 + 2 * heads),
        scratch_shapes=[
            pltpu.VMEM((rows, features), bf16),
            pltpu.VMEM((2, width, local_width), bf16),
            pltpu.VMEM((2, width), jnp.float32),
            pltpu.VMEM((rows, local_width), bf16),
            pltpu.SemaphoreType.DMA((3,)),
        ],
        compiler_params=pltpu.CompilerParams(vmem_limit_bytes=PROJECT_VMEM),
        cost_estimate=cost(4 * rows * width * local_width, 4 * width * local_width),
        name="project",
    )(pack_lengths, tokens, weights, affine, notes, *received)
    pages = [
        jnp.stack([own[page]] + [paired(own[2 * bit + page], "req", bit) for bit in range(1, heads)])
        for page in range(2)
    ]
    queries = pl.pallas_call(
        functools.partial(query_kernel, heads),
        out_shape=[jax.ShapeDtypeStruct((rows, HD), bf16)] * heads,
        in_specs=[VMEM, HBM],
        out_specs=[VMEM] * heads,
        scratch_shapes=[
            pltpu.VMEM((rows, local_width), bf16),
            pltpu.VMEM((width, local_width), bf16),
            pltpu.SemaphoreType.DMA,
        ],
        compiler_params=pltpu.CompilerParams(vmem_limit_bytes=24 << 20),
        cost_estimate=cost(2 * rows * width * local_width, 2 * width * local_width),
        name="queries",
    )(normed, weights)
    pages[0], queries = lax.optimization_barrier((pages[0], queries))
    layers = [pages]
    queries = [queries[0]] + [paired(queries[bit], "req", bit) for bit in range(1, heads)]

    def ahead(buffer):
        return forward(buffer, "req", heads)

    layers.append([ahead(buffer) for buffer in layers[0]])

    state_shape = [
        jax.ShapeDtypeStruct((heads, rows, HD), jnp.float32),
        jax.ShapeDtypeStruct((heads, rows, 2 * HD), jnp.float32),
    ]

    def attend(tiles, state, last, cache_page):
        pairs = heads * rows * heads * PAGE * len(tiles)
        operands = (
            list(queries)
            + [layers[layer][0] for layer in noted_layers(reach, tiles, cache_page)]
            + [layers[layer][page] for layer, page in page_list(reach, tiles, cache_page)]
            + list(state)
        )
        if last:
            outs = [jax.ShapeDtypeStruct((rows + 2 * PAGE, HD), bf16)] * heads
        else:
            outs = ([] if state else state_shape[:1]) + state_shape + (
                [jax.ShapeDtypeStruct((2 * PAGE, HD), bf16)] * heads
                if cache_page is not None
                else []
            )
        return pl.pallas_call(
            functools.partial(
                attend_kernel, heads, reach, packs, tiles, not state, last, cache_page
            ),
            out_shape=outs,
            in_specs=[VMEM] * len(operands),
            out_specs=[VMEM] * len(outs),
            compiler_params=pltpu.CompilerParams(vmem_limit_bytes=32 << 20),
            cost_estimate=cost(6 * pairs * HD, 4 << 20, pairs),
            name="attend",
        )(*operands)

    ids, *state = attend([(0, 0), (0, 1)], [], False, None)
    first_page = layers[1][0]
    second_page, state = lax.optimization_barrier((layers[1][1], state))
    for _ in range(1, reach):
        first_page, second_page = ahead(first_page), ahead(second_page)
        layers.append([first_page, second_page])
    for layer in range(1, reach):
        state = attend([(layer, 0), (layer, 1)], [ids, *state], False, None)
    early = pl.pallas_call(
        functools.partial(select_kernel, heads, reach),
        out_shape=[jax.ShapeDtypeStruct((2 * PAGE, HD), bf16)] * heads,
        in_specs=[VMEM] * (reach + 1),
        out_specs=[VMEM] * heads,
        compiler_params=pltpu.CompilerParams(vmem_limit_bytes=8 << 20),
        cost_estimate=cost(0, 1 << 20),
        name="select",
    )(*[layer[0] for layer in layers])
    early = [early[0]] + [paired(early[bit], "req", bit) for bit in range(1, heads)]
    final = attend([(reach, 0), (reach, 1)], [ids, *state], True, 1)
    final, near = lax.optimization_barrier((final, early[:-1]))
    early = near + early[-1:]
    final = [final[0]] + [paired(final[bit], "req", bit) for bit in range(1, heads)]

    context, cache = pl.pallas_call(
        functools.partial(finish_kernel, heads),
        out_shape=[
            jax.ShapeDtypeStruct((rows, local_width), bf16),
            jax.ShapeDtypeStruct((4, 2, PAGE, local_width), bf16),
        ],
        in_specs=[HBM, SMEM] + [VMEM] * (4 * heads),
        out_specs=[VMEM] * 2,
        scratch_shapes=[pltpu.SMEM((2, 2), jnp.int32), pltpu.SemaphoreType.DMA],
        compiler_params=pltpu.CompilerParams(vmem_limit_bytes=16 << 20),
        name="finish",
    )(page_table, pack_lengths, *final, *early, *own)
    return context, cache


def solution(mesh):
    return jax.shard_map(
        per_device,
        mesh=mesh,
        in_specs=(P("req", "tp"), P(), P(), P(None, None, "tp"), P("req"), P(), P("req", None)),
        out_specs=(P("req", "tp"), P("req", None, None, "tp")),
        check_vma=False,
    )
```

time: 74.4 us -> 57.6 us (0.77)
  waiting for transfers between devices: 13.7 us -> 5.38 us
  Pallas kernels: 17.1 us -> 12.2 us
  local copies, waits for them, and re-layouts: 6.57 us -> 1.9 us
  other arithmetic: 0.07 us -> 1.88 us
    pallas_call x4 -> x3, Pallas kernels: 10.4 us -> 5.43 us  [attend(): pl.pallas_call(functools.partial(attend_kernel, heads, reach, packs, tile...]
    ppermute x4, waiting for transfers between devices: 4.74 us -> 0.01 us  [forward(): return lax.ppermute(shard, axis, [(i, i + by) for i in range(devices - by)])]
    unnamed x12 -> x6, local copies, waits for them, and re-layouts: 5.19 us -> 1.05 us
    ppermute x16, waiting for transfers between devices: 8.96 us -> 5.37 us  [paired(): return lax.ppermute(shard, axis, [(i, i ^ bit) for i in range(devices)])]
    reshape x2 -> x0, local copies, waits for them, and re-layouts: 1.39 us -> none  [per_device(): gain, bias = (norm_gain.reshape(1, -1), norm_bias.reshape(1, -1))]
    concatenate x0 -> x1, other arithmetic: none -> 0.91 us  [per_device(): jnp.concatenate([norm_gain.reshape(-1, HD), norm_bias.reshape(-1, HD)])]
    ppermute x4, starting transfers between devices: 15.8 us -> 14.9 us  [forward(): return lax.ppermute(shard, axis, [(i, i + by) for i in range(devices - by)])]
    another operation x2 -> x3, other arithmetic: 0.07 us -> 0.97 us  [per_device(): layers = [[jnp.stack(pieces) for pieces in received]]]
  transfers between devices with their start and end apart: 20 -> 20, of which waited for: 8 -> 5; matrix products, arithmetic and copies ran while one was open for 2% -> 5% of each run, Pallas kernels for 15% -> 12%
where the time goes in v2:
time: 57.6 us; the launch traced here: 57.3 us
  starting transfers between devices  34.4 us (60%)
  Pallas kernels  12.2 us (21%)
  waiting for transfers between devices  5.38 us (9%)
  local copies, waits for them, and re-layouts  1.9 us (3%)
  other arithmetic  1.88 us (3%)
  between operations  1.47 us (3%)
    ppermute x16, starting transfers between devices, paired(): return lax.ppermute(shard, axis, [(i, i ^ bit) for i in range(devices)])  19.6 us
    ppermute x4, starting transfers between devices, forward(): return lax.ppermute(shard, axis, [(i, i + by) for i in range(devices - by)])  14.9 us
    pallas_call x3, Pallas kernels, attend(): pl.pallas_call(functools.partial(attend_kernel, heads, reach, packs, tile...  5.43 us
    ppermute x16, waiting for transfers between devices, paired(): return lax.ppermute(shard, axis, [(i, i ^ bit) for i in range(devices)])  5.37 us
    pallas_call x1, Pallas kernels, per_device(): pl.pallas_call(functools.partial(project_kernel, tp, heads), out_shape=[j...  3.56 us
    pallas_call x1, Pallas kernels, per_device(): pl.pallas_call(functools.partial(finish_kernel, heads), out_shape=[jax.Sh...  1.94 us
  transfers between devices with their start and end apart: 20, of which 5 were waited for; matrix products, arithmetic and copies ran while one was open for 5% of the time, Pallas kernels for 12%

profile of v2, /device:TPU:0, one launch (start us, length us, event | category | flops | bytes accessed | tf_op | source)
XLA Modules:
  0.0 57.3 jit_solution(7382909940805979203)
XLA Ops:
  0.6 0.5 collective-permute-start
  1.8 0.8 %reshape.18 = s32[4]{0:T(128)S(1)} reshape(s32[2,2]{1,0:T(2,128)} %table_hbm.1) | data formatting | bytes 32 | tf_op jit(solution)/shard_map/broadcast_in_dim | solution.py:289
  2.6 0.9 %fusion = bf16[6,128]{1,0:T(8,128)(2,1)S(1)} fusion(s32[2,128]{1,0:T(2,128)} %bitcast.24, s32[6]{0:T(128)S(1)} %pad.15.clone), kind=kLoop, calls=%fused_computation.4 | loop fusion | flops 2304 | bytes 2584 | tf_op jit(solution)/shard_map/convert
  3.5 0.9 %pad_maximum_fusion.2.refs_3_ = bf16[32,128]{1,0:T(8,128)(2,1)S(1)} fusion(bf16[16,128]{1,0:T(8,128)(2,1)} %bitcast.22, bf16[16,128]{1,0:T(8,128)(2,1)} %bitcast.23), kind=kLoop, calls=%fused_computation.2 | loop fusion | flops 16384 | bytes 16384 | tf_op jit(solution)/shard_map/concatenate | solution.py:288
  4.5 1.0 %copy-done.1 = bf16[256,1024]{1,0:T(8,128)(2,1)S(1)} copy-done((bf16[256,1024]{1,0:T(8,128)(2,1)S(1)}, bf16[256,1024]{1,0:T(8,128)(2,1)}, u32[]{:S(2)}) %copy-start.1) | copy-done | bytes 524312
  5.5 3.6 %project.1 = (bf16[256,2048]{1,0:T(8,128)(2,1)S(1)}, bf16[272,128]{1,0:T(8,128)(2,1)S(1)}, bf16[256,128]{1,0:T(8,128)(2,1)S(1)}, bf16[272,128]{1,0:T(8,128)(2,1)...) custom-call(s32[1]{0:T(128)S(6)} %copy.9.refs_0_.lengths_ref, ...), custom_call_target="tpu_custom_call" | custom-call | flops 1073741824 | bytes 4194304 | tf_op jit(solution)/shard_map/project/pallas_call | solution.py:294
  9.1 3.5 %collective-permute-start.3 = (bf16[272,128]{1,0:T(8,128)(2,1)S(1)}, bf16[272,128]{1,0:T(8,128)(2,1)S(1)}, u32[]{:S(2)}, u32[]{:S(2)}) collective-permute-start(bf16[272,128]{1,0:T(8,128)(2,1)S(1)} %get-tuple-element.46.refs_14_), channel_id=1, source_target_pairs={{0,6},{2,4},{4,2},{6,0},{8,14},{10,12},{12,10},{14,8},{16,22},{18,... | collective-permute-start | bytes 208904 | tf_op jit(solution)/shard_map/ppermute | solution.py:22
  12.6 0.5 collective-permute-start.2
  13.2 2.8 %collective-permute-start.11 = (bf16[256,128]{1,0:T(8,128)(2,1)S(1)}, bf16[256,128]{1,0:T(8,128)(2,1)S(1)}, u32[]{:S(2)}, u32[]{:S(2)}) collective-permute-start(bf16[256,128]{1,0:T(8,128)(2,1)S(1)} %get-tuple-element.60.refs_15_), channel_id=1, source_target_pairs={{0,6},{2,4},{4,2},{6,0},{8,14},{10,12},{12,10},{14,8},{16,22},{18,... | collective-permute-start | bytes 196616 | tf_op jit(solution)/shard_map/ppermute | solution.py:22
  16.1 0.5 collective-permute-start.10
  16.6 0.9 %queries.1 = (bf16[256,128]{1,0:T(8,128)(2,1)S(1)}, bf16[256,128]{1,0:T(8,128)(2,1)S(1)}, bf16[256,128]{1,0:T(8,128)(2,1)S(1)}, bf16[256,128]{1,0:T(8,128)(2,1)S(1)}) custom-call(bf16[256,2048]{1,0:T(8,128)(2,1)S(1)} %get-tuple-element.47.normed_ref, bf16[3,2048,512]{2,1,0:T(8,128)(2,1)S(1)} %bitcast.13), custom_call_target="tpu_custom_call" | custom-call | flops 536870912 | bytes 2097152 | tf_op jit(solution)/shard_map/queries/pallas_call | solution.py:315
  18.0 3.7 %collective-permute-start.7 = (bf16[4,272,128]{2,1,0:T(8,128)(2,1)S(1)}, bf16[4,272,128]{2,1,0:T(8,128)(2,1)S(1)}, u32[]{:S(2)}, u32[]{:S(2)}) collective-permute-start(bf16[4,272,128]{2,1,0:T(8,128)(2,1)S(1)} %pad_maximum_fusion.refs_4_.refs_0_), channel_id=1, source_target_pairs={{0,8},{2,10},{4,12},{6,14},{8,16},{10,18},{12,20},{14,22},{16,24},... | collective-permute-start | bytes 835592 | tf_op jit(solution)/shard_map/ppermute | solution.py:27
  21.9 3.5 %collective-permute-start.12 = (bf16[4,256,128]{2,1,0:T(8,128)(2,1)S(1)}, bf16[4,256,128]{2,1,0:T(8,128)(2,1)S(1)}, u32[]{:S(2)}, u32[]{:S(2)}) collective-permute-start(bf16[4,256,128]{2,1,0:T(8,128)(2,1)S(1)} %pad_maximum_fusion.1.refs_5_.refs_7_), channel_id=1, source_target_pairs={{0,8},{2,10},{4,12},{6,14},{8,16},{10,18},{12,20},{14,22},{16,24},... | collective-permute-start | bytes 786440 | tf_op jit(solution)/shard_map/ppermute | solution.py:27
  25.4 1.4 %collective-permute-start.4 = (bf16[256,128]{1,0:T(8,128)(2,1)S(1)}, bf16[256,128]{1,0:T(8,128)(2,1)S(1)}, u32[]{:S(2)}, u32[]{:S(2)}) collective-permute-start(bf16[256,128]{1,0:T(8,128)(2,1)S(1)} %get-tuple-element.53), channel_id=1, source_target_pairs={{0,2},{2,0},{4,6},{6,4},{8,10},{10,8},{12,14},{14,12},{16,18},{18,... | collective-permute-start | bytes 196616 | tf_op jit(solution)/shard_map/ppermute | solution.py:22
  26.8 1.5 %collective-permute-start.5 = (bf16[256,128]{1,0:T(8,128)(2,1)S(1)}, bf16[256,128]{1,0:T(8,128)(2,1)S(1)}, u32[]{:S(2)}, u32[]{:S(2)}) collective-permute-start(bf16[256,128]{1,0:T(8,128)(2,1)S(1)} %get-tuple-element.54), channel_id=1, source_target_pairs={{0,4},{2,6},{4,0},{6,2},{8,12},{10,14},{12,8},{14,10},{16,20},{18,... | collective-permute-start | bytes 196616 | tf_op jit(solution)/shard_map/ppermute | solution.py:22
  28.3 0.6 %collective-permute-start.6 = (bf16[256,128]{1,0:T(8,128)(2,1)S(1)}, bf16[256,128]{1,0:T(8,128)(2,1)S(1)}, u32[]{:S(2)}, u32[]{:S(2)}) collective-permute-start(bf16[256,128]{1,0:T(8,128)(2,1)S(1)} %get-tuple-element.55), channel_id=1, source_target_pairs={{0,6},{2,4},{4,2},{6,0},{8,14},{10,12},{12,10},{14,8},{16,22},{18,... | collective-permute-start | bytes 196616 | tf_op jit(solution)/shard_map/ppermute | solution.py:22
  29.0 4.2 %collective-permute-start.8 = (bf16[4,272,128]{2,1,0:T(8,128)(2,1)S(1)}, bf16[4,272,128]{2,1,0:T(8,128)(2,1)S(1)}, u32[]{:S(2)}, u32[]{:S(2)}) collective-permute-start(bf16[4,272,128]{2,1,0:T(8,128)(2,1)S(1)} %collective-permute-done.7.refs_5_.refs_1_), channel_id=1, source_target_pairs={{0,8},{2,10},{4,12},{6,14},{8,16},{10,18},{12,20},{14,22},{16,24},... | collective-permute-start | bytes 835592 | tf_op jit(solution)/shard_map/ppermute | solution.py:27
  33.2 0.3 collective-permute-done.6.refs_3_
  33.5 2.0 %attend.3 = (f32[4,256,128]{2,1,0:T(8,128)S(1)}, f32[4,256,128]{2,1,0:T(8,128)S(1)}, f32[4,256,256]{2,1,0:T(8,128)S(1)}) custom-call(bf16[256,128]{1,0:T(8,128)(2,1)S(1)} %get-tuple-element.52.refs_0_, bf16[256,128]{1,0:T(8,128)(2,1)S(1)} %collective-permute-done.4.refs_1_, bf16[256,128]{1,0:T(8,128)(2,1)S(1)} %collective-permute-done.5.refs_2_, ...), custom_call_target="tpu_custom_call" | custom-call | flops 805306368 | bytes 4194304 | tf_op jit(solution)/shard_map/attend/pallas_call | solution.py:359
  35.6 3.5 %collective-permute-start.13 = (bf16[4,256,128]{2,1,0:T(8,128)(2,1)S(1)}, bf16[4,256,128]{2,1,0:T(8,128)(2,1)S(1)}, u32[]{:S(2)}, u32[]{:S(2)}) collective-permute-start(bf16[4,256,128]{2,1,0:T(8,128)(2,1)S(1)} %collective-permute-done.12.refs_6_.refs_8_), channel_id=1, source_target_pairs={{0,8},{2,10},{4,12},{6,14},{8,16},{10,18},{12,20},{14,22},{16,24},... | collective-permute-start | bytes 786440 | tf_op jit(solution)/shard_map/ppermute | solution.py:27
  39.0 1.6 %attend.4 = (f32[4,256,128]{2,1,0:T(8,128)S(1)}, f32[4,256,256]{2,1,0:T(8,128)S(1)}) custom-call(bf16[256,128]{1,0:T(8,128)(2,1)S(1)} %get-tuple-element.52.refs_0_, bf16[256,128]{1,0:T(8,128)(2,1)S(1)} %collective-permute-done.4.refs_1_, bf16[256,128]{1,0:T(8,128)(2,1)S(1)} %collective-permute-done.5.refs_2_, ...), custom_call_target="tpu_custom_call" | custom-call | flops 805306368 | bytes 4194304 | tf_op jit(solution)/shard_map/attend/pallas_call | solution.py:359
  40.7 0.4 select.2
  41.0 1.3 %collective-permute-start.14 = (bf16[256,128]{1,0:T(8,128)(2,1)S(1)}, bf16[256,128]{1,0:T(8,128)(2,1)S(1)}, u32[]{:S(2)}, u32[]{:S(2)}) collective-permute-start(bf16[256,128]{1,0:T(8,128)(2,1)S(1)} %get-tuple-element.74), channel_id=1, source_target_pairs={{0,2},{2,0},{4,6},{6,4},{8,10},{10,8},{12,14},{14,12},{16,18},{18,... | collective-permute-start | bytes 196616 | tf_op jit(solution)/shard_map/ppermute | solution.py:22
  42.3 1.5 %collective-permute-start.15 = (bf16[256,128]{1,0:T(8,128)(2,1)S(1)}, bf16[256,128]{1,0:T(8,128)(2,1)S(1)}, u32[]{:S(2)}, u32[]{:S(2)}) collective-permute-start(bf16[256,128]{1,0:T(8,128)(2,1)S(1)} %get-tuple-element.75), channel_id=1, source_target_pairs={{0,4},{2,6},{4,0},{6,2},{8,12},{10,14},{12,8},{14,10},{16,20},{18,... | collective-permute-start | bytes 196616 | tf_op jit(solution)/shard_map/ppermute | solution.py:22
  43.8 1.8 %attend.5 = (bf16[512,128]{1,0:T(8,128)(2,1)S(1)}, bf16[512,128]{1,0:T(8,128)(2,1)S(1)}, bf16[512,128]{1,0:T(8,128)(2,1)S(1)}, bf16[512,128]{1,0:T(8,128)(2,1)S(1)}) custom-call(bf16[256,128]{1,0:T(8,128)(2,1)S(1)} %get-tuple-element.52.refs_0_, bf16[256,128]{1,0:T(8,128)(2,1)S(1)} %collective-permute-done.4.refs_1_, ...), custom_call_target="tpu_custom_call" | custom-call | flops 805306368 | bytes 4194304 | tf_op jit(solution)/shard_map/attend/pallas_call | solution.py:359
  45.7 0.9 %collective-permute-done.15.refs_6_ = bf16[256,128]{1,0:T(8,128)(2,1)S(1)} collective-permute-done((bf16[256,128]{1,0:T(8,128)(2,1)S(1)}, bf16[256,128]{1,0:T(8,128)(2,1)S(1)}, u32[]{:S(2)}, u32[]{:S(2)}) %collective-permute-start.15) | collective-permute-done | bytes 65568 | tf_op jit(solution)/shard_map/ppermute | solution.py:22
  46.6 1.0 %collective-permute-start.16 = (bf16[512,128]{1,0:T(8,128)(2,1)S(1)}, bf16[512,128]{1,0:T(8,128)(2,1)S(1)}, u32[]{:S(2)}, u32[]{:S(2)}) collective-permute-start(bf16[512,128]{1,0:T(8,128)(2,1)S(1)} %get-tuple-element.77), channel_id=1, source_target_pairs={{0,2},{2,0},{4,6},{6,4},{8,10},{10,8},{12,14},{14,12},{16,18},{18,... | collective-permute-start | bytes 393224 | tf_op jit(solution)/shard_map/ppermute | solution.py:22
  47.6 1.1 %collective-permute-start.17 = (bf16[512,128]{1,0:T(8,128)(2,1)S(1)}, bf16[512,128]{1,0:T(8,128)(2,1)S(1)}, u32[]{:S(2)}, u32[]{:S(2)}) collective-permute-start(bf16[512,128]{1,0:T(8,128)(2,1)S(1)} %get-tuple-element.78), channel_id=1, source_target_pairs={{0,4},{2,6},{4,0},{6,2},{8,12},{10,14},{12,8},{14,10},{16,20},{18,... | collective-permute-start | bytes 393224 | tf_op jit(solution)/shard_map/ppermute | solution.py:22
  48.7 1.4 %collective-permute-start.18 = (bf16[512,128]{1,0:T(8,128)(2,1)S(1)}, bf16[512,128]{1,0:T(8,128)(2,1)S(1)}, u32[]{:S(2)}, u32[]{:S(2)}) collective-permute-start(bf16[512,128]{1,0:T(8,128)(2,1)S(1)} %get-tuple-element.79), channel_id=1, source_target_pairs={{0,6},{2,4},{4,2},{6,0},{8,14},{10,12},{12,10},{14,8},{16,22},{18,... | collective-permute-start | bytes 393224 | tf_op jit(solution)/shard_map/ppermute | solution.py:22
  50.1 1.5 %collective-permute-start.19 = (bf16[256,128]{1,0:T(8,128)(2,1)S(1)}, bf16[256,128]{1,0:T(8,128)(2,1)S(1)}, u32[]{:S(2)}, u32[]{:S(2)}) collective-permute-start(bf16[256,128]{1,0:T(8,128)(2,1)S(1)} %get-tuple-element.83), channel_id=1, source_target_pairs={{0,6},{2,4},{4,2},{6,0},{8,14},{10,12},{12,10},{14,8},{16,22},{18,... | collective-permute-start | bytes 196616 | tf_op jit(solution)/shard_map/ppermute | solution.py:22
  51.6 3.7 %collective-permute-done.19.refs_7_ = bf16[256,128]{1,0:T(8,128)(2,1)S(1)} collective-permute-done((bf16[256,128]{1,0:T(8,128)(2,1)S(1)}, bf16[256,128]{1,0:T(8,128)(2,1)S(1)}, u32[]{:S(2)}, u32[]{:S(2)}) %collective-permute-start.19) | collective-permute-done | bytes 65568 | tf_op jit(solution)/shard_map/ppermute | solution.py:22
  55.3 1.9 %finish.1 = (bf16[256,512]{1,0:T(8,128)(2,1)}, bf16[4,2,128,512]{3,2,1,0:T(8,128)(2,1)}) custom-call(s32[2,2]{1,0:T(2,128)S(1)} %copy-done.2, s32[1]{0:T(128)S(6)} %copy.9.refs_0_.lengths_ref, bf16[512,128]{1,0:T(8,128)(2,1)S(1)} %get-tuple-element.76.refs_0_, bf16[512,128]{1,0:T(8,128)(2,1)S(1)} %collective-permute-done.16.refs_1_, ...), custom_call_target="tpu_custom_call" | custom-call | tf_op jit(solution)/shard_map/finish/pallas_call | solution.py:394
  (28 shorter events, 0.9 us)
Async XLA Ops:
  0.6 3.8 %collective-permute-start = (bf16[256,1024]{1,0:T(8,128)(2,1)}, bf16[256,1024]{1,0:T(8,128)(2,1)S(1)}, u32[]{:S(2)}, u32[]{:S(2)}) collective-permute-start(bf16[256,1024]{1,0:T(8,128)(2,1)} %refs_1_.1), channel_id=1, source_target_pairs={{0,1},{1,0},{2,3},{3,2},{4,5},{5,4},{6,7},{7,6},{8,9},{9,8},{10,11... | collective-permute-start | bytes 1572872 | tf_op jit(solution)/shard_map/ppermute | solution.py:22
  2.6 14.0 %copy-start = (bf16[2048,3,512]{2,0,1:T(8,128)(2,1)S(1)}, bf16[2048,3,512]{2,0,1:T(8,128)(2,1)}, u32[]{:S(2)}) copy-start(bf16[2048,3,512]{2,0,1:T(8,128)(2,1)} %param.10) | copy-start | bytes 18874372
  4.5 1.0 %copy-start.1 = (bf16[256,1024]{1,0:T(8,128)(2,1)S(1)}, bf16[256,1024]{1,0:T(8,128)(2,1)}, u32[]{:S(2)}) copy-start(bf16[256,1024]{1,0:T(8,128)(2,1)} %refs_1_.1) | copy-start | bytes 1572868
  9.1 8.5 %collective-permute-start.3 = (bf16[272,128]{1,0:T(8,128)(2,1)S(1)}, bf16[272,128]{1,0:T(8,128)(2,1)S(1)}, u32[]{:S(2)}, u32[]{:S(2)}) collective-permute-start(bf16[272,128]{1,0:T(8,128)(2,1)S(1)} %get-tuple-element.46.refs_14_), channel_id=1, source_target_pairs={{0,6},{2,4},{4,2},{6,0},{8,14},{10,12},{12,10},{14,8},{16,22},{18,... | collective-permute-start | bytes 208904 | tf_op jit(solution)/shard_map/ppermute | solution.py:22
  12.6 5.1 %collective-permute-start.2 = (bf16[272,128]{1,0:T(8,128)(2,1)S(1)}, bf16[272,128]{1,0:T(8,128)(2,1)S(1)}, u32[]{:S(2)}, u32[]{:S(2)}) collective-permute-start(bf16[272,128]{1,0:T(8,128)(2,1)S(1)} %get-tuple-element.45.refs_12_), channel_id=1, source_target_pairs={{0,4},{2,6},{4,0},{6,2},{8,12},{10,14},{12,8},{14,10},{16,20},{18,... | collective-permute-start | bytes 208904 | tf_op jit(solution)/shard_map/ppermute | solution.py:22
  13.1 4.9 %collective-permute-start.1 = (bf16[272,128]{1,0:T(8,128)(2,1)S(1)}, bf16[272,128]{1,0:T(8,128)(2,1)S(1)}, u32[]{:S(2)}, u32[]{:S(2)}) collective-permute-start(bf16[272,128]{1,0:T(8,128)(2,1)S(1)} %get-tuple-element.44.refs_10_), channel_id=1, source_target_pairs={{0,2},{2,0},{4,6},{6,4},{8,10},{10,8},{12,14},{14,12},{16,18},{18,... | collective-permute-start | bytes 208904 | tf_op jit(solution)/shard_map/ppermute | solution.py:22
  13.2 8.5 %collective-permute-start.11 = (bf16[256,128]{1,0:T(8,128)(2,1)S(1)}, bf16[256,128]{1,0:T(8,128)(2,1)S(1)}, u32[]{:S(2)}, u32[]{:S(2)}) collective-permute-start(bf16[256,128]{1,0:T(8,128)(2,1)S(1)} %get-tuple-element.60.refs_15_), channel_id=1, source_target_pairs={{0,6},{2,4},{4,2},{6,0},{8,14},{10,12},{12,10},{14,8},{16,22},{18,... | collective-permute-start | bytes 196616 | tf_op jit(solution)/shard_map/ppermute | solution.py:22
  16.1 5.6 %collective-permute-start.10 = (bf16[256,128]{1,0:T(8,128)(2,1)S(1)}, bf16[256,128]{1,0:T(8,128)(2,1)S(1)}, u32[]{:S(2)}, u32[]{:S(2)}) collective-permute-start(bf16[256,128]{1,0:T(8,128)(2,1)S(1)} %get-tuple-element.59.refs_13_), channel_id=1, source_target_pairs={{0,4},{2,6},{4,0},{6,2},{8,12},{10,14},{12,8},{14,10},{16,20},{18,... | collective-permute-start | bytes 196616 | tf_op jit(solution)/shard_map/ppermute | solution.py:22
  17.5 37.8 %copy-start.2 = (s32[2,2]{1,0:T(2,128)S(1)}, s32[2,2]{1,0:T(2,128)}, u32[]{:S(2)}) copy-start(s32[2,2]{1,0:T(2,128)} %table_hbm.1) | copy-start | bytes 52
  17.5 4.3 %collective-permute-start.9 = (bf16[256,128]{1,0:T(8,128)(2,1)S(1)}, bf16[256,128]{1,0:T(8,128)(2,1)S(1)}, u32[]{:S(2)}, u32[]{:S(2)}) collective-permute-start(bf16[256,128]{1,0:T(8,128)(2,1)S(1)} %get-tuple-element.58.refs_11_), channel_id=1, source_target_pairs={{0,2},{2,0},{4,6},{6,4},{8,10},{10,8},{12,14},{14,12},{16,18},{18,... | collective-permute-start | bytes 196616 | tf_op jit(solution)/shard_map/ppermute | solution.py:22
  18.0 11.0 %collective-permute-start.7 = (bf16[4,272,128]{2,1,0:T(8,128)(2,1)S(1)}, bf16[4,272,128]{2,1,0:T(8,128)(2,1)S(1)}, u32[]{:S(2)}, u32[]{:S(2)}) collective-permute-start(bf16[4,272,128]{2,1,0:T(8,128)(2,1)S(1)} %pad_maximum_fusion.refs_4_.refs_0_), channel_id=1, source_target_pairs={{0,8},{2,10},{4,12},{6,14},{8,16},{10,18},{12,20},{14,22},{16,24},... | collective-permute-start | bytes 835592 | tf_op jit(solution)/shard_map/ppermute | solution.py:27
  21.9 13.6 %collective-permute-start.12 = (bf16[4,256,128]{2,1,0:T(8,128)(2,1)S(1)}, bf16[4,256,128]{2,1,0:T(8,128)(2,1)S(1)}, u32[]{:S(2)}, u32[]{:S(2)}) collective-permute-start(bf16[4,256,128]{2,1,0:T(8,128)(2,1)S(1)} %pad_maximum_fusion.1.refs_5_.refs_7_), channel_id=1, source_target_pairs={{0,8},{2,10},{4,12},{6,14},{8,16},{10,18},{12,20},{14,22},{16,24},... | collective-permute-start | bytes 786440 | tf_op jit(solution)/shard_map/ppermute | solution.py:27
  25.4 7.8 %collective-permute-start.4 = (bf16[256,128]{1,0:T(8,128)(2,1)S(1)}, bf16[256,128]{1,0:T(8,128)(2,1)S(1)}, u32[]{:S(2)}, u32[]{:S(2)}) collective-permute-start(bf16[256,128]{1,0:T(8,128)(2,1)S(1)} %get-tuple-element.53), channel_id=1, source_target_pairs={{0,2},{2,0},{4,6},{6,4},{8,10},{10,8},{12,14},{14,12},{16,18},{18,... | collective-permute-start | bytes 196616 | tf_op jit(solution)/shard_map/ppermute | solution.py:22
  26.8 6.4 %collective-permute-start.5 = (bf16[256,128]{1,0:T(8,128)(2,1)S(1)}, bf16[256,128]{1,0:T(8,128)(2,1)S(1)}, u32[]{:S(2)}, u32[]{:S(2)}) collective-permute-start(bf16[256,128]{1,0:T(8,128)(2,1)S(1)} %get-tuple-element.54), channel_id=1, source_target_pairs={{0,4},{2,6},{4,0},{6,2},{8,12},{10,14},{12,8},{14,10},{16,20},{18,... | collective-permute-start | bytes 196616 | tf_op jit(solution)/shard_map/ppermute | solution.py:22
  28.3 5.2 %collective-permute-start.6 = (bf16[256,128]{1,0:T(8,128)(2,1)S(1)}, bf16[256,128]{1,0:T(8,128)(2,1)S(1)}, u32[]{:S(2)}, u32[]{:S(2)}) collective-permute-start(bf16[256,128]{1,0:T(8,128)(2,1)S(1)} %get-tuple-element.55), channel_id=1, source_target_pairs={{0,6},{2,4},{4,2},{6,0},{8,14},{10,12},{12,10},{14,8},{16,22},{18,... | collective-permute-start | bytes 196616 | tf_op jit(solution)/shard_map/ppermute | solution.py:22
  29.0 11.7 %collective-permute-start.8 = (bf16[4,272,128]{2,1,0:T(8,128)(2,1)S(1)}, bf16[4,272,128]{2,1,0:T(8,128)(2,1)S(1)}, u32[]{:S(2)}, u32[]{:S(2)}) collective-permute-start(bf16[4,272,128]{2,1,0:T(8,128)(2,1)S(1)} %collective-permute-done.7.refs_5_.refs_1_), channel_id=1, source_target_pairs={{0,8},{2,10},{4,12},{6,14},{8,16},{10,18},{12,20},{14,22},{16,24},... | collective-permute-start | bytes 835592 | tf_op jit(solution)/shard_map/ppermute | solution.py:27
  35.6 8.3 %collective-permute-start.13 = (bf16[4,256,128]{2,1,0:T(8,128)(2,1)S(1)}, bf16[4,256,128]{2,1,0:T(8,128)(2,1)S(1)}, u32[]{:S(2)}, u32[]{:S(2)}) collective-permute-start(bf16[4,256,128]{2,1,0:T(8,128)(2,1)S(1)} %collective-permute-done.12.refs_6_.refs_8_), channel_id=1, source_target_pairs={{0,8},{2,10},{4,12},{6,14},{8,16},{10,18},{12,20},{14,22},{16,24},... | collective-permute-start | bytes 786440 | tf_op jit(solution)/shard_map/ppermute | solution.py:27
  41.0 4.6 %collective-permute-start.14 = (bf16[256,128]{1,0:T(8,128)(2,1)S(1)}, bf16[256,128]{1,0:T(8,128)(2,1)S(1)}, u32[]{:S(2)}, u32[]{:S(2)}) collective-permute-start(bf16[256,128]{1,0:T(8,128)(2,1)S(1)} %get-tuple-element.74), channel_id=1, source_target_pairs={{0,2},{2,0},{4,6},{6,4},{8,10},{10,8},{12,14},{14,12},{16,18},{18,... | collective-permute-start | bytes 196616 | tf_op jit(solution)/shard_map/ppermute | solution.py:22
  42.3 4.3 %collective-permute-start.15 = (bf16[256,128]{1,0:T(8,128)(2,1)S(1)}, bf16[256,128]{1,0:T(8,128)(2,1)S(1)}, u32[]{:S(2)}, u32[]{:S(2)}) collective-permute-start(bf16[256,128]{1,0:T(8,128)(2,1)S(1)} %get-tuple-element.75), channel_id=1, source_target_pairs={{0,4},{2,6},{4,0},{6,2},{8,12},{10,14},{12,8},{14,10},{16,20},{18,... | collective-permute-start | bytes 196616 | tf_op jit(solution)/shard_map/ppermute | solution.py:22
  46.6 8.7 %collective-permute-start.16 = (bf16[512,128]{1,0:T(8,128)(2,1)S(1)}, bf16[512,128]{1,0:T(8,128)(2,1)S(1)}, u32[]{:S(2)}, u32[]{:S(2)}) collective-permute-start(bf16[512,128]{1,0:T(8,128)(2,1)S(1)} %get-tuple-element.77), channel_id=1, source_target_pairs={{0,2},{2,0},{4,6},{6,4},{8,10},{10,8},{12,14},{14,12},{16,18},{18,... | collective-permute-start | bytes 393224 | tf_op jit(solution)/shard_map/ppermute | solution.py:22
  47.6 7.7 %collective-permute-start.17 = (bf16[512,128]{1,0:T(8,128)(2,1)S(1)}, bf16[512,128]{1,0:T(8,128)(2,1)S(1)}, u32[]{:S(2)}, u32[]{:S(2)}) collective-permute-start(bf16[512,128]{1,0:T(8,128)(2,1)S(1)} %get-tuple-element.78), channel_id=1, source_target_pairs={{0,4},{2,6},{4,0},{6,2},{8,12},{10,14},{12,8},{14,10},{16,20},{18,... | collective-permute-start | bytes 393224 | tf_op jit(solution)/shard_map/ppermute | solution.py:22
  48.7 6.6 %collective-permute-start.18 = (bf16[512,128]{1,0:T(8,128)(2,1)S(1)}, bf16[512,128]{1,0:T(8,128)(2,1)S(1)}, u32[]{:S(2)}, u32[]{:S(2)}) collective-permute-start(bf16[512,128]{1,0:T(8,128)(2,1)S(1)} %get-tuple-element.79), channel_id=1, source_target_pairs={{0,6},{2,4},{4,2},{6,0},{8,14},{10,12},{12,10},{14,8},{16,22},{18,... | collective-permute-start | bytes 393224 | tf_op jit(solution)/shard_map/ppermute | solution.py:22
  50.1 5.2 %collective-permute-start.19 = (bf16[256,128]{1,0:T(8,128)(2,1)S(1)}, bf16[256,128]{1,0:T(8,128)(2,1)S(1)}, u32[]{:S(2)}, u32[]{:S(2)}) collective-permute-start(bf16[256,128]{1,0:T(8,128)(2,1)S(1)} %get-tuple-element.83), channel_id=1, source_target_pairs={{0,6},{2,4},{4,2},{6,0},{8,14},{10,12},{12,10},{14,8},{16,22},{18,... | collective-permute-start | bytes 196616 | tf_op jit(solution)/shard_map/ppermute | solution.py:22

commit v3 on v2

--- a/solution.py
+++ b/solution.py
@@ -10,6 +10,7 @@
 PAGE = 128
 REACH = 8
 NOTES = 16
+LIMIT_ROW = 6
 MASKED = -1e30
 PROJECT_VMEM = 48 << 20
 VMEM = pl.BlockSpec(memory_space=pltpu.VMEM)
@@ -31,37 +32,38 @@
     return pl.CostEstimate(flops=flops, bytes_accessed=moved, transcendentals=transcendentals)
 
 
-def valid_rows(lengths_ref, row_count):
-    device = lax.axis_index("req")
-    per_pack = lax.axis_size("req") // lengths_ref.shape[0]
-    limit = lengths_ref[device // per_pack] - device % per_pack * row_count
-    return lax.broadcasted_iota(jnp.int32, (row_count, 1), 0) < limit
+def keep_kernel(tokens_ref, kept_ref):
+    kept_ref[...] = tokens_ref[...]
+
+
+def below_limit(notes, row_count):
+    rows = lax.broadcasted_iota(jnp.int32, (row_count, HD), 0)
+    return rows.astype(jnp.float32) < notes[LIMIT_ROW : LIMIT_ROW + 1]
 
 
 def project_kernel(tp, heads, *refs):
     refs = list(refs)
     take = lambda count: [refs.pop(0) for _ in range(count)]
-    lengths_ref, tokens_hbm, w_hbm, affine_ref, notes_ref = take(5)
+    lengths_ref, tokens_ref, w_hbm, table_ref = take(4)
     received, (normed_ref,), pieces = take(tp - 1), take(1), take(2 * heads)
-    tokens_ref, w_ref, spread_ref, columns, sems = refs
+    w_ref, spread_ref, columns, sems = refs
     rows, features = tokens_ref.shape
     here = lax.axis_index("tp")
     me = lax.axis_index("req") % heads
     loads = [
-        pltpu.make_async_copy(tokens_hbm, tokens_ref, sems.at[0]),
-        pltpu.make_async_copy(w_hbm.at[1], w_ref.at[0], sems.at[1]),
-        pltpu.make_async_copy(w_hbm.at[2], w_ref.at[1], sems.at[2]),
+        pltpu.make_async_copy(w_hbm.at[1 + which], w_ref.at[which], sems.at[which])
+        for which in range(2)
     ]
     for load in loads:
         load.start()
-    lines = affine_ref.shape[0] // 2
-    affine = affine_ref[...].astype(jnp.float32)
+    notes = table_ref[:NOTES, :] + 1.0
+    affine = table_ref[NOTES:, :]
+    lines = affine.shape[0] // 2
     for row in range(2):
         for line in range(lines):
             spread_ref[row : row + 1, line * HD : (line + 1) * HD] = affine[
                 row * lines + line : row * lines + line + 1
             ]
-    loads[0].wait()
     parts = [tokens_ref] + received
     step = 32
 
@@ -82,11 +84,21 @@
 
     lax.fori_loop(0, rows // step, norm_rows, 0)
 
-    valid = valid_rows(lengths_ref, rows)
+    device = lax.axis_index("req")
+    per_pack = lax.axis_size("req") // lengths_ref.shape[0]
+    limit = lengths_ref[device // per_pack] - device % per_pack * rows
+    limit = jnp.clip(limit, 0, rows).astype(jnp.float32)
+    row = lax.broadcasted_iota(jnp.int32, notes.shape, 0)
+    entries = [notes[2 + page : 3 + page, at : at + 1] for page in range(2) for at in range(2)]
+    for at, entry in enumerate(entries):
+        notes = jnp.where(row == 2 + at, entry, notes)
+    notes = jnp.where(row == LIMIT_ROW, limit, notes)
+    valid = below_limit(notes, rows)
+    notes = notes.astype(jnp.bfloat16)
     for which in range(2):
-        loads[1 + which].wait()
+        loads[which].wait()
         projected = jnp.dot(normed_ref[...], w_ref[which], preferred_element_type=jnp.float32)
-        columns[...] = jnp.where(valid, projected, 0.0).astype(jnp.bfloat16)
+        columns[...] = jnp.where(valid[:, :1], projected, 0.0).astype(jnp.bfloat16)
         for bit in range(heads):
             lanes = pl.ds(pl.multiple_of((me ^ bit) * HD, HD), HD)
             for page in range(2):
@@ -95,7 +107,7 @@
                 ]
 
     for bit in range(heads):
-        pieces[2 * bit][2 * PAGE :, :] = notes_ref[...]
+        pieces[2 * bit][2 * PAGE :, :] = notes
 
 
 def query_kernel(heads, normed_ref, w_hbm, *refs):
@@ -247,30 +259,35 @@
     return sorted(set(place for place in wanted if place[1] == 1))
 
 
-def finish_kernel(heads, table_hbm, lengths_ref, *refs):
+def finish_kernel(heads, *refs):
     refs = list(refs)
     take = lambda count: [refs.pop(0) for _ in range(count)]
     final, early, own = take(heads), take(heads), take(2 * heads)
-    context_ref, cache_ref, table_ref, sem = refs
-    load = pltpu.make_async_copy(table_hbm, table_ref, sem)
-    load.start()
-    load.wait()
+    context_ref, cache_ref = refs
     device = lax.axis_index("req")
     me = device % heads
     rows = context_ref.shape[0]
-    valid = valid_rows(lengths_ref, rows)
+    notes = own[0][2 * PAGE :, :].astype(jnp.float32)
+    valid = below_limit(notes, rows)
+    here = (device + 1).astype(jnp.float32)
+    stays = [
+        (notes[2 + 2 * page : 3 + 2 * page] == here)
+        & (notes[3 + 2 * page : 4 + 2 * page] == page + 3.0)
+        for page in range(2)
+    ]
     for bit in range(heads):
         lanes = pl.ds(pl.multiple_of((me ^ bit) * HD, HD), HD)
-        context_ref[:, lanes] = jnp.where(valid, final[bit][0:rows, :], 0).astype(jnp.bfloat16)
+        context = final[bit][0:rows, :].astype(jnp.float32)
+        context_ref[:, lanes] = jnp.where(valid, context, 0.0).astype(jnp.bfloat16)
         for part in range(2):
             first = part * PAGE
             cache_ref[0, part, :, lanes] = early[bit][first : first + PAGE, :]
             cache_ref[1, part, :, lanes] = final[bit][rows + first : rows + first + PAGE, :]
             for page in range(2):
-                stays = (table_ref[page, 0] == device) & (table_ref[page, 1] == page + 2)
-                cache_ref[2 + page, part, :, lanes] = jnp.where(
-                    stays, own[2 * bit + page][first : first + PAGE, :], 0
-                ).astype(jnp.bfloat16)
+                kept = own[2 * bit + page][first : first + PAGE, :].astype(jnp.float32)
+                cache_ref[2 + page, part, :, lanes] = jnp.where(stays[page], kept, 0.0).astype(
+                    jnp.bfloat16
+                )
 
 
 def per_device(tokens, norm_gain, norm_bias, w_qkv, segment_ids, pack_lengths, page_table):
@@ -285,29 +302,49 @@
 
     received = [paired(tokens, "tp", bit) for bit in range(1, tp)]
     weights = jnp.transpose(w_qkv, (1, 0, 2))
-    affine = jnp.concatenate([norm_gain.reshape(-1, HD), norm_bias.reshape(-1, HD)])
-    entries = jnp.broadcast_to(page_table.reshape(-1, 1), (page_table.size, HD))
-    notes = jnp.concatenate([segment_ids.reshape(2, HD), entries]) + 1
-    notes = jnp.pad(notes, ((0, NOTES - notes.shape[0]), (0, 0))).astype(bf16)
+    lines = width // HD
+
+    def placed(entries, row):
+        below = NOTES + 2 * lines - row - entries.shape[0]
+        return jnp.pad(entries, ((row, below), (0, HD - entries.shape[1])))
+
+    ids, gain, bias = lax.optimization_barrier(
+        (
+            segment_ids.reshape(2, HD),
+            norm_gain.reshape(lines, HD),
+            norm_bias.reshape(lines, HD),
+        )
+    )
+    integers = placed(ids, 0) + placed(page_table, 2)
+    affine = placed(gain, NOTES) + placed(bias, NOTES + lines)
+    table = integers.astype(jnp.float32) + affine.astype(jnp.float32)
+    kept = pl.pallas_call(
+        keep_kernel,
+        out_shape=jax.ShapeDtypeStruct((rows, features), bf16),
+        in_specs=[VMEM],
+        out_specs=VMEM,
+        compiler_params=pltpu.CompilerParams(vmem_limit_bytes=4 << 20),
+        cost_estimate=cost(rows * features, 2 * rows * features),
+        name="keep",
+    )(tokens)
 
     piece_shapes = [(2 * PAGE + NOTES, HD), (2 * PAGE, HD)] * heads
     normed, *own = pl.pallas_call(
         functools.partial(project_kernel, tp, heads),
         out_shape=[jax.ShapeDtypeStruct((rows, width), bf16)]
         + [jax.ShapeDtypeStruct(shape, bf16) for shape in piece_shapes],
-        in_specs=[SMEM] + [HBM] * 2 + [VMEM] * (1 + tp),
+        in_specs=[SMEM, VMEM, HBM] + [VMEM] * tp,
         out_specs=[VMEM] * (1 + 2 * heads),
         scratch_shapes=[
-            pltpu.VMEM((rows, features), bf16),
             pltpu.VMEM((2, width, local_width), bf16),
             pltpu.VMEM((2, width), jnp.float32),
             pltpu.VMEM((rows, local_width), bf16),
-            pltpu.SemaphoreType.DMA((3,)),
+            pltpu.SemaphoreType.DMA((2,)),
         ],
         compiler_params=pltpu.CompilerParams(vmem_limit_bytes=PROJECT_VMEM),
         cost_estimate=cost(4 * rows * width * local_width, 4 * width * local_width),
         name="project",
-    )(pack_lengths, tokens, weights, affine, notes, *received)
+    )(pack_lengths, kept, weights, table, *received)
     pages = [
         jnp.stack([own[page]] + [paired(own[2 * bit + page], "req", bit) for bit in range(1, heads)])
         for page in range(2)
@@ -326,7 +363,6 @@
         cost_estimate=cost(2 * rows * width * local_width, 2 * width * local_width),
         name="queries",
     )(normed, weights)
-    pages[0], queries = lax.optimization_barrier((pages[0], queries))
     layers = [pages]
     queries = [queries[0]] + [paired(queries[bit], "req", bit) for bit in range(1, heads)]
 
@@ -386,9 +422,9 @@
         name="select",
     )(*[layer[0] for layer in layers])
     early = [early[0]] + [paired(early[bit], "req", bit) for bit in range(1, heads)]
-    final = attend([(reach, 0), (reach, 1)], [ids, *state], True, 1)
-    final, near = lax.optimization_barrier((final, early[:-1]))
-    early = near + early[-1:]
+    final = list(attend([(reach, 0), (reach, 1)], [ids, *state], True, 1))
+    for bit in range(1, heads):
+        final[bit], early[bit] = lax.optimization_barrier((final[bit], early[bit]))
     final = [final[0]] + [paired(final[bit], "req", bit) for bit in range(1, heads)]
 
     context, cache = pl.pallas_call(
@@ -397,12 +433,11 @@
             jax.ShapeDtypeStruct((rows, local_width), bf16),
             jax.ShapeDtypeStruct((4, 2, PAGE, local_width), bf16),
         ],
-        in_specs=[HBM, SMEM] + [VMEM] * (4 * heads),
+        in_specs=[VMEM] * (4 * heads),
         out_specs=[VMEM] * 2,
-        scratch_shapes=[pltpu.SMEM((2, 2), jnp.int32), pltpu.SemaphoreType.DMA],
         compiler_params=pltpu.CompilerParams(vmem_limit_bytes=16 << 20),
         name="finish",
-    )(page_table, pack_lengths, *final, *early, *own)
+    )(*final, *early, *own)
     return context, cache
 
 

time: 57.6 us -> 54.4 us (0.944)
  starting transfers between devices: 34.4 us -> 33.2 us
  other arithmetic: 1.88 us -> 0.82 us
  local copies, waits for them, and re-layouts: 1.9 us -> 1.28 us
  Pallas kernels: 12.2 us -> 11.6 us
    concatenate x1 -> x0, other arithmetic: 0.91 us -> none  [per_device(): jnp.concatenate([norm_gain.reshape(-1, HD), norm_bias.reshape(-1, HD)])]
    ppermute x4, starting transfers between devices: 14.9 us -> 13.9 us  [forward(): return lax.ppermute(shard, axis, [(i, i + by) for i in range(devices - by)])]
    another operation x1 -> x0, other arithmetic: 0.9 us -> none
    broadcast_in_dim x1 -> x0, local copies, waits for them, and re-layouts: 0.76 us -> none  [per_device(): entries = jnp.broadcast_to(page_table.reshape(-1, 1), (page_table.size, HD))]
    add x0 -> x1, other arithmetic: none -> 0.75 us  [per_device(): table = integers.astype(jnp.float32) + affine.astype(jnp.float32)]
    pallas_call x1, Pallas kernels: 1.94 us -> 1.24 us  [per_device(): pl.pallas_call(functools.partial(finish_kernel, heads), out_shape=[jax.Sh...]
    unnamed x6 -> x4, local copies, waits for them, and re-layouts: 1.05 us -> 1.28 us
  transfers between devices with their start and end apart: 20 -> 20, of which waited for: 5 -> 5; matrix products, arithmetic and copies ran while one was open for 5% -> 2% of each run, Pallas kernels for 12% -> 12%
where the time goes in v3:
time: 54.4 us; the launch traced here: 54.1 us
  starting transfers between devices  33.2 us (61%)
  Pallas kernels  11.6 us (21%)
  waiting for transfers between devices  5.66 us (10%)
  between operations  1.6 us (3%)
  local copies, waits for them, and re-layouts  1.28 us (2%)
  other arithmetic  0.82 us (2%)
    ppermute x16, starting transfers between devices, paired(): return lax.ppermute(shard, axis, [(i, i ^ bit) for i in range(devices)])  19.3 us
    ppermute x4, starting transfers between devices, forward(): return lax.ppermute(shard, axis, [(i, i + by) for i in range(devices - by)])  13.9 us
    ppermute x16, waiting for transfers between devices, paired(): return lax.ppermute(shard, axis, [(i, i ^ bit) for i in range(devices)])  5.65 us
    pallas_call x3, Pallas kernels, attend(): pl.pallas_call(functools.partial(attend_kernel, heads, reach, packs, tile...  5.42 us
    pallas_call x1, Pallas kernels, per_device(): pl.pallas_call(functools.partial(project_kernel, tp, heads), out_shape=[j...  3.61 us
    unnamed x4, local copies, waits for them, and re-layouts  1.28 us
    pallas_call x1, Pallas kernels, per_device(): pl.pallas_call(functools.partial(finish_kernel, heads), out_shape=[jax.Sh...  1.24 us
  transfers between devices with their start and end apart: 20, of which 5 were waited for; matrix products, arithmetic and copies ran while one was open for 2% of the time, Pallas kernels for 12%

profile of v3, /device:TPU:0, one launch (start us, length us, event | category | flops | bytes accessed | tf_op | source)
XLA Modules:
  0.0 54.1 jit_solution(14455718607748535236)
XLA Ops:
  0.6 0.5 collective-permute-start
  1.2 1.3 %copy-done.1 = bf16[256,1024]{1,0:T(8,128)(2,1)S(1)} copy-done((bf16[256,1024]{1,0:T(8,128)(2,1)S(1)}, bf16[256,1024]{1,0:T(8,128)(2,1)}, u32[]{:S(2)}) %copy-start.1) | copy-done | bytes 524312
  3.3 0.7 %convert_add_fusion.refs_3_ = f32[48,128]{1,0:T(8,128)S(1)} fusion(s32[2,2]{1,0:T(2,128)} %param.13, s32[2,128]{1,0:T(2,128)} %bitcast.24, bf16[16,128]{1,0:T(8,128)(2,1)} %bitcast.22, bf16[16,128]{1,0:T(8,128)(2,1)} %bitcast.23), kind=kLoop, calls=%fused_computation.2 | loop fusion | flops 43008 | bytes 33808 | tf_op jit(solution)/shard_map/add | solution.py:320
  4.0 3.6 %project.1 = (bf16[256,2048]{1,0:T(8,128)(2,1)S(1)}, bf16[272,128]{1,0:T(8,128)(2,1)S(1)}, bf16[256,128]{1,0:T(8,128)(2,1)S(1)}, bf16[272,128]{1,0:T(8,128)(2,1)...) custom-call(s32[1]{0:T(128)S(6)} %copy.9.refs_0_, ...), custom_call_target="tpu_custom_call" | custom-call | flops 1073741824 | bytes 4194304 | tf_op jit(solution)/shard_map/project/pallas_call | solution.py:332
  7.6 3.6 %collective-permute-start.6 = (bf16[272,128]{1,0:T(8,128)(2,1)S(1)}, bf16[272,128]{1,0:T(8,128)(2,1)S(1)}, u32[]{:S(2)}, u32[]{:S(2)}) collective-permute-start(bf16[272,128]{1,0:T(8,128)(2,1)S(1)} %get-tuple-element.51.refs_14_), channel_id=1, source_target_pairs={{0,6},{2,4},{4,2},{6,0},{8,14},{10,12},{12,10},{14,8},{16,22},{18,... | collective-permute-start | bytes 208904 | tf_op jit(solution)/shard_map/ppermute | solution.py:23
  11.2 0.5 collective-permute-start.5
  11.9 2.8 %collective-permute-start.11 = (bf16[256,128]{1,0:T(8,128)(2,1)S(1)}, bf16[256,128]{1,0:T(8,128)(2,1)S(1)}, u32[]{:S(2)}, u32[]{:S(2)}) collective-permute-start(bf16[256,128]{1,0:T(8,128)(2,1)S(1)} %get-tuple-element.55.refs_15_), channel_id=1, source_target_pairs={{0,6},{2,4},{4,2},{6,0},{8,14},{10,12},{12,10},{14,8},{16,22},{18,... | collective-permute-start | bytes 196616 | tf_op jit(solution)/shard_map/ppermute | solution.py:23
  14.7 0.5 collective-permute-start.10
  15.2 0.5 collective-permute-start.9
  15.7 1.0 %collective-permute-done.4 = bf16[272,128]{1,0:T(8,128)(2,1)S(1)} collective-permute-done((bf16[272,128]{1,0:T(8,128)(2,1)S(1)}, bf16[272,128]{1,0:T(8,128)(2,1)S(1)}, u32[]{:S(2)}, u32[]{:S(2)}) %collective-permute-start.4) | collective-permute-done | bytes 69664 | tf_op jit(solution)/shard_map/ppermute | solution.py:23
  16.8 3.5 %collective-permute-start.7 = (bf16[4,272,128]{2,1,0:T(8,128)(2,1)S(1)}, bf16[4,272,128]{2,1,0:T(8,128)(2,1)S(1)}, u32[]{:S(2)}, u32[]{:S(2)}) collective-permute-start(bf16[4,272,128]{2,1,0:T(8,128)(2,1)S(1)} %pad_maximum_fusion.refs_4_.refs_0_), channel_id=1, source_target_pairs={{0,8},{2,10},{4,12},{6,14},{8,16},{10,18},{12,20},{14,22},{16,24},... | collective-permute-start | bytes 835592 | tf_op jit(solution)/shard_map/ppermute | solution.py:28
  20.4 3.5 %collective-permute-start.12 = (bf16[4,256,128]{2,1,0:T(8,128)(2,1)S(1)}, bf16[4,256,128]{2,1,0:T(8,128)(2,1)S(1)}, u32[]{:S(2)}, u32[]{:S(2)}) collective-permute-start(bf16[4,256,128]{2,1,0:T(8,128)(2,1)S(1)} %pad_maximum_fusion.1.refs_5_.refs_7_), channel_id=1, source_target_pairs={{0,8},{2,10},{4,12},{6,14},{8,16},{10,18},{12,20},{14,22},{16,24},... | collective-permute-start | bytes 786440 | tf_op jit(solution)/shard_map/ppermute | solution.py:28
  23.9 0.9 %queries.1 = (bf16[256,128]{1,0:T(8,128)(2,1)S(1)}, bf16[256,128]{1,0:T(8,128)(2,1)S(1)}, bf16[256,128]{1,0:T(8,128)(2,1)S(1)}, bf16[256,128]{1,0:T(8,128)(2,1)S(1)}) custom-call(bf16[256,2048]{1,0:T(8,128)(2,1)S(1)} %get-tuple-element.43.normed_ref, bf16[3,2048,512]{2,1,0:T(8,128)(2,1)S(1)} %bitcast.13), custom_call_target="tpu_custom_call" | custom-call | flops 536870912 | bytes 2097152 | tf_op jit(solution)/shard_map/queries/pallas_call | solution.py:352
  24.8 0.9 %collective-permute-start.1 = (bf16[256,128]{1,0:T(8,128)(2,1)S(1)}, bf16[256,128]{1,0:T(8,128)(2,1)S(1)}, u32[]{:S(2)}, u32[]{:S(2)}) collective-permute-start(bf16[256,128]{1,0:T(8,128)(2,1)S(1)} %get-tuple-element.45), channel_id=1, source_target_pairs={{0,2},{2,0},{4,6},{6,4},{8,10},{10,8},{12,14},{14,12},{16,18},{18,... | collective-permute-start | bytes 196616 | tf_op jit(solution)/shard_map/ppermute | solution.py:23
  25.7 1.2 %collective-permute-start.2 = (bf16[256,128]{1,0:T(8,128)(2,1)S(1)}, bf16[256,128]{1,0:T(8,128)(2,1)S(1)}, u32[]{:S(2)}, u32[]{:S(2)}) collective-permute-start(bf16[256,128]{1,0:T(8,128)(2,1)S(1)} %get-tuple-element.46), channel_id=1, source_target_pairs={{0,4},{2,6},{4,0},{6,2},{8,12},{10,14},{12,8},{14,10},{16,20},{18,... | collective-permute-start | bytes 196616 | tf_op jit(solution)/shard_map/ppermute | solution.py:23
  26.9 1.4 %collective-permute-start.3 = (bf16[256,128]{1,0:T(8,128)(2,1)S(1)}, bf16[256,128]{1,0:T(8,128)(2,1)S(1)}, u32[]{:S(2)}, u32[]{:S(2)}) collective-permute-start(bf16[256,128]{1,0:T(8,128)(2,1)S(1)} %get-tuple-element.47), channel_id=1, source_target_pairs={{0,6},{2,4},{4,2},{6,0},{8,14},{10,12},{12,10},{14,8},{16,22},{18,... | collective-permute-start | bytes 196616 | tf_op jit(solution)/shard_map/ppermute | solution.py:23
  28.3 3.5 %collective-permute-start.8 = (bf16[4,272,128]{2,1,0:T(8,128)(2,1)S(1)}, bf16[4,272,128]{2,1,0:T(8,128)(2,1)S(1)}, u32[]{:S(2)}, u32[]{:S(2)}) collective-permute-start(bf16[4,272,128]{2,1,0:T(8,128)(2,1)S(1)} %collective-permute-done.7.refs_5_.refs_1_), channel_id=1, source_target_pairs={{0,8},{2,10},{4,12},{6,14},{8,16},{10,18},{12,20},{14,22},{16,24},... | collective-permute-start | bytes 835592 | tf_op jit(solution)/shard_map/ppermute | solution.py:28
  32.1 2.0 %attend.3 = (f32[4,256,128]{2,1,0:T(8,128)S(1)}, f32[4,256,128]{2,1,0:T(8,128)S(1)}, f32[4,256,256]{2,1,0:T(8,128)S(1)}) custom-call(bf16[256,128]{1,0:T(8,128)(2,1)S(1)} %get-tuple-element.44.refs_0_, bf16[256,128]{1,0:T(8,128)(2,1)S(1)} %collective-permute-done.1.refs_1_, bf16[256,128]{1,0:T(8,128)(2,1)S(1)} %collective-permute-done.2.refs_2_, ...), custom_call_target="tpu_custom_call" | custom-call | flops 805306368 | bytes 4194304 | tf_op jit(solution)/shard_map/attend/pallas_call | solution.py:395
  34.1 3.5 %collective-permute-start.13 = (bf16[4,256,128]{2,1,0:T(8,128)(2,1)S(1)}, bf16[4,256,128]{2,1,0:T(8,128)(2,1)S(1)}, u32[]{:S(2)}, u32[]{:S(2)}) collective-permute-start(bf16[4,256,128]{2,1,0:T(8,128)(2,1)S(1)} %collective-permute-done.12.refs_6_.refs_8_), channel_id=1, source_target_pairs={{0,8},{2,10},{4,12},{6,14},{8,16},{10,18},{12,20},{14,22},{16,24},... | collective-permute-start | bytes 786440 | tf_op jit(solution)/shard_map/ppermute | solution.py:28
  37.6 1.6 %attend.4 = (f32[4,256,128]{2,1,0:T(8,128)S(1)}, f32[4,256,256]{2,1,0:T(8,128)S(1)}) custom-call(bf16[256,128]{1,0:T(8,128)(2,1)S(1)} %get-tuple-element.44.refs_0_, bf16[256,128]{1,0:T(8,128)(2,1)S(1)} %collective-permute-done.1.refs_1_, bf16[256,128]{1,0:T(8,128)(2,1)S(1)} %collective-permute-done.2.refs_2_, ...), custom_call_target="tpu_custom_call" | custom-call | flops 805306368 | bytes 4194304 | tf_op jit(solution)/shard_map/attend/pallas_call | solution.py:395
  39.2 0.4 select.5
  39.6 1.1 %collective-permute-start.14 = (bf16[256,128]{1,0:T(8,128)(2,1)S(1)}, bf16[256,128]{1,0:T(8,128)(2,1)S(1)}, u32[]{:S(2)}, u32[]{:S(2)}) collective-permute-start(bf16[256,128]{1,0:T(8,128)(2,1)S(1)} %get-tuple-element.66), channel_id=1, source_target_pairs={{0,2},{2,0},{4,6},{6,4},{8,10},{10,8},{12,14},{14,12},{16,18},{18,... | collective-permute-start | bytes 196616 | tf_op jit(solution)/shard_map/ppermute | solution.py:23
  40.7 0.9 %collective-permute-start.16 = (bf16[256,128]{1,0:T(8,128)(2,1)S(1)}, bf16[256,128]{1,0:T(8,128)(2,1)S(1)}, u32[]{:S(2)}, u32[]{:S(2)}) collective-permute-start(bf16[256,128]{1,0:T(8,128)(2,1)S(1)} %get-tuple-element.69), channel_id=1, source_target_pairs={{0,4},{2,6},{4,0},{6,2},{8,12},{10,14},{12,8},{14,10},{16,20},{18,... | collective-permute-start | bytes 196616 | tf_op jit(solution)/shard_map/ppermute | solution.py:23
  41.7 1.5 %collective-permute-start.18 = (bf16[256,128]{1,0:T(8,128)(2,1)S(1)}, bf16[256,128]{1,0:T(8,128)(2,1)S(1)}, u32[]{:S(2)}, u32[]{:S(2)}) collective-permute-start(bf16[256,128]{1,0:T(8,128)(2,1)S(1)} %get-tuple-element.72), channel_id=1, source_target_pairs={{0,6},{2,4},{4,2},{6,0},{8,14},{10,12},{12,10},{14,8},{16,22},{18,... | collective-permute-start | bytes 196616 | tf_op jit(solution)/shard_map/ppermute | solution.py:23
  43.1 1.8 %attend.5 = (bf16[512,128]{1,0:T(8,128)(2,1)S(1)}, bf16[512,128]{1,0:T(8,128)(2,1)S(1)}, bf16[512,128]{1,0:T(8,128)(2,1)S(1)}, bf16[512,128]{1,0:T(8,128)(2,1)S(1)}) custom-call(bf16[256,128]{1,0:T(8,128)(2,1)S(1)} %get-tuple-element.44.refs_0_, bf16[256,128]{1,0:T(8,128)(2,1)S(1)} %collective-permute-done.1.refs_1_, ...), custom_call_target="tpu_custom_call" | custom-call | flops 805306368 | bytes 4194304 | tf_op jit(solution)/shard_map/attend/pallas_call | solution.py:395
  45.0 1.1 %collective-permute-start.15 = (bf16[512,128]{1,0:T(8,128)(2,1)S(1)}, bf16[512,128]{1,0:T(8,128)(2,1)S(1)}, u32[]{:S(2)}, u32[]{:S(2)}) collective-permute-start(bf16[512,128]{1,0:T(8,128)(2,1)S(1)} %get-tuple-element.67), channel_id=1, source_target_pairs={{0,2},{2,0},{4,6},{6,4},{8,10},{10,8},{12,14},{14,12},{16,18},{18,... | collective-permute-start | bytes 393224 | tf_op jit(solution)/shard_map/ppermute | solution.py:23
  46.1 0.9 %collective-permute-start.17 = (bf16[512,128]{1,0:T(8,128)(2,1)S(1)}, bf16[512,128]{1,0:T(8,128)(2,1)S(1)}, u32[]{:S(2)}, u32[]{:S(2)}) collective-permute-start(bf16[512,128]{1,0:T(8,128)(2,1)S(1)} %get-tuple-element.70), channel_id=1, source_target_pairs={{0,4},{2,6},{4,0},{6,2},{8,12},{10,14},{12,8},{14,10},{16,20},{18,... | collective-permute-start | bytes 393224 | tf_op jit(solution)/shard_map/ppermute | solution.py:23
  47.0 1.5 %collective-permute-start.19 = (bf16[512,128]{1,0:T(8,128)(2,1)S(1)}, bf16[512,128]{1,0:T(8,128)(2,1)S(1)}, u32[]{:S(2)}, u32[]{:S(2)}) collective-permute-start(bf16[512,128]{1,0:T(8,128)(2,1)S(1)} %get-tuple-element.73), channel_id=1, source_target_pairs={{0,6},{2,4},{4,2},{6,0},{8,14},{10,12},{12,10},{14,8},{16,22},{18,... | collective-permute-start | bytes 393224 | tf_op jit(solution)/shard_map/ppermute | solution.py:23
  48.5 2.8 %collective-permute-done.15.refs_1_ = bf16[512,128]{1,0:T(8,128)(2,1)S(1)} collective-permute-done((bf16[512,128]{1,0:T(8,128)(2,1)S(1)}, bf16[512,128]{1,0:T(8,128)(2,1)S(1)}, u32[]{:S(2)}, u32[]{:S(2)}) %collective-permute-start.15) | collective-permute-done | bytes 131104 | tf_op jit(solution)/shard_map/ppermute | solution.py:23
  51.3 0.2 collective-permute-done.17.refs_2_
  51.5 1.4 %collective-permute-done.19.refs_3_ = bf16[512,128]{1,0:T(8,128)(2,1)S(1)} collective-permute-done((bf16[512,128]{1,0:T(8,128)(2,1)S(1)}, bf16[512,128]{1,0:T(8,128)(2,1)S(1)}, u32[]{:S(2)}, u32[]{:S(2)}) %collective-permute-start.19) | collective-permute-done | bytes 131104 | tf_op jit(solution)/shard_map/ppermute | solution.py:23
  52.9 1.2 %finish.1 = (bf16[256,512]{1,0:T(8,128)(2,1)}, bf16[4,2,128,512]{3,2,1,0:T(8,128)(2,1)}) custom-call(bf16[512,128]{1,0:T(8,128)(2,1)S(1)} %get-tuple-element.64.refs_0_, bf16[512,128]{1,0:T(8,128)(2,1)S(1)} %collective-permute-done.15.refs_1_, bf16[512,128]{1,0:T(8,128)(2,1)S(1)} %collective-permute-done.17.refs_2_, ...), custom_call_target="tpu_custom_call" | custom-call | tf_op jit(solution)/shard_map/finish/pallas_call | solution.py:430
  (23 shorter events, 0.5 us)
Async XLA Ops:
  0.6 23.2 %copy-start = (bf16[2048,3,512]{2,0,1:T(8,128)(2,1)S(1)}, bf16[2048,3,512]{2,0,1:T(8,128)(2,1)}, u32[]{:S(2)}) copy-start(bf16[2048,3,512]{2,0,1:T(8,128)(2,1)} %param.10) | copy-start | bytes 18874372
  0.6 3.4 %collective-permute-start = (bf16[256,1024]{1,0:T(8,128)(2,1)}, bf16[256,1024]{1,0:T(8,128)(2,1)S(1)}, u32[]{:S(2)}, u32[]{:S(2)}) collective-permute-start(bf16[256,1024]{1,0:T(8,128)(2,1)} %tokens_ref.1), channel_id=1, source_target_pairs={{0,1},{1,0},{2,3},{3,2},{4,5},{5,4},{6,7},{7,6},{8,9},{9,8},{10,11... | collective-permute-start | bytes 1572872 | tf_op jit(solution)/shard_map/ppermute | solution.py:23
  1.2 1.3 %copy-start.1 = (bf16[256,1024]{1,0:T(8,128)(2,1)S(1)}, bf16[256,1024]{1,0:T(8,128)(2,1)}, u32[]{:S(2)}) copy-start(bf16[256,1024]{1,0:T(8,128)(2,1)} %tokens_ref.1) | copy-start | bytes 1572868
  7.6 7.6 %collective-permute-start.6 = (bf16[272,128]{1,0:T(8,128)(2,1)S(1)}, bf16[272,128]{1,0:T(8,128)(2,1)S(1)}, u32[]{:S(2)}, u32[]{:S(2)}) collective-permute-start(bf16[272,128]{1,0:T(8,128)(2,1)S(1)} %get-tuple-element.51.refs_14_), channel_id=1, source_target_pairs={{0,6},{2,4},{4,2},{6,0},{8,14},{10,12},{12,10},{14,8},{16,22},{18,... | collective-permute-start | bytes 208904 | tf_op jit(solution)/shard_map/ppermute | solution.py:23
  11.2 4.5 %collective-permute-start.5 = (bf16[272,128]{1,0:T(8,128)(2,1)S(1)}, bf16[272,128]{1,0:T(8,128)(2,1)S(1)}, u32[]{:S(2)}, u32[]{:S(2)}) collective-permute-start(bf16[272,128]{1,0:T(8,128)(2,1)S(1)} %get-tuple-element.50.refs_12_), channel_id=1, source_target_pairs={{0,4},{2,6},{4,0},{6,2},{8,12},{10,14},{12,8},{14,10},{16,20},{18,... | collective-permute-start | bytes 208904 | tf_op jit(solution)/shard_map/ppermute | solution.py:23
  11.7 5.0 %collective-permute-start.4 = (bf16[272,128]{1,0:T(8,128)(2,1)S(1)}, bf16[272,128]{1,0:T(8,128)(2,1)S(1)}, u32[]{:S(2)}, u32[]{:S(2)}) collective-permute-start(bf16[272,128]{1,0:T(8,128)(2,1)S(1)} %get-tuple-element.49.refs_10_), channel_id=1, source_target_pairs={{0,2},{2,0},{4,6},{6,4},{8,10},{10,8},{12,14},{14,12},{16,18},{18,... | collective-permute-start | bytes 208904 | tf_op jit(solution)/shard_map/ppermute | solution.py:23
  11.9 8.4 %collective-permute-start.11 = (bf16[256,128]{1,0:T(8,128)(2,1)S(1)}, bf16[256,128]{1,0:T(8,128)(2,1)S(1)}, u32[]{:S(2)}, u32[]{:S(2)}) collective-permute-start(bf16[256,128]{1,0:T(8,128)(2,1)S(1)} %get-tuple-element.55.refs_15_), channel_id=1, source_target_pairs={{0,6},{2,4},{4,2},{6,0},{8,14},{10,12},{12,10},{14,8},{16,22},{18,... | collective-permute-start | bytes 196616 | tf_op jit(solution)/shard_map/ppermute | solution.py:23
  14.7 5.6 %collective-permute-start.10 = (bf16[256,128]{1,0:T(8,128)(2,1)S(1)}, bf16[256,128]{1,0:T(8,128)(2,1)S(1)}, u32[]{:S(2)}, u32[]{:S(2)}) collective-permute-start(bf16[256,128]{1,0:T(8,128)(2,1)S(1)} %get-tuple-element.54.refs_13_), channel_id=1, source_target_pairs={{0,4},{2,6},{4,0},{6,2},{8,12},{10,14},{12,8},{14,10},{16,20},{18,... | collective-permute-start | bytes 196616 | tf_op jit(solution)/shard_map/ppermute | solution.py:23
  15.2 5.1 %collective-permute-start.9 = (bf16[256,128]{1,0:T(8,128)(2,1)S(1)}, bf16[256,128]{1,0:T(8,128)(2,1)S(1)}, u32[]{:S(2)}, u32[]{:S(2)}) collective-permute-start(bf16[256,128]{1,0:T(8,128)(2,1)S(1)} %get-tuple-element.53.refs_11_), channel_id=1, source_target_pairs={{0,2},{2,0},{4,6},{6,4},{8,10},{10,8},{12,14},{14,12},{16,18},{18,... | collective-permute-start | bytes 196616 | tf_op jit(solution)/shard_map/ppermute | solution.py:23
  16.8 11.6 %collective-permute-start.7 = (bf16[4,272,128]{2,1,0:T(8,128)(2,1)S(1)}, bf16[4,272,128]{2,1,0:T(8,128)(2,1)S(1)}, u32[]{:S(2)}, u32[]{:S(2)}) collective-permute-start(bf16[4,272,128]{2,1,0:T(8,128)(2,1)S(1)} %pad_maximum_fusion.refs_4_.refs_0_), channel_id=1, source_target_pairs={{0,8},{2,10},{4,12},{6,14},{8,16},{10,18},{12,20},{14,22},{16,24},... | collective-permute-start | bytes 835592 | tf_op jit(solution)/shard_map/ppermute | solution.py:28
  20.4 13.7 %collective-permute-start.12 = (bf16[4,256,128]{2,1,0:T(8,128)(2,1)S(1)}, bf16[4,256,128]{2,1,0:T(8,128)(2,1)S(1)}, u32[]{:S(2)}, u32[]{:S(2)}) collective-permute-start(bf16[4,256,128]{2,1,0:T(8,128)(2,1)S(1)} %pad_maximum_fusion.1.refs_5_.refs_7_), channel_id=1, source_target_pairs={{0,8},{2,10},{4,12},{6,14},{8,16},{10,18},{12,20},{14,22},{16,24},... | collective-permute-start | bytes 786440 | tf_op jit(solution)/shard_map/ppermute | solution.py:28
  24.8 7.0 %collective-permute-start.1 = (bf16[256,128]{1,0:T(8,128)(2,1)S(1)}, bf16[256,128]{1,0:T(8,128)(2,1)S(1)}, u32[]{:S(2)}, u32[]{:S(2)}) collective-permute-start(bf16[256,128]{1,0:T(8,128)(2,1)S(1)} %get-tuple-element.45), channel_id=1, source_target_pairs={{0,2},{2,0},{4,6},{6,4},{8,10},{10,8},{12,14},{14,12},{16,18},{18,... | collective-permute-start | bytes 196616 | tf_op jit(solution)/shard_map/ppermute | solution.py:23
  25.7 6.1 %collective-permute-start.2 = (bf16[256,128]{1,0:T(8,128)(2,1)S(1)}, bf16[256,128]{1,0:T(8,128)(2,1)S(1)}, u32[]{:S(2)}, u32[]{:S(2)}) collective-permute-start(bf16[256,128]{1,0:T(8,128)(2,1)S(1)} %get-tuple-element.46), channel_id=1, source_target_pairs={{0,4},{2,6},{4,0},{6,2},{8,12},{10,14},{12,8},{14,10},{16,20},{18,... | collective-permute-start | bytes 196616 | tf_op jit(solution)/shard_map/ppermute | solution.py:23
  26.9 5.2 %collective-permute-start.3 = (bf16[256,128]{1,0:T(8,128)(2,1)S(1)}, bf16[256,128]{1,0:T(8,128)(2,1)S(1)}, u32[]{:S(2)}, u32[]{:S(2)}) collective-permute-start(bf16[256,128]{1,0:T(8,128)(2,1)S(1)} %get-tuple-element.47), channel_id=1, source_target_pairs={{0,6},{2,4},{4,2},{6,0},{8,14},{10,12},{12,10},{14,8},{16,22},{18,... | collective-permute-start | bytes 196616 | tf_op jit(solution)/shard_map/ppermute | solution.py:23
  28.3 10.9 %collective-permute-start.8 = (bf16[4,272,128]{2,1,0:T(8,128)(2,1)S(1)}, bf16[4,272,128]{2,1,0:T(8,128)(2,1)S(1)}, u32[]{:S(2)}, u32[]{:S(2)}) collective-permute-start(bf16[4,272,128]{2,1,0:T(8,128)(2,1)S(1)} %collective-permute-done.7.refs_5_.refs_1_), channel_id=1, source_target_pairs={{0,8},{2,10},{4,12},{6,14},{8,16},{10,18},{12,20},{14,22},{16,24},... | collective-permute-start | bytes 835592 | tf_op jit(solution)/shard_map/ppermute | solution.py:28
  34.1 9.0 %collective-permute-start.13 = (bf16[4,256,128]{2,1,0:T(8,128)(2,1)S(1)}, bf16[4,256,128]{2,1,0:T(8,128)(2,1)S(1)}, u32[]{:S(2)}, u32[]{:S(2)}) collective-permute-start(bf16[4,256,128]{2,1,0:T(8,128)(2,1)S(1)} %collective-permute-done.12.refs_6_.refs_8_), channel_id=1, source_target_pairs={{0,8},{2,10},{4,12},{6,14},{8,16},{10,18},{12,20},{14,22},{16,24},... | collective-permute-start | bytes 786440 | tf_op jit(solution)/shard_map/ppermute | solution.py:28
  39.6 5.4 %collective-permute-start.14 = (bf16[256,128]{1,0:T(8,128)(2,1)S(1)}, bf16[256,128]{1,0:T(8,128)(2,1)S(1)}, u32[]{:S(2)}, u32[]{:S(2)}) collective-permute-start(bf16[256,128]{1,0:T(8,128)(2,1)S(1)} %get-tuple-element.66), channel_id=1, source_target_pairs={{0,2},{2,0},{4,6},{6,4},{8,10},{10,8},{12,14},{14,12},{16,18},{18,... | collective-permute-start | bytes 196616 | tf_op jit(solution)/shard_map/ppermute | solution.py:23
  40.7 5.4 %collective-permute-start.16 = (bf16[256,128]{1,0:T(8,128)(2,1)S(1)}, bf16[256,128]{1,0:T(8,128)(2,1)S(1)}, u32[]{:S(2)}, u32[]{:S(2)}) collective-permute-start(bf16[256,128]{1,0:T(8,128)(2,1)S(1)} %get-tuple-element.69), channel_id=1, source_target_pairs={{0,4},{2,6},{4,0},{6,2},{8,12},{10,14},{12,8},{14,10},{16,20},{18,... | collective-permute-start | bytes 196616 | tf_op jit(solution)/shard_map/ppermute | solution.py:23
  41.7 5.4 %collective-permute-start.18 = (bf16[256,128]{1,0:T(8,128)(2,1)S(1)}, bf16[256,128]{1,0:T(8,128)(2,1)S(1)}, u32[]{:S(2)}, u32[]{:S(2)}) collective-permute-start(bf16[256,128]{1,0:T(8,128)(2,1)S(1)} %get-tuple-element.72), channel_id=1, source_target_pairs={{0,6},{2,4},{4,2},{6,0},{8,14},{10,12},{12,10},{14,8},{16,22},{18,... | collective-permute-start | bytes 196616 | tf_op jit(solution)/shard_map/ppermute | solution.py:23
  45.0 6.3 %collective-permute-start.15 = (bf16[512,128]{1,0:T(8,128)(2,1)S(1)}, bf16[512,128]{1,0:T(8,128)(2,1)S(1)}, u32[]{:S(2)}, u32[]{:S(2)}) collective-permute-start(bf16[512,128]{1,0:T(8,128)(2,1)S(1)} %get-tuple-element.67), channel_id=1, source_target_pairs={{0,2},{2,0},{4,6},{6,4},{8,10},{10,8},{12,14},{14,12},{16,18},{18,... | collective-permute-start | bytes 393224 | tf_op jit(solution)/shard_map/ppermute | solution.py:23
  46.1 5.4 %collective-permute-start.17 = (bf16[512,128]{1,0:T(8,128)(2,1)S(1)}, bf16[512,128]{1,0:T(8,128)(2,1)S(1)}, u32[]{:S(2)}, u32[]{:S(2)}) collective-permute-start(bf16[512,128]{1,0:T(8,128)(2,1)S(1)} %get-tuple-element.70), channel_id=1, source_target_pairs={{0,4},{2,6},{4,0},{6,2},{8,12},{10,14},{12,8},{14,10},{16,20},{18,... | collective-permute-start | bytes 393224 | tf_op jit(solution)/shard_map/ppermute | solution.py:23
  47.0 5.9 %collective-permute-start.19 = (bf16[512,128]{1,0:T(8,128)(2,1)S(1)}, bf16[512,128]{1,0:T(8,128)(2,1)S(1)}, u32[]{:S(2)}, u32[]{:S(2)}) collective-permute-start(bf16[512,128]{1,0:T(8,128)(2,1)S(1)} %get-tuple-element.73), channel_id=1, source_target_pairs={{0,6},{2,4},{4,2},{6,0},{8,14},{10,12},{12,10},{14,8},{16,22},{18,... | collective-permute-start | bytes 393224 | tf_op jit(solution)/shard_map/ppermute | solution.py:23

commit v4 on v3

--- a/solution.py
+++ b/solution.py
@@ -46,7 +46,7 @@
     take = lambda count: [refs.pop(0) for _ in range(count)]
     lengths_ref, tokens_ref, w_hbm, table_ref = take(4)
     received, (normed_ref,), pieces = take(tp - 1), take(1), take(2 * heads)
-    w_ref, spread_ref, columns, sems = refs
+    w_ref, spread_ref, means_ref, columns, sems = refs
     rows, features = tokens_ref.shape
     here = lax.axis_index("tp")
     me = lax.axis_index("req") % heads
@@ -65,21 +65,28 @@
                 row * lines + line : row * lines + line + 1
             ]
     parts = [tokens_ref] + received
-    step = 32
+    ones = jnp.ones((features, HD), jnp.bfloat16)
+    share = 1.0 / (tp * features)
+    means_ref[...] = share * sum(
+        jnp.dot(part[...], ones, preferred_element_type=jnp.float32) for part in parts
+    )
+    step = 64
 
     def norm_rows(index, carry):
         at = pl.ds(pl.multiple_of(index * step, step), step)
-        shares = [part[at, :].astype(jnp.float32) for part in parts]
-        total = sum(jnp.sum(share, axis=1, keepdims=True) for share in shares)
-        mean = total * (1.0 / (tp * features))
-        centred = [share - mean for share in shares]
-        squares = sum(jnp.sum(share * share, axis=1, keepdims=True) for share in centred)
-        scale = lax.rsqrt(squares * (1.0 / (tp * features)) + 1e-05)
-        for bit, share in enumerate(centred):
-            lanes = pl.ds(pl.multiple_of((here ^ bit) * features, features), features)
-            gain = spread_ref[0:1, lanes]
-            bias = spread_ref[1:2, lanes]
-            normed_ref[at, lanes] = (share * scale * gain + bias).astype(jnp.bfloat16)
+        mean = means_ref[at, :]
+        chunks = [(bit, lane) for bit in range(tp) for lane in range(0, features, HD)]
+        squares = jnp.zeros((step, HD), jnp.float32)
+        for bit, lane in chunks:
+            centred = parts[bit][at, lane : lane + HD].astype(jnp.float32) - mean
+            squares = squares + centred * centred
+        variance = share * jnp.sum(squares, axis=1, keepdims=True)
+        scale = jnp.broadcast_to(lax.rsqrt(variance + 1e-05), (step, HD))
+        for bit, lane in chunks:
+            lanes = pl.ds(pl.multiple_of((here ^ bit) * features + lane, HD), HD)
+            centred = parts[bit][at, lane : lane + HD].astype(jnp.float32) - mean
+            normed = centred * scale * spread_ref[0:1, lanes] + spread_ref[1:2, lanes]
+            normed_ref[at, lanes] = normed.astype(jnp.bfloat16)
         return carry
 
     lax.fori_loop(0, rows // step, norm_rows, 0)
@@ -338,6 +345,7 @@
         scratch_shapes=[
             pltpu.VMEM((2, width, local_width), bf16),
             pltpu.VMEM((2, width), jnp.float32),
+            pltpu.VMEM((rows, HD), jnp.float32),
             pltpu.VMEM((rows, local_width), bf16),
             pltpu.SemaphoreType.DMA((2,)),
         ],
@@ -424,7 +432,7 @@
     early = [early[0]] + [paired(early[bit], "req", bit) for bit in range(1, heads)]
     final = list(attend([(reach, 0), (reach, 1)], [ids, *state], True, 1))
     for bit in range(1, heads):
-        final[bit], early[bit] = lax.optimization_barrier((final[bit], early[bit]))
+        final[bit], early[1 : bit + 1] = lax.optimization_barrier((final[bit], early[1 : bit + 1]))
     final = [final[0]] + [paired(final[bit], "req", bit) for bit in range(1, heads)]
 
     context, cache = pl.pallas_call(

time: 54.4 us -> 53.9 us (level)
  transfers between devices with their start and end apart: 20 -> 20, of which waited for: 5 -> 5; matrix products, arithmetic and copies ran while one was open for 2% -> 2% of each run, Pallas kernels for 12% -> 13%
where the time goes in v4:
time: 53.9 us; the launch traced here: 53.7 us
  starting transfers between devices  33.2 us (62%)
  Pallas kernels  11.1 us (21%)
  waiting for transfers between devices  5.66 us (11%)
  between operations  1.6 us (3%)
  local copies, waits for them, and re-layouts  1.28 us (2%)
  other arithmetic  0.82 us (2%)
    ppermute x16, starting transfers between devices, paired(): return lax.ppermute(shard, axis, [(i, i ^ bit) for i in range(devices)])  19.3 us
    ppermute x4, starting transfers between devices, forward(): return lax.ppermute(shard, axis, [(i, i + by) for i in range(devices - by)])  13.9 us
    ppermute x16, waiting for transfers between devices, paired(): return lax.ppermute(shard, axis, [(i, i ^ bit) for i in range(devices)])  5.65 us
    pallas_call x3, Pallas kernels, attend(): pl.pallas_call(functools.partial(attend_kernel, heads, reach, packs, tile...  5.42 us
    pallas_call x1, Pallas kernels, per_device(): pl.pallas_call(functools.partial(project_kernel, tp, heads), out_shape=[j...  3.14 us
    unnamed x4, local copies, waits for them, and re-layouts  1.28 us
    pallas_call x1, Pallas kernels, per_device(): pl.pallas_call(functools.partial(finish_kernel, heads), out_shape=[jax.Sh...  1.24 us
  transfers between devices with their start and end apart: 20, of which 5 were waited for; matrix products, arithmetic and copies ran while one was open for 2% of the time, Pallas kernels for 13%

profile of v4, /device:TPU:0, one launch (start us, length us, event | category | flops | bytes accessed | tf_op | source)
XLA Modules:
  0.0 53.7 jit_solution(11668987540806326119)
XLA Ops:
  0.6 0.5 collective-permute-start
  1.2 1.3 %copy-done.1 = bf16[256,1024]{1,0:T(8,128)(2,1)S(1)} copy-done((bf16[256,1024]{1,0:T(8,128)(2,1)S(1)}, bf16[256,1024]{1,0:T(8,128)(2,1)}, u32[]{:S(2)}) %copy-start.1) | copy-done | bytes 524312
  3.3 0.7 %convert_add_fusion.refs_3_ = f32[48,128]{1,0:T(8,128)S(1)} fusion(s32[2,2]{1,0:T(2,128)} %param.13, s32[2,128]{1,0:T(2,128)} %bitcast.24, bf16[16,128]{1,0:T(8,128)(2,1)} %bitcast.22, bf16[16,128]{1,0:T(8,128)(2,1)} %bitcast.23), kind=kLoop, calls=%fused_computation.2 | loop fusion | flops 43008 | bytes 33808 | tf_op jit(solution)/shard_map/add | solution.py:327
  4.0 3.1 %project.1 = (bf16[256,2048]{1,0:T(8,128)(2,1)S(1)}, bf16[272,128]{1,0:T(8,128)(2,1)S(1)}, bf16[256,128]{1,0:T(8,128)(2,1)S(1)}, bf16[272,128]{1,0:T(8,128)(2,1)...) custom-call(s32[1]{0:T(128)S(6)} %copy.9.refs_0_, ...), custom_call_target="tpu_custom_call" | custom-call | flops 1073741824 | bytes 4194304 | tf_op jit(solution)/shard_map/project/pallas_call | solution.py:339
  7.2 3.6 %collective-permute-start.6 = (bf16[272,128]{1,0:T(8,128)(2,1)S(1)}, bf16[272,128]{1,0:T(8,128)(2,1)S(1)}, u32[]{:S(2)}, u32[]{:S(2)}) collective-permute-start(bf16[272,128]{1,0:T(8,128)(2,1)S(1)} %get-tuple-element.54.refs_14_), channel_id=1, source_target_pairs={{0,6},{2,4},{4,2},{6,0},{8,14},{10,12},{12,10},{14,8},{16,22},{18,... | collective-permute-start | bytes 208904 | tf_op jit(solution)/shard_map/ppermute | solution.py:23
  10.8 0.5 collective-permute-start.5
  11.4 2.8 %collective-permute-start.11 = (bf16[256,128]{1,0:T(8,128)(2,1)S(1)}, bf16[256,128]{1,0:T(8,128)(2,1)S(1)}, u32[]{:S(2)}, u32[]{:S(2)}) collective-permute-start(bf16[256,128]{1,0:T(8,128)(2,1)S(1)} %get-tuple-element.58.refs_15_), channel_id=1, source_target_pairs={{0,6},{2,4},{4,2},{6,0},{8,14},{10,12},{12,10},{14,8},{16,22},{18,... | collective-permute-start | bytes 196616 | tf_op jit(solution)/shard_map/ppermute | solution.py:23
  14.3 0.5 collective-permute-start.10
  14.8 0.5 collective-permute-start.9
  15.3 1.0 %collective-permute-done.4 = bf16[272,128]{1,0:T(8,128)(2,1)S(1)} collective-permute-done((bf16[272,128]{1,0:T(8,128)(2,1)S(1)}, bf16[272,128]{1,0:T(8,128)(2,1)S(1)}, u32[]{:S(2)}, u32[]{:S(2)}) %collective-permute-start.4) | collective-permute-done | bytes 69664 | tf_op jit(solution)/shard_map/ppermute | solution.py:23
  16.3 3.5 %collective-permute-start.7 = (bf16[4,272,128]{2,1,0:T(8,128)(2,1)S(1)}, bf16[4,272,128]{2,1,0:T(8,128)(2,1)S(1)}, u32[]{:S(2)}, u32[]{:S(2)}) collective-permute-start(bf16[4,272,128]{2,1,0:T(8,128)(2,1)S(1)} %pad_maximum_fusion.refs_4_.refs_0_), channel_id=1, source_target_pairs={{0,8},{2,10},{4,12},{6,14},{8,16},{10,18},{12,20},{14,22},{16,24},... | collective-permute-start | bytes 835592 | tf_op jit(solution)/shard_map/ppermute | solution.py:28
  19.9 3.5 %collective-permute-start.12 = (bf16[4,256,128]{2,1,0:T(8,128)(2,1)S(1)}, bf16[4,256,128]{2,1,0:T(8,128)(2,1)S(1)}, u32[]{:S(2)}, u32[]{:S(2)}) collective-permute-start(bf16[4,256,128]{2,1,0:T(8,128)(2,1)S(1)} %pad_maximum_fusion.1.refs_5_.refs_7_), channel_id=1, source_target_pairs={{0,8},{2,10},{4,12},{6,14},{8,16},{10,18},{12,20},{14,22},{16,24},... | collective-permute-start | bytes 786440 | tf_op jit(solution)/shard_map/ppermute | solution.py:28
  23.4 0.9 %queries.1 = (bf16[256,128]{1,0:T(8,128)(2,1)S(1)}, bf16[256,128]{1,0:T(8,128)(2,1)S(1)}, bf16[256,128]{1,0:T(8,128)(2,1)S(1)}, bf16[256,128]{1,0:T(8,128)(2,1)S(1)}) custom-call(bf16[256,2048]{1,0:T(8,128)(2,1)S(1)} %get-tuple-element.46.normed_ref, bf16[3,2048,512]{2,1,0:T(8,128)(2,1)S(1)} %bitcast.13), custom_call_target="tpu_custom_call" | custom-call | flops 536870912 | bytes 2097152 | tf_op jit(solution)/shard_map/queries/pallas_call | solution.py:360
  24.3 0.9 %collective-permute-start.1 = (bf16[256,128]{1,0:T(8,128)(2,1)S(1)}, bf16[256,128]{1,0:T(8,128)(2,1)S(1)}, u32[]{:S(2)}, u32[]{:S(2)}) collective-permute-start(bf16[256,128]{1,0:T(8,128)(2,1)S(1)} %get-tuple-element.48), channel_id=1, source_target_pairs={{0,2},{2,0},{4,6},{6,4},{8,10},{10,8},{12,14},{14,12},{16,18},{18,... | collective-permute-start | bytes 196616 | tf_op jit(solution)/shard_map/ppermute | solution.py:23
  25.3 1.2 %collective-permute-start.2 = (bf16[256,128]{1,0:T(8,128)(2,1)S(1)}, bf16[256,128]{1,0:T(8,128)(2,1)S(1)}, u32[]{:S(2)}, u32[]{:S(2)}) collective-permute-start(bf16[256,128]{1,0:T(8,128)(2,1)S(1)} %get-tuple-element.49), channel_id=1, source_target_pairs={{0,4},{2,6},{4,0},{6,2},{8,12},{10,14},{12,8},{14,10},{16,20},{18,... | collective-permute-start | bytes 196616 | tf_op jit(solution)/shard_map/ppermute | solution.py:23
  26.4 1.4 %collective-permute-start.3 = (bf16[256,128]{1,0:T(8,128)(2,1)S(1)}, bf16[256,128]{1,0:T(8,128)(2,1)S(1)}, u32[]{:S(2)}, u32[]{:S(2)}) collective-permute-start(bf16[256,128]{1,0:T(8,128)(2,1)S(1)} %get-tuple-element.50), channel_id=1, source_target_pairs={{0,6},{2,4},{4,2},{6,0},{8,14},{10,12},{12,10},{14,8},{16,22},{18,... | collective-permute-start | bytes 196616 | tf_op jit(solution)/shard_map/ppermute | solution.py:23
  27.9 3.5 %collective-permute-start.8 = (bf16[4,272,128]{2,1,0:T(8,128)(2,1)S(1)}, bf16[4,272,128]{2,1,0:T(8,128)(2,1)S(1)}, u32[]{:S(2)}, u32[]{:S(2)}) collective-permute-start(bf16[4,272,128]{2,1,0:T(8,128)(2,1)S(1)} %collective-permute-done.7.refs_5_.refs_1_), channel_id=1, source_target_pairs={{0,8},{2,10},{4,12},{6,14},{8,16},{10,18},{12,20},{14,22},{16,24},... | collective-permute-start | bytes 835592 | tf_op jit(solution)/shard_map/ppermute | solution.py:28
  31.6 2.0 %attend.3 = (f32[4,256,128]{2,1,0:T(8,128)S(1)}, f32[4,256,128]{2,1,0:T(8,128)S(1)}, f32[4,256,256]{2,1,0:T(8,128)S(1)}) custom-call(bf16[256,128]{1,0:T(8,128)(2,1)S(1)} %get-tuple-element.47.refs_0_, bf16[256,128]{1,0:T(8,128)(2,1)S(1)} %collective-permute-done.1.refs_1_, bf16[256,128]{1,0:T(8,128)(2,1)S(1)} %collective-permute-done.2.refs_2_, ...), custom_call_target="tpu_custom_call" | custom-call | flops 805306368 | bytes 4194304 | tf_op jit(solution)/shard_map/attend/pallas_call | solution.py:403
  33.6 3.5 %collective-permute-start.13 = (bf16[4,256,128]{2,1,0:T(8,128)(2,1)S(1)}, bf16[4,256,128]{2,1,0:T(8,128)(2,1)S(1)}, u32[]{:S(2)}, u32[]{:S(2)}) collective-permute-start(bf16[4,256,128]{2,1,0:T(8,128)(2,1)S(1)} %collective-permute-done.12.refs_6_.refs_8_), channel_id=1, source_target_pairs={{0,8},{2,10},{4,12},{6,14},{8,16},{10,18},{12,20},{14,22},{16,24},... | collective-permute-start | bytes 786440 | tf_op jit(solution)/shard_map/ppermute | solution.py:28
  37.1 1.6 %attend.4 = (f32[4,256,128]{2,1,0:T(8,128)S(1)}, f32[4,256,256]{2,1,0:T(8,128)S(1)}) custom-call(bf16[256,128]{1,0:T(8,128)(2,1)S(1)} %get-tuple-element.47.refs_0_, bf16[256,128]{1,0:T(8,128)(2,1)S(1)} %collective-permute-done.1.refs_1_, bf16[256,128]{1,0:T(8,128)(2,1)S(1)} %collective-permute-done.2.refs_2_, ...), custom_call_target="tpu_custom_call" | custom-call | flops 805306368 | bytes 4194304 | tf_op jit(solution)/shard_map/attend/pallas_call | solution.py:403
  38.8 0.4 select.5
  39.1 1.1 %collective-permute-start.14 = (bf16[256,128]{1,0:T(8,128)(2,1)S(1)}, bf16[256,128]{1,0:T(8,128)(2,1)S(1)}, u32[]{:S(2)}, u32[]{:S(2)}) collective-permute-start(bf16[256,128]{1,0:T(8,128)(2,1)S(1)} %get-tuple-element.69), channel_id=1, source_target_pairs={{0,2},{2,0},{4,6},{6,4},{8,10},{10,8},{12,14},{14,12},{16,18},{18,... | collective-permute-start | bytes 196616 | tf_op jit(solution)/shard_map/ppermute | solution.py:23
  40.3 0.9 %collective-permute-start.16 = (bf16[256,128]{1,0:T(8,128)(2,1)S(1)}, bf16[256,128]{1,0:T(8,128)(2,1)S(1)}, u32[]{:S(2)}, u32[]{:S(2)}) collective-permute-start(bf16[256,128]{1,0:T(8,128)(2,1)S(1)} %get-tuple-element.73), channel_id=1, source_target_pairs={{0,4},{2,6},{4,0},{6,2},{8,12},{10,14},{12,8},{14,10},{16,20},{18,... | collective-permute-start | bytes 196616 | tf_op jit(solution)/shard_map/ppermute | solution.py:23
  41.2 1.5 %collective-permute-start.18 = (bf16[256,128]{1,0:T(8,128)(2,1)S(1)}, bf16[256,128]{1,0:T(8,128)(2,1)S(1)}, u32[]{:S(2)}, u32[]{:S(2)}) collective-permute-start(bf16[256,128]{1,0:T(8,128)(2,1)S(1)} %get-tuple-element.78), channel_id=1, source_target_pairs={{0,6},{2,4},{4,2},{6,0},{8,14},{10,12},{12,10},{14,8},{16,22},{18,... | collective-permute-start | bytes 196616 | tf_op jit(solution)/shard_map/ppermute | solution.py:23
  42.7 1.8 %attend.5 = (bf16[512,128]{1,0:T(8,128)(2,1)S(1)}, bf16[512,128]{1,0:T(8,128)(2,1)S(1)}, bf16[512,128]{1,0:T(8,128)(2,1)S(1)}, bf16[512,128]{1,0:T(8,128)(2,1)S(1)}) custom-call(bf16[256,128]{1,0:T(8,128)(2,1)S(1)} %get-tuple-element.47.refs_0_, bf16[256,128]{1,0:T(8,128)(2,1)S(1)} %collective-permute-done.1.refs_1_, ...), custom_call_target="tpu_custom_call" | custom-call | flops 805306368 | bytes 4194304 | tf_op jit(solution)/shard_map/attend/pallas_call | solution.py:403
  44.5 1.1 %collective-permute-start.15 = (bf16[512,128]{1,0:T(8,128)(2,1)S(1)}, bf16[512,128]{1,0:T(8,128)(2,1)S(1)}, u32[]{:S(2)}, u32[]{:S(2)}) collective-permute-start(bf16[512,128]{1,0:T(8,128)(2,1)S(1)} %get-tuple-element.70), channel_id=1, source_target_pairs={{0,2},{2,0},{4,6},{6,4},{8,10},{10,8},{12,14},{14,12},{16,18},{18,... | collective-permute-start | bytes 393224 | tf_op jit(solution)/shard_map/ppermute | solution.py:23
  45.6 0.9 %collective-permute-start.17 = (bf16[512,128]{1,0:T(8,128)(2,1)S(1)}, bf16[512,128]{1,0:T(8,128)(2,1)S(1)}, u32[]{:S(2)}, u32[]{:S(2)}) collective-permute-start(bf16[512,128]{1,0:T(8,128)(2,1)S(1)} %get-tuple-element.74), channel_id=1, source_target_pairs={{0,4},{2,6},{4,0},{6,2},{8,12},{10,14},{12,8},{14,10},{16,20},{18,... | collective-permute-start | bytes 393224 | tf_op jit(solution)/shard_map/ppermute | solution.py:23
  46.6 1.5 %collective-permute-start.19 = (bf16[512,128]{1,0:T(8,128)(2,1)S(1)}, bf16[512,128]{1,0:T(8,128)(2,1)S(1)}, u32[]{:S(2)}, u32[]{:S(2)}) collective-permute-start(bf16[512,128]{1,0:T(8,128)(2,1)S(1)} %get-tuple-element.79), channel_id=1, source_target_pairs={{0,6},{2,4},{4,2},{6,0},{8,14},{10,12},{12,10},{14,8},{16,22},{18,... | collective-permute-start | bytes 393224 | tf_op jit(solution)/shard_map/ppermute | solution.py:23
  48.1 2.8 %collective-permute-done.15.refs_1_ = bf16[512,128]{1,0:T(8,128)(2,1)S(1)} collective-permute-done((bf16[512,128]{1,0:T(8,128)(2,1)S(1)}, bf16[512,128]{1,0:T(8,128)(2,1)S(1)}, u32[]{:S(2)}, u32[]{:S(2)}) %collective-permute-start.15) | collective-permute-done | bytes 131104 | tf_op jit(solution)/shard_map/ppermute | solution.py:23
  50.8 0.2 collective-permute-done.17.refs_2_
  51.0 1.4 %collective-permute-done.19.refs_3_ = bf16[512,128]{1,0:T(8,128)(2,1)S(1)} collective-permute-done((bf16[512,128]{1,0:T(8,128)(2,1)S(1)}, bf16[512,128]{1,0:T(8,128)(2,1)S(1)}, u32[]{:S(2)}, u32[]{:S(2)}) %collective-permute-start.19) | collective-permute-done | bytes 131104 | tf_op jit(solution)/shard_map/ppermute | solution.py:23
  52.4 1.2 %finish.1 = (bf16[256,512]{1,0:T(8,128)(2,1)}, bf16[4,2,128,512]{3,2,1,0:T(8,128)(2,1)}) custom-call(bf16[512,128]{1,0:T(8,128)(2,1)S(1)} %get-tuple-element.67.refs_0_, bf16[512,128]{1,0:T(8,128)(2,1)S(1)} %collective-permute-done.15.refs_1_, bf16[512,128]{1,0:T(8,128)(2,1)S(1)} %collective-permute-done.17.refs_2_, ...), custom_call_target="tpu_custom_call" | custom-call | tf_op jit(solution)/shard_map/finish/pallas_call | solution.py:438
  (23 shorter events, 0.5 us)
Async XLA Ops:
  0.6 22.8 %copy-start = (bf16[2048,3,512]{2,0,1:T(8,128)(2,1)S(1)}, bf16[2048,3,512]{2,0,1:T(8,128)(2,1)}, u32[]{:S(2)}) copy-start(bf16[2048,3,512]{2,0,1:T(8,128)(2,1)} %param.10) | copy-start | bytes 18874372
  0.6 3.4 %collective-permute-start = (bf16[256,1024]{1,0:T(8,128)(2,1)}, bf16[256,1024]{1,0:T(8,128)(2,1)S(1)}, u32[]{:S(2)}, u32[]{:S(2)}) collective-permute-start(bf16[256,1024]{1,0:T(8,128)(2,1)} %tokens_ref.1), channel_id=1, source_target_pairs={{0,1},{1,0},{2,3},{3,2},{4,5},{5,4},{6,7},{7,6},{8,9},{9,8},{10,11... | collective-permute-start | bytes 1572872 | tf_op jit(solution)/shard_map/ppermute | solution.py:23
  1.2 1.3 %copy-start.1 = (bf16[256,1024]{1,0:T(8,128)(2,1)S(1)}, bf16[256,1024]{1,0:T(8,128)(2,1)}, u32[]{:S(2)}) copy-start(bf16[256,1024]{1,0:T(8,128)(2,1)} %tokens_ref.1) | copy-start | bytes 1572868
  7.2 7.6 %collective-permute-start.6 = (bf16[272,128]{1,0:T(8,128)(2,1)S(1)}, bf16[272,128]{1,0:T(8,128)(2,1)S(1)}, u32[]{:S(2)}, u32[]{:S(2)}) collective-permute-start(bf16[272,128]{1,0:T(8,128)(2,1)S(1)} %get-tuple-element.54.refs_14_), channel_id=1, source_target_pairs={{0,6},{2,4},{4,2},{6,0},{8,14},{10,12},{12,10},{14,8},{16,22},{18,... | collective-permute-start | bytes 208904 | tf_op jit(solution)/shard_map/ppermute | solution.py:23
  10.8 4.5 %collective-permute-start.5 = (bf16[272,128]{1,0:T(8,128)(2,1)S(1)}, bf16[272,128]{1,0:T(8,128)(2,1)S(1)}, u32[]{:S(2)}, u32[]{:S(2)}) collective-permute-start(bf16[272,128]{1,0:T(8,128)(2,1)S(1)} %get-tuple-element.53.refs_12_), channel_id=1, source_target_pairs={{0,4},{2,6},{4,0},{6,2},{8,12},{10,14},{12,8},{14,10},{16,20},{18,... | collective-permute-start | bytes 208904 | tf_op jit(solution)/shard_map/ppermute | solution.py:23
  11.3 5.0 %collective-permute-start.4 = (bf16[272,128]{1,0:T(8,128)(2,1)S(1)}, bf16[272,128]{1,0:T(8,128)(2,1)S(1)}, u32[]{:S(2)}, u32[]{:S(2)}) collective-permute-start(bf16[272,128]{1,0:T(8,128)(2,1)S(1)} %get-tuple-element.52.refs_10_), channel_id=1, source_target_pairs={{0,2},{2,0},{4,6},{6,4},{8,10},{10,8},{12,14},{14,12},{16,18},{18,... | collective-permute-start | bytes 208904 | tf_op jit(solution)/shard_map/ppermute | solution.py:23
  11.4 8.4 %collective-permute-start.11 = (bf16[256,128]{1,0:T(8,128)(2,1)S(1)}, bf16[256,128]{1,0:T(8,128)(2,1)S(1)}, u32[]{:S(2)}, u32[]{:S(2)}) collective-permute-start(bf16[256,128]{1,0:T(8,128)(2,1)S(1)} %get-tuple-element.58.refs_15_), channel_id=1, source_target_pairs={{0,6},{2,4},{4,2},{6,0},{8,14},{10,12},{12,10},{14,8},{16,22},{18,... | collective-permute-start | bytes 196616 | tf_op jit(solution)/shard_map/ppermute | solution.py:23
  14.3 5.6 %collective-permute-start.10 = (bf16[256,128]{1,0:T(8,128)(2,1)S(1)}, bf16[256,128]{1,0:T(8,128)(2,1)S(1)}, u32[]{:S(2)}, u32[]{:S(2)}) collective-permute-start(bf16[256,128]{1,0:T(8,128)(2,1)S(1)} %get-tuple-element.57.refs_13_), channel_id=1, source_target_pairs={{0,4},{2,6},{4,0},{6,2},{8,12},{10,14},{12,8},{14,10},{16,20},{18,... | collective-permute-start | bytes 196616 | tf_op jit(solution)/shard_map/ppermute | solution.py:23
  14.8 5.1 %collective-permute-start.9 = (bf16[256,128]{1,0:T(8,128)(2,1)S(1)}, bf16[256,128]{1,0:T(8,128)(2,1)S(1)}, u32[]{:S(2)}, u32[]{:S(2)}) collective-permute-start(bf16[256,128]{1,0:T(8,128)(2,1)S(1)} %get-tuple-element.56.refs_11_), channel_id=1, source_target_pairs={{0,2},{2,0},{4,6},{6,4},{8,10},{10,8},{12,14},{14,12},{16,18},{18,... | collective-permute-start | bytes 196616 | tf_op jit(solution)/shard_map/ppermute | solution.py:23
  16.3 11.6 %collective-permute-start.7 = (bf16[4,272,128]{2,1,0:T(8,128)(2,1)S(1)}, bf16[4,272,128]{2,1,0:T(8,128)(2,1)S(1)}, u32[]{:S(2)}, u32[]{:S(2)}) collective-permute-start(bf16[4,272,128]{2,1,0:T(8,128)(2,1)S(1)} %pad_maximum_fusion.refs_4_.refs_0_), channel_id=1, source_target_pairs={{0,8},{2,10},{4,12},{6,14},{8,16},{10,18},{12,20},{14,22},{16,24},... | collective-permute-start | bytes 835592 | tf_op jit(solution)/shard_map/ppermute | solution.py:28
  19.9 13.7 %collective-permute-start.12 = (bf16[4,256,128]{2,1,0:T(8,128)(2,1)S(1)}, bf16[4,256,128]{2,1,0:T(8,128)(2,1)S(1)}, u32[]{:S(2)}, u32[]{:S(2)}) collective-permute-start(bf16[4,256,128]{2,1,0:T(8,128)(2,1)S(1)} %pad_maximum_fusion.1.refs_5_.refs_7_), channel_id=1, source_target_pairs={{0,8},{2,10},{4,12},{6,14},{8,16},{10,18},{12,20},{14,22},{16,24},... | collective-permute-start | bytes 786440 | tf_op jit(solution)/shard_map/ppermute | solution.py:28
  24.3 7.0 %collective-permute-start.1 = (bf16[256,128]{1,0:T(8,128)(2,1)S(1)}, bf16[256,128]{1,0:T(8,128)(2,1)S(1)}, u32[]{:S(2)}, u32[]{:S(2)}) collective-permute-start(bf16[256,128]{1,0:T(8,128)(2,1)S(1)} %get-tuple-element.48), channel_id=1, source_target_pairs={{0,2},{2,0},{4,6},{6,4},{8,10},{10,8},{12,14},{14,12},{16,18},{18,... | collective-permute-start | bytes 196616 | tf_op jit(solution)/shard_map/ppermute | solution.py:23
  25.3 6.1 %collective-permute-start.2 = (bf16[256,128]{1,0:T(8,128)(2,1)S(1)}, bf16[256,128]{1,0:T(8,128)(2,1)S(1)}, u32[]{:S(2)}, u32[]{:S(2)}) collective-permute-start(bf16[256,128]{1,0:T(8,128)(2,1)S(1)} %get-tuple-element.49), channel_id=1, source_target_pairs={{0,4},{2,6},{4,0},{6,2},{8,12},{10,14},{12,8},{14,10},{16,20},{18,... | collective-permute-start | bytes 196616 | tf_op jit(solution)/shard_map/ppermute | solution.py:23
  26.4 5.2 %collective-permute-start.3 = (bf16[256,128]{1,0:T(8,128)(2,1)S(1)}, bf16[256,128]{1,0:T(8,128)(2,1)S(1)}, u32[]{:S(2)}, u32[]{:S(2)}) collective-permute-start(bf16[256,128]{1,0:T(8,128)(2,1)S(1)} %get-tuple-element.50), channel_id=1, source_target_pairs={{0,6},{2,4},{4,2},{6,0},{8,14},{10,12},{12,10},{14,8},{16,22},{18,... | collective-permute-start | bytes 196616 | tf_op jit(solution)/shard_map/ppermute | solution.py:23
  27.9 10.9 %collective-permute-start.8 = (bf16[4,272,128]{2,1,0:T(8,128)(2,1)S(1)}, bf16[4,272,128]{2,1,0:T(8,128)(2,1)S(1)}, u32[]{:S(2)}, u32[]{:S(2)}) collective-permute-start(bf16[4,272,128]{2,1,0:T(8,128)(2,1)S(1)} %collective-permute-done.7.refs_5_.refs_1_), channel_id=1, source_target_pairs={{0,8},{2,10},{4,12},{6,14},{8,16},{10,18},{12,20},{14,22},{16,24},... | collective-permute-start | bytes 835592 | tf_op jit(solution)/shard_map/ppermute | solution.py:28
  33.6 9.0 %collective-permute-start.13 = (bf16[4,256,128]{2,1,0:T(8,128)(2,1)S(1)}, bf16[4,256,128]{2,1,0:T(8,128)(2,1)S(1)}, u32[]{:S(2)}, u32[]{:S(2)}) collective-permute-start(bf16[4,256,128]{2,1,0:T(8,128)(2,1)S(1)} %collective-permute-done.12.refs_6_.refs_8_), channel_id=1, source_target_pairs={{0,8},{2,10},{4,12},{6,14},{8,16},{10,18},{12,20},{14,22},{16,24},... | collective-permute-start | bytes 786440 | tf_op jit(solution)/shard_map/ppermute | solution.py:28
  39.1 5.4 %collective-permute-start.14 = (bf16[256,128]{1,0:T(8,128)(2,1)S(1)}, bf16[256,128]{1,0:T(8,128)(2,1)S(1)}, u32[]{:S(2)}, u32[]{:S(2)}) collective-permute-start(bf16[256,128]{1,0:T(8,128)(2,1)S(1)} %get-tuple-element.69), channel_id=1, source_target_pairs={{0,2},{2,0},{4,6},{6,4},{8,10},{10,8},{12,14},{14,12},{16,18},{18,... | collective-permute-start | bytes 196616 | tf_op jit(solution)/shard_map/ppermute | solution.py:23
  40.3 5.4 %collective-permute-start.16 = (bf16[256,128]{1,0:T(8,128)(2,1)S(1)}, bf16[256,128]{1,0:T(8,128)(2,1)S(1)}, u32[]{:S(2)}, u32[]{:S(2)}) collective-permute-start(bf16[256,128]{1,0:T(8,128)(2,1)S(1)} %get-tuple-element.73), channel_id=1, source_target_pairs={{0,4},{2,6},{4,0},{6,2},{8,12},{10,14},{12,8},{14,10},{16,20},{18,... | collective-permute-start | bytes 196616 | tf_op jit(solution)/shard_map/ppermute | solution.py:23
  41.2 5.4 %collective-permute-start.18 = (bf16[256,128]{1,0:T(8,128)(2,1)S(1)}, bf16[256,128]{1,0:T(8,128)(2,1)S(1)}, u32[]{:S(2)}, u32[]{:S(2)}) collective-permute-start(bf16[256,128]{1,0:T(8,128)(2,1)S(1)} %get-tuple-element.78), channel_id=1, source_target_pairs={{0,6},{2,4},{4,2},{6,0},{8,14},{10,12},{12,10},{14,8},{16,22},{18,... | collective-permute-start | bytes 196616 | tf_op jit(solution)/shard_map/ppermute | solution.py:23
  44.5 6.3 %collective-permute-start.15 = (bf16[512,128]{1,0:T(8,128)(2,1)S(1)}, bf16[512,128]{1,0:T(8,128)(2,1)S(1)}, u32[]{:S(2)}, u32[]{:S(2)}) collective-permute-start(bf16[512,128]{1,0:T(8,128)(2,1)S(1)} %get-tuple-element.70), channel_id=1, source_target_pairs={{0,2},{2,0},{4,6},{6,4},{8,10},{10,8},{12,14},{14,12},{16,18},{18,... | collective-permute-start | bytes 393224 | tf_op jit(solution)/shard_map/ppermute | solution.py:23
  45.6 5.4 %collective-permute-start.17 = (bf16[512,128]{1,0:T(8,128)(2,1)S(1)}, bf16[512,128]{1,0:T(8,128)(2,1)S(1)}, u32[]{:S(2)}, u32[]{:S(2)}) collective-permute-start(bf16[512,128]{1,0:T(8,128)(2,1)S(1)} %get-tuple-element.74), channel_id=1, source_target_pairs={{0,4},{2,6},{4,0},{6,2},{8,12},{10,14},{12,8},{14,10},{16,20},{18,... | collective-permute-start | bytes 393224 | tf_op jit(solution)/shard_map/ppermute | solution.py:23
  46.6 5.9 %collective-permute-start.19 = (bf16[512,128]{1,0:T(8,128)(2,1)S(1)}, bf16[512,128]{1,0:T(8,128)(2,1)S(1)}, u32[]{:S(2)}, u32[]{:S(2)}) collective-permute-start(bf16[512,128]{1,0:T(8,128)(2,1)S(1)} %get-tuple-element.79), channel_id=1, source_target_pairs={{0,6},{2,4},{4,2},{6,0},{8,14},{10,12},{12,10},{14,8},{16,22},{18,... | collective-permute-start | bytes 393224 | tf_op jit(solution)/shard_map/ppermute | solution.py:23

commit v5 on v4

--- a/solution.py
+++ b/solution.py
@@ -10,7 +10,6 @@
 PAGE = 128
 REACH = 8
 NOTES = 16
-LIMIT_ROW = 6
 MASKED = -1e30
 PROJECT_VMEM = 48 << 20
 VMEM = pl.BlockSpec(memory_space=pltpu.VMEM)
@@ -36,16 +35,15 @@
     kept_ref[...] = tokens_ref[...]
 
 
-def below_limit(notes, row_count):
-    rows = lax.broadcasted_iota(jnp.int32, (row_count, HD), 0)
-    return rows.astype(jnp.float32) < notes[LIMIT_ROW : LIMIT_ROW + 1]
+def move(distance, slot):
+    return 4 * distance + slot + 1
 
 
 def project_kernel(tp, heads, *refs):
     refs = list(refs)
     take = lambda count: [refs.pop(0) for _ in range(count)]
     lengths_ref, tokens_ref, w_hbm, table_ref = take(4)
-    received, (normed_ref,), pieces = take(tp - 1), take(1), take(2 * heads)
+    received, (normed_ref, valid_ref), pieces = take(tp - 1), take(2), take(2 * heads)
     w_ref, spread_ref, means_ref, columns, sems = refs
     rows, features = tokens_ref.shape
     here = lax.axis_index("tp")
@@ -56,7 +54,6 @@
     ]
     for load in loads:
         load.start()
-    notes = table_ref[:NOTES, :] + 1.0
     affine = table_ref[NOTES:, :]
     lines = affine.shape[0] // 2
     for row in range(2):
@@ -94,14 +91,15 @@
     device = lax.axis_index("req")
     per_pack = lax.axis_size("req") // lengths_ref.shape[0]
     limit = lengths_ref[device // per_pack] - device % per_pack * rows
-    limit = jnp.clip(limit, 0, rows).astype(jnp.float32)
-    row = lax.broadcasted_iota(jnp.int32, notes.shape, 0)
-    entries = [notes[2 + page : 3 + page, at : at + 1] for page in range(2) for at in range(2)]
-    for at, entry in enumerate(entries):
-        notes = jnp.where(row == 2 + at, entry, notes)
-    notes = jnp.where(row == LIMIT_ROW, limit, notes)
-    valid = below_limit(notes, rows)
-    notes = notes.astype(jnp.bfloat16)
+    valid = lax.broadcasted_iota(jnp.int32, (rows, HD), 0) < limit
+    valid_ref[...] = valid.astype(jnp.float32)
+    row = lax.broadcasted_iota(jnp.int32, (NOTES, HD), 0)
+    notes = jnp.zeros((NOTES, HD), jnp.float32)
+    for page in range(2):
+        entry = table_ref[2 + page : 3 + page, :]
+        way = move(entry[:, 0:1] - device.astype(jnp.float32), entry[:, 1:2])
+        notes = jnp.where(row % 4 == page, table_ref[page : page + 1, :] + 1.0, notes)
+        notes = jnp.where(row % 4 == 2 + page, way, notes)
     for which in range(2):
         loads[which].wait()
         projected = jnp.dot(normed_ref[...], w_ref[which], preferred_element_type=jnp.float32)
@@ -114,7 +112,8 @@
                 ]
 
     for bit in range(heads):
-        pieces[2 * bit][2 * PAGE :, :] = notes
+        kept = jnp.where(row // 4 == bit, notes, 0.0)
+        pieces[2 * bit][2 * PAGE :, :] = kept.astype(jnp.bfloat16)
 
 
 def query_kernel(heads, normed_ref, w_hbm, *refs):
@@ -147,69 +146,81 @@
     rows = 2 * PAGE
     width = heads * PAGE
     notes = {
-        layer: [buffer[bit, 2 * PAGE :, :].astype(jnp.float32) for bit in range(heads)]
-        for layer, buffer in noted.items()
+        layer: buffer[2 * PAGE * heads :, :].astype(jnp.float32) for layer, buffer in noted.items()
     }
-    keys, values, key_ids, key_places = [], [], [], []
-    ones = jnp.ones((width, HD), jnp.bfloat16)
-    lane = lax.broadcasted_iota(jnp.int32, (1, PAGE), 1)
-    for layer, page in tiles:
-        buffer = pages[layer, page]
-        keys.append(buffer[:, :PAGE].reshape(width, HD))
-        values.append(
-            jnp.concatenate([buffer[:, PAGE : 2 * PAGE].reshape(width, HD), ones], axis=1)
-        )
-        ids = jnp.concatenate([note[page : page + 1] for note in notes[layer]], axis=1)
-        if layer > 0:
-            same_pack = (device - layer * heads) // per_pack == device // per_pack
-            ids = jnp.where(same_pack, ids, 0.0)
-        key_ids.append(ids)
-        key_places.append(
-            jnp.concatenate(
-                [lane + ((me ^ bit) * rows + page * PAGE) for bit in range(heads)], axis=1
+
+    def accumulate(used):
+        keys, values, key_ids, key_places = [], [], [], []
+        ones = jnp.ones((width, HD), jnp.bfloat16)
+        lane = lax.broadcasted_iota(jnp.int32, (1, PAGE), 1)
+        for layer, page in used:
+            buffer = pages[layer, page]
+            blocks = buffer.at[: 2 * PAGE * heads].reshape(heads, 2 * PAGE, HD)
+            keys.append(blocks[:, :PAGE].reshape(width, HD))
+            values.append(jnp.concatenate([blocks[:, PAGE:].reshape(width, HD), ones], axis=1))
+            ids = [notes[layer][4 * bit + page : 4 * bit + page + 1] for bit in range(heads)]
+            ids = jnp.concatenate(ids, axis=1)
+            if layer > 0:
+                same_pack = (device - layer * heads) // per_pack == device // per_pack
+                ids = jnp.where(same_pack, ids, 0.0)
+            key_ids.append(ids)
+            key_places.append(
+                jnp.concatenate(
+                    [lane + ((me ^ bit) * rows + page * PAGE) for bit in range(heads)], axis=1
+                )
             )
-        )
-    wide = (PAGE, HD)
-    for bit in range(heads):
-        for page in range(2):
-            at = pl.ds(page * PAGE, PAGE)
-            query = queries[bit][at, :]
-            if first:
-                query_ids = jnp.broadcast_to(notes[0][bit][page : page + 1], wide).T
-                ids_ref[bit, at] = query_ids
-                place = lax.broadcasted_iota(jnp.int32, wide, 0) + ((me ^ bit) * rows + page * PAGE)
-                top = jnp.full(wide, MASKED, jnp.float32)
-                total = [jnp.zeros(wide, jnp.float32)] * 2
-            else:
-                query_ids = ids_ref[bit, at]
-                top = top_ref[bit, at]
-                total = [total_ref[bit, at, half * HD : (half + 1) * HD] for half in range(2)]
-            for index, (layer, _) in enumerate(tiles):
-                scores = lax.dot_general(
-                    query, keys[index], (((1,), (1,)), ((), ())), preferred_element_type=jnp.float32
-                )
-                chunks = []
-                for other in range(heads):
-                    lanes = slice(other * PAGE, (other + 1) * PAGE)
-                    allowed = key_ids[index][:, lanes] == query_ids
-                    if layer == 0:
-                        allowed = allowed & (key_places[index][:, lanes] <= place)
-                    chunks.append(jnp.where(allowed, scores[:, lanes], MASKED))
-                highest = jnp.max(functools.reduce(jnp.maximum, chunks), axis=1, keepdims=True)
-                higher = jnp.maximum(top, jnp.broadcast_to(highest, wide))
-                weights = jnp.concatenate(
-                    [jnp.exp(chunk - higher).astype(jnp.bfloat16) for chunk in chunks], axis=1
-                )
-                shrink = jnp.exp(top - higher)
-                added = jnp.dot(weights, values[index], preferred_element_type=jnp.float32)
-                total = [total[half] * shrink + added[:, half * HD : (half + 1) * HD] for half in range(2)]
-                top = higher
-            if last:
-                outs[bit][at, :] = (total[0] / total[1]).astype(jnp.bfloat16)
-            else:
-                top_out[bit, at] = top
-                for half in range(2):
-                    total_out[bit, at, half * HD : (half + 1) * HD] = total[half]
+        wide = (PAGE, HD)
+        for bit in range(heads):
+            for page in range(2):
+                at = pl.ds(page * PAGE, PAGE)
+                query = queries[bit][at, :]
+                if first:
+                    query_ids = jnp.broadcast_to(
+                        notes[0][4 * bit + page : 4 * bit + page + 1], wide
+                    ).T
+                    ids_ref[bit, at] = query_ids
+                    place = lax.broadcasted_iota(jnp.int32, wide, 0) + ((me ^ bit) * rows + page * PAGE)
+                    top = jnp.full(wide, MASKED, jnp.float32)
+                    total = [jnp.zeros(wide, jnp.float32)] * 2
+                else:
+                    query_ids = ids_ref[bit, at]
+                    top = top_ref[bit, at]
+                    total = [total_ref[bit, at, half * HD : (half + 1) * HD] for half in range(2)]
+                for index, (layer, _) in enumerate(used):
+                    scores = lax.dot_general(
+                        query, keys[index], (((1,), (1,)), ((), ())), preferred_element_type=jnp.float32
+                    )
+                    chunks = []
+                    for other in range(heads):
+                        lanes = slice(other * PAGE, (other + 1) * PAGE)
+                        allowed = key_ids[index][:, lanes] == query_ids
+                        if layer == 0:
+                            allowed = allowed & (key_places[index][:, lanes] <= place)
+                        chunks.append(jnp.where(allowed, scores[:, lanes], MASKED))
+                    highest = jnp.max(functools.reduce(jnp.maximum, chunks), axis=1, keepdims=True)
+                    higher = jnp.maximum(top, jnp.broadcast_to(highest, wide))
+                    weights = jnp.concatenate(
+                        [jnp.exp(chunk - higher).astype(jnp.bfloat16) for chunk in chunks], axis=1
+                    )
+                    shrink = jnp.exp(top - higher)
+                    added = jnp.dot(weights, values[index], preferred_element_type=jnp.float32)
+                    total = [total[half] * shrink + added[:, half * HD : (half + 1) * HD] for half in range(2)]
+                    top = higher
+                if last:
+                    outs[bit][at, :] = (total[0] / total[1]).astype(jnp.bfloat16)
+                else:
+                    top_out[bit, at] = top
+                    for half in range(2):
+                        total_out[bit, at, half * HD : (half + 1) * HD] = total[half]
+
+    if first:
+        accumulate(tiles)
+    else:
+        (back,) = set(layer for layer, _ in tiles)
+        present = (device - back * heads) // per_pack == device // per_pack
+        pl.when(present)(lambda: accumulate(tiles))
+        pl.when(jnp.logical_not(present))(lambda: accumulate([]))
+
     if cache_page is not None:
         select_pages(heads, reach, cache_page, device, notes, pages, outs, rows)
 
@@ -218,16 +229,15 @@
     me = device % heads
     sought = jnp.zeros((1, HD), jnp.int32)
     for bit in range(heads):
-        owner = ((device ^ bit) + 1).astype(jnp.float32)
         for layer in range(reach + 1):
             for other in range(heads):
                 if layer == 0 and other == bit:
                     continue
-                note = notes[layer][other]
-                at = 2 + 2 * page
-                hit = (note[at : at + 1] == owner) & (note[at + 1 : at + 2] == page + 1.0)
+                distance = layer * heads + (me ^ bit) - (me ^ other)
+                at = 4 * other + 2 + page
+                hit = notes[layer][at : at + 1] == move(distance, page).astype(jnp.float32)
                 place = (layer * heads + other + 1) << (6 * bit)
-                sought = sought | jnp.where(hit, place, 0)
+                sought = sought | jnp.where(hit & (distance > 0), place, 0)
     sought = jnp.max(sought)
     for bit in range(heads):
         found = ((sought >> (6 * bit)) & 63) - 1
@@ -235,9 +245,8 @@
 
             @pl.when((found >= layer * heads) & (found < (layer + 1) * heads))
             def _():
-                outs[bit][start : start + 2 * PAGE, :] = pages[layer, page][
-                    found - layer * heads, : 2 * PAGE, :
-                ]
+                at = pl.multiple_of((found - layer * heads) * (2 * PAGE), 2 * PAGE)
+                outs[bit][start : start + 2 * PAGE, :] = pages[layer, page][pl.ds(at, 2 * PAGE), :]
 
         @pl.when(found < 0)
         def _():
@@ -246,10 +255,7 @@
 
 def select_kernel(heads, reach, *refs):
     buffers, outs = refs[: reach + 1], refs[reach + 1 :]
-    notes = [
-        [buffer[bit, 2 * PAGE :, :].astype(jnp.float32) for bit in range(heads)]
-        for buffer in buffers
-    ]
+    notes = [buffer[2 * PAGE * heads :, :].astype(jnp.float32) for buffer in buffers]
     pages = {(layer, 0): buffer for layer, buffer in enumerate(buffers)}
     select_pages(heads, reach, 0, lax.axis_index("req"), notes, pages, outs, 0)
 
@@ -269,19 +275,14 @@
 def finish_kernel(heads, *refs):
     refs = list(refs)
     take = lambda count: [refs.pop(0) for _ in range(count)]
-    final, early, own = take(heads), take(heads), take(2 * heads)
+    final, early, own, (valid_ref,) = take(heads), take(heads), take(2 * heads), take(1)
     context_ref, cache_ref = refs
     device = lax.axis_index("req")
     me = device % heads
     rows = context_ref.shape[0]
     notes = own[0][2 * PAGE :, :].astype(jnp.float32)
-    valid = below_limit(notes, rows)
-    here = (device + 1).astype(jnp.float32)
-    stays = [
-        (notes[2 + 2 * page : 3 + 2 * page] == here)
-        & (notes[3 + 2 * page : 4 + 2 * page] == page + 3.0)
-        for page in range(2)
-    ]
+    valid = valid_ref[...] > 0.0
+    stays = [notes[2 + page : 3 + page] == move(0, page + 2) for page in range(2)]
     for bit in range(heads):
         lanes = pl.ds(pl.multiple_of((me ^ bit) * HD, HD), HD)
         context = final[bit][0:rows, :].astype(jnp.float32)
@@ -336,12 +337,15 @@
     )(tokens)
 
     piece_shapes = [(2 * PAGE + NOTES, HD), (2 * PAGE, HD)] * heads
-    normed, *own = pl.pallas_call(
+    normed, valid, *own = pl.pallas_call(
         functools.partial(project_kernel, tp, heads),
-        out_shape=[jax.ShapeDtypeStruct((rows, width), bf16)]
+        out_shape=[
+            jax.ShapeDtypeStruct((rows, width), bf16),
+            jax.ShapeDtypeStruct((rows, HD), jnp.float32),
+        ]
         + [jax.ShapeDtypeStruct(shape, bf16) for shape in piece_shapes],
         in_specs=[SMEM, VMEM, HBM] + [VMEM] * tp,
-        out_specs=[VMEM] * (1 + 2 * heads),
+        out_specs=[VMEM] * (2 + 2 * heads),
         scratch_shapes=[
             pltpu.VMEM((2, width, local_width), bf16),
             pltpu.VMEM((2, width), jnp.float32),
@@ -353,10 +357,22 @@
         cost_estimate=cost(4 * rows * width * local_width, 4 * width * local_width),
         name="project",
     )(pack_lengths, kept, weights, table, *received)
+    firsts, seconds = (
+        [own[page]] + [paired(own[2 * bit + page], "req", bit) for bit in range(1, heads)]
+        for page in range(2)
+    )
+    all_notes = sum(piece[2 * PAGE :] for piece in firsts)
+    size = 2 * PAGE * heads + NOTES
+
+    def laid(piece, row):
+        return jnp.pad(piece, ((row, size - row - piece.shape[0]), (0, 0)))
+
     pages = [
-        jnp.stack([own[page]] + [paired(own[2 * bit + page], "req", bit) for bit in range(1, heads)])
-        for page in range(2)
+        laid(all_notes, 2 * PAGE * heads)
+        + sum(laid(piece[: 2 * PAGE], 2 * PAGE * bit) for bit, piece in enumerate(firsts)),
+        jnp.stack(seconds).reshape(-1, HD),
     ]
+
     queries = pl.pallas_call(
         functools.partial(query_kernel, heads),
         out_shape=[jax.ShapeDtypeStruct((rows, HD), bf16)] * heads,
@@ -441,11 +457,11 @@
             jax.ShapeDtypeStruct((rows, local_width), bf16),
             jax.ShapeDtypeStruct((4, 2, PAGE, local_width), bf16),
         ],
-        in_specs=[VMEM] * (4 * heads),
+        in_specs=[VMEM] * (4 * heads + 1),
         out_specs=[VMEM] * 2,
         compiler_params=pltpu.CompilerParams(vmem_limit_bytes=16 << 20),
         name="finish",
-    )(*final, *early, *own)
+    )(*final, *early, *own, valid)
     return context, cache
 
 

time: 53.9 us -> 53.3 us (0.989)
  Pallas kernels: 11.1 us -> 8.51 us
  waiting for transfers between devices: 5.66 us -> 7.6 us
    pallas_call x3, Pallas kernels: 5.42 us -> 2.8 us  [attend(): pl.pallas_call(functools.partial(attend_kernel, heads, reach, packs, tile...]
    ppermute x16, waiting for transfers between devices: 5.65 us -> 7.59 us  [paired(): return lax.ppermute(shard, axis, [(i, i ^ bit) for i in range(devices)])]
  transfers between devices with their start and end apart: 20 -> 20, of which waited for: 5 -> 7; matrix products, arithmetic and copies ran while one was open for 2% -> 2% of each run, Pallas kernels for 13% -> 8%
where the time goes in v5:
time: 53.3 us; the launch traced here: 52.9 us
  starting transfers between devices  33.1 us (62%)
  Pallas kernels  8.51 us (16%)
  waiting for transfers between devices  7.6 us (14%)
  between operations  1.61 us (3%)
  local copies, waits for them, and re-layouts  1.3 us (2%)
  other arithmetic  0.81 us (2%)
    ppermute x16, starting transfers between devices, paired(): return lax.ppermute(shard, axis, [(i, i ^ bit) for i in range(devices)])  19.1 us
    ppermute x4, starting transfers between devices, forward(): return lax.ppermute(shard, axis, [(i, i + by) for i in range(devices - by)])  13.9 us
    ppermute x16, waiting for transfers between devices, paired(): return lax.ppermute(shard, axis, [(i, i ^ bit) for i in range(devices)])  7.59 us
    pallas_call x1, Pallas kernels, per_device(): pl.pallas_call(functools.partial(project_kernel, tp, heads), out_shape=[j...  3.14 us
    pallas_call x3, Pallas kernels, attend(): pl.pallas_call(functools.partial(attend_kernel, heads, reach, packs, tile...  2.8 us
    unnamed x4, local copies, waits for them, and re-layouts  1.28 us
    pallas_call x1, Pallas kernels, per_device(): pl.pallas_call(functools.partial(finish_kernel, heads), out_shape=[jax.Sh...  1.23 us
  transfers between devices with their start and end apart: 20, of which 7 were waited for; matrix products, arithmetic and copies ran while one was open for 2% of the time, Pallas kernels for 8%

profile of v5, /device:TPU:0, one launch (start us, length us, event | category | flops | bytes accessed | tf_op | source)
XLA Modules:
  0.0 52.9 jit_solution(17860563021092587804)
XLA Ops:
  0.6 0.5 collective-permute-start
  1.2 1.3 %copy-done.1 = bf16[256,1024]{1,0:T(8,128)(2,1)S(1)} copy-done((bf16[256,1024]{1,0:T(8,128)(2,1)S(1)}, bf16[256,1024]{1,0:T(8,128)(2,1)}, u32[]{:S(2)}) %copy-start.1) | copy-done | bytes 524312
  3.3 0.7 %convert_add_fusion.refs_3_ = f32[48,128]{1,0:T(8,128)S(1)} fusion(s32[2,2]{1,0:T(2,128)} %param.13, s32[2,128]{1,0:T(2,128)} %bitcast.20, bf16[16,128]{1,0:T(8,128)(2,1)} %bitcast.18, bf16[16,128]{1,0:T(8,128)(2,1)} %bitcast.19), kind=kLoop, calls=%fused_computation.2 | loop fusion | flops 43008 | bytes 33808 | tf_op jit(solution)/shard_map/add | solution.py:328
  4.0 3.1 %project.1 = (bf16[256,2048]{1,0:T(8,128)(2,1)S(1)}, f32[256,128]{1,0:T(8,128)S(1)}, bf16[272,128]{1,0:T(8,128)(2,1)S(1)}, bf16[256,128]{1,0:T(8,128)(2,1)S(1)},...) custom-call(s32[1]{0:T(128)S(6)} %copy.9.refs_0_, ...), custom_call_target="tpu_custom_call" | custom-call | flops 1073741824 | bytes 4194304 | tf_op jit(solution)/shard_map/project/pallas_call | solution.py:340
  7.2 3.6 %collective-permute-start.6 = (bf16[272,128]{1,0:T(8,128)(2,1)S(1)}, bf16[272,128]{1,0:T(8,128)(2,1)S(1)}, u32[]{:S(2)}, u32[]{:S(2)}) collective-permute-start(bf16[272,128]{1,0:T(8,128)(2,1)S(1)} %get-tuple-element.55.refs_14_), channel_id=1, source_target_pairs={{0,6},{2,4},{4,2},{6,0},{8,14},{10,12},{12,10},{14,8},{16,22},{18,... | collective-permute-start | bytes 208904 | tf_op jit(solution)/shard_map/ppermute | solution.py:22
  10.8 0.5 collective-permute-start.5
  11.4 2.8 %collective-permute-start.11 = (bf16[256,128]{1,0:T(8,128)(2,1)S(1)}, bf16[256,128]{1,0:T(8,128)(2,1)S(1)}, u32[]{:S(2)}, u32[]{:S(2)}) collective-permute-start(bf16[256,128]{1,0:T(8,128)(2,1)S(1)} %get-tuple-element.59.refs_15_), channel_id=1, source_target_pairs={{0,6},{2,4},{4,2},{6,0},{8,14},{10,12},{12,10},{14,8},{16,22},{18,... | collective-permute-start | bytes 196616 | tf_op jit(solution)/shard_map/ppermute | solution.py:22
  14.3 0.5 collective-permute-start.10
  14.8 0.5 collective-permute-start.9
  15.3 1.0 %collective-permute-done.4 = bf16[272,128]{1,0:T(8,128)(2,1)S(1)} collective-permute-done((bf16[272,128]{1,0:T(8,128)(2,1)S(1)}, bf16[272,128]{1,0:T(8,128)(2,1)S(1)}, u32[]{:S(2)}, u32[]{:S(2)}) %collective-permute-start.4) | collective-permute-done | bytes 69664 | tf_op jit(solution)/shard_map/ppermute | solution.py:22
  16.3 3.5 %collective-permute-start.7 = (bf16[1040,128]{1,0:T(8,128)(2,1)S(1)}, bf16[1040,128]{1,0:T(8,128)(2,1)S(1)}, u32[]{:S(2)}, u32[]{:S(2)}) collective-permute-start(bf16[1040,128]{1,0:T(8,128)(2,1)S(1)} %add_add_fusion.refs_4_.refs_0_), channel_id=1, source_target_pairs={{0,8},{2,10},{4,12},{6,14},{8,16},{10,18},{12,20},{14,22},{16,24},... | collective-permute-start | bytes 798728 | tf_op jit(solution)/shard_map/ppermute | solution.py:27
  19.9 3.5 %collective-permute-start.12 = (bf16[1024,128]{1,0:T(8,128)(2,1)S(1)}, bf16[1024,128]{1,0:T(8,128)(2,1)S(1)}, u32[]{:S(2)}, u32[]{:S(2)}) collective-permute-start(bf16[1024,128]{1,0:T(8,128)(2,1)S(1)} %bitcast.11), channel_id=1, source_target_pairs={{0,8},{2,10},{4,12},{6,14},{8,16},{10,18},{12,20},{14,22},{16,24},... | collective-permute-start | bytes 786440 | tf_op jit(solution)/shard_map/ppermute | solution.py:27
  23.4 0.9 %queries.1 = (bf16[256,128]{1,0:T(8,128)(2,1)S(1)}, bf16[256,128]{1,0:T(8,128)(2,1)S(1)}, bf16[256,128]{1,0:T(8,128)(2,1)S(1)}, bf16[256,128]{1,0:T(8,128)(2,1)S(1)}) custom-call(bf16[256,2048]{1,0:T(8,128)(2,1)S(1)} %get-tuple-element.47.normed_ref, bf16[3,2048,512]{2,1,0:T(8,128)(2,1)S(1)} %bitcast.10), custom_call_target="tpu_custom_call" | custom-call | flops 536870912 | bytes 2097152 | tf_op jit(solution)/shard_map/queries/pallas_call | solution.py:376
  24.3 1.0 %collective-permute-start.1 = (bf16[256,128]{1,0:T(8,128)(2,1)S(1)}, bf16[256,128]{1,0:T(8,128)(2,1)S(1)}, u32[]{:S(2)}, u32[]{:S(2)}) collective-permute-start(bf16[256,128]{1,0:T(8,128)(2,1)S(1)} %get-tuple-element.49), channel_id=1, source_target_pairs={{0,2},{2,0},{4,6},{6,4},{8,10},{10,8},{12,14},{14,12},{16,18},{18,... | collective-permute-start | bytes 196616 | tf_op jit(solution)/shard_map/ppermute | solution.py:22
  25.3 1.2 %collective-permute-start.2 = (bf16[256,128]{1,0:T(8,128)(2,1)S(1)}, bf16[256,128]{1,0:T(8,128)(2,1)S(1)}, u32[]{:S(2)}, u32[]{:S(2)}) collective-permute-start(bf16[256,128]{1,0:T(8,128)(2,1)S(1)} %get-tuple-element.50), channel_id=1, source_target_pairs={{0,4},{2,6},{4,0},{6,2},{8,12},{10,14},{12,8},{14,10},{16,20},{18,... | collective-permute-start | bytes 196616 | tf_op jit(solution)/shard_map/ppermute | solution.py:22
  26.5 1.4 %collective-permute-start.3 = (bf16[256,128]{1,0:T(8,128)(2,1)S(1)}, bf16[256,128]{1,0:T(8,128)(2,1)S(1)}, u32[]{:S(2)}, u32[]{:S(2)}) collective-permute-start(bf16[256,128]{1,0:T(8,128)(2,1)S(1)} %get-tuple-element.51), channel_id=1, source_target_pairs={{0,6},{2,4},{4,2},{6,0},{8,14},{10,12},{12,10},{14,8},{16,22},{18,... | collective-permute-start | bytes 196616 | tf_op jit(solution)/shard_map/ppermute | solution.py:22
  27.9 3.5 %collective-permute-start.8 = (bf16[1040,128]{1,0:T(8,128)(2,1)S(1)}, bf16[1040,128]{1,0:T(8,128)(2,1)S(1)}, u32[]{:S(2)}, u32[]{:S(2)}) collective-permute-start(bf16[1040,128]{1,0:T(8,128)(2,1)S(1)} %collective-permute-done.7.refs_5_.refs_1_), channel_id=1, source_target_pairs={{0,8},{2,10},{4,12},{6,14},{8,16},{10,18},{12,20},{14,22},{16,24},... | collective-permute-start | bytes 798728 | tf_op jit(solution)/shard_map/ppermute | solution.py:27
  31.6 2.2 %attend.3 = (f32[4,256,128]{2,1,0:T(8,128)S(1)}, f32[4,256,128]{2,1,0:T(8,128)S(1)}, f32[4,256,256]{2,1,0:T(8,128)S(1)}) custom-call(bf16[256,128]{1,0:T(8,128)(2,1)S(1)} %get-tuple-element.48.refs_0_, bf16[256,128]{1,0:T(8,128)(2,1)S(1)} %collective-permute-done.1.refs_1_, bf16[256,128]{1,0:T(8,128)(2,1)S(1)} %collective-permute-done.2.refs_2_, ...), custom_call_target="tpu_custom_call" | custom-call | flops 805306368 | bytes 4194304 | tf_op jit(solution)/shard_map/attend/pallas_call | solution.py:419
  33.9 3.5 %collective-permute-start.13 = (bf16[1024,128]{1,0:T(8,128)(2,1)S(1)}, bf16[1024,128]{1,0:T(8,128)(2,1)S(1)}, u32[]{:S(2)}, u32[]{:S(2)}) collective-permute-start(bf16[1024,128]{1,0:T(8,128)(2,1)S(1)} %collective-permute-done.12.refs_6_.refs_8_), channel_id=1, source_target_pairs={{0,8},{2,10},{4,12},{6,14},{8,16},{10,18},{12,20},{14,22},{16,24},... | collective-permute-start | bytes 786440 | tf_op jit(solution)/shard_map/ppermute | solution.py:27
  37.5 0.4 select.10
  37.9 1.2 %collective-permute-start.14 = (bf16[256,128]{1,0:T(8,128)(2,1)S(1)}, bf16[256,128]{1,0:T(8,128)(2,1)S(1)}, u32[]{:S(2)}, u32[]{:S(2)}) collective-permute-start(bf16[256,128]{1,0:T(8,128)(2,1)S(1)} %get-tuple-element.70), channel_id=1, source_target_pairs={{0,2},{2,0},{4,6},{6,4},{8,10},{10,8},{12,14},{14,12},{16,18},{18,... | collective-permute-start | bytes 196616 | tf_op jit(solution)/shard_map/ppermute | solution.py:22
  39.1 0.8 %collective-permute-start.16 = (bf16[256,128]{1,0:T(8,128)(2,1)S(1)}, bf16[256,128]{1,0:T(8,128)(2,1)S(1)}, u32[]{:S(2)}, u32[]{:S(2)}) collective-permute-start(bf16[256,128]{1,0:T(8,128)(2,1)S(1)} %get-tuple-element.74), channel_id=1, source_target_pairs={{0,4},{2,6},{4,0},{6,2},{8,12},{10,14},{12,8},{14,10},{16,20},{18,... | collective-permute-start | bytes 196616 | tf_op jit(solution)/shard_map/ppermute | solution.py:22
  39.9 1.5 %collective-permute-start.18 = (bf16[256,128]{1,0:T(8,128)(2,1)S(1)}, bf16[256,128]{1,0:T(8,128)(2,1)S(1)}, u32[]{:S(2)}, u32[]{:S(2)}) collective-permute-start(bf16[256,128]{1,0:T(8,128)(2,1)S(1)} %get-tuple-element.79), channel_id=1, source_target_pairs={{0,6},{2,4},{4,2},{6,0},{8,14},{10,12},{12,10},{14,8},{16,22},{18,... | collective-permute-start | bytes 196616 | tf_op jit(solution)/shard_map/ppermute | solution.py:22
  41.5 0.5 attend.5
  42.2 1.5 %collective-permute-start.15 = (bf16[512,128]{1,0:T(8,128)(2,1)S(1)}, bf16[512,128]{1,0:T(8,128)(2,1)S(1)}, u32[]{:S(2)}, u32[]{:S(2)}) collective-permute-start(bf16[512,128]{1,0:T(8,128)(2,1)S(1)} %get-tuple-element.71), channel_id=1, source_target_pairs={{0,2},{2,0},{4,6},{6,4},{8,10},{10,8},{12,14},{14,12},{16,18},{18,... | collective-permute-start | bytes 393224 | tf_op jit(solution)/shard_map/ppermute | solution.py:22
  43.8 0.4 collective-permute-start.17
  44.2 1.6 %collective-permute-done.18.refs_7_ = bf16[256,128]{1,0:T(8,128)(2,1)S(1)} collective-permute-done((bf16[256,128]{1,0:T(8,128)(2,1)S(1)}, bf16[256,128]{1,0:T(8,128)(2,1)S(1)}, u32[]{:S(2)}, u32[]{:S(2)}) %collective-permute-start.18) | collective-permute-done | bytes 65568 | tf_op jit(solution)/shard_map/ppermute | solution.py:22
  45.8 1.4 %collective-permute-start.19 = (bf16[512,128]{1,0:T(8,128)(2,1)S(1)}, bf16[512,128]{1,0:T(8,128)(2,1)S(1)}, u32[]{:S(2)}, u32[]{:S(2)}) collective-permute-start(bf16[512,128]{1,0:T(8,128)(2,1)S(1)} %get-tuple-element.80), channel_id=1, source_target_pairs={{0,6},{2,4},{4,2},{6,0},{8,14},{10,12},{12,10},{14,8},{16,22},{18,... | collective-permute-start | bytes 393224 | tf_op jit(solution)/shard_map/ppermute | solution.py:22
  47.2 1.0 %collective-permute-done.15.refs_1_ = bf16[512,128]{1,0:T(8,128)(2,1)S(1)} collective-permute-done((bf16[512,128]{1,0:T(8,128)(2,1)S(1)}, bf16[512,128]{1,0:T(8,128)(2,1)S(1)}, u32[]{:S(2)}, u32[]{:S(2)}) %collective-permute-start.15) | collective-permute-done | bytes 131104 | tf_op jit(solution)/shard_map/ppermute | solution.py:22
  48.3 1.1 %collective-permute-done.17.refs_2_ = bf16[512,128]{1,0:T(8,128)(2,1)S(1)} collective-permute-done((bf16[512,128]{1,0:T(8,128)(2,1)S(1)}, bf16[512,128]{1,0:T(8,128)(2,1)S(1)}, u32[]{:S(2)}, u32[]{:S(2)}) %collective-permute-start.17) | collective-permute-done | bytes 131104 | tf_op jit(solution)/shard_map/ppermute | solution.py:22
  49.4 2.3 %collective-permute-done.19.refs_3_ = bf16[512,128]{1,0:T(8,128)(2,1)S(1)} collective-permute-done((bf16[512,128]{1,0:T(8,128)(2,1)S(1)}, bf16[512,128]{1,0:T(8,128)(2,1)S(1)}, u32[]{:S(2)}, u32[]{:S(2)}) %collective-permute-start.19) | collective-permute-done | bytes 131104 | tf_op jit(solution)/shard_map/ppermute | solution.py:22
  51.7 1.2 %finish.1 = (bf16[256,512]{1,0:T(8,128)(2,1)}, bf16[4,2,128,512]{3,2,1,0:T(8,128)(2,1)}) custom-call(bf16[512,128]{1,0:T(8,128)(2,1)S(1)} %get-tuple-element.68.refs_0_, bf16[512,128]{1,0:T(8,128)(2,1)S(1)} %collective-permute-done.15.refs_1_, bf16[512,128]{1,0:T(8,128)(2,1)S(1)} %collective-permute-done.17.refs_2_, ...), custom_call_target="tpu_custom_call" | custom-call | tf_op jit(solution)/shard_map/finish/pallas_call | solution.py:454
  (28 shorter events, 1.0 us)
Async XLA Ops:
  0.6 22.8 %copy-start = (bf16[2048,3,512]{2,0,1:T(8,128)(2,1)S(1)}, bf16[2048,3,512]{2,0,1:T(8,128)(2,1)}, u32[]{:S(2)}) copy-start(bf16[2048,3,512]{2,0,1:T(8,128)(2,1)} %param.10) | copy-start | bytes 18874372
  0.6 3.4 %collective-permute-start = (bf16[256,1024]{1,0:T(8,128)(2,1)}, bf16[256,1024]{1,0:T(8,128)(2,1)S(1)}, u32[]{:S(2)}, u32[]{:S(2)}) collective-permute-start(bf16[256,1024]{1,0:T(8,128)(2,1)} %tokens_ref.1), channel_id=1, source_target_pairs={{0,1},{1,0},{2,3},{3,2},{4,5},{5,4},{6,7},{7,6},{8,9},{9,8},{10,11... | collective-permute-start | bytes 1572872 | tf_op jit(solution)/shard_map/ppermute | solution.py:22
  1.2 1.3 %copy-start.1 = (bf16[256,1024]{1,0:T(8,128)(2,1)S(1)}, bf16[256,1024]{1,0:T(8,128)(2,1)}, u32[]{:S(2)}) copy-start(bf16[256,1024]{1,0:T(8,128)(2,1)} %tokens_ref.1) | copy-start | bytes 1572868
  7.2 7.6 %collective-permute-start.6 = (bf16[272,128]{1,0:T(8,128)(2,1)S(1)}, bf16[272,128]{1,0:T(8,128)(2,1)S(1)}, u32[]{:S(2)}, u32[]{:S(2)}) collective-permute-start(bf16[272,128]{1,0:T(8,128)(2,1)S(1)} %get-tuple-element.55.refs_14_), channel_id=1, source_target_pairs={{0,6},{2,4},{4,2},{6,0},{8,14},{10,12},{12,10},{14,8},{16,22},{18,... | collective-permute-start | bytes 208904 | tf_op jit(solution)/shard_map/ppermute | solution.py:22
  10.8 4.5 %collective-permute-start.5 = (bf16[272,128]{1,0:T(8,128)(2,1)S(1)}, bf16[272,128]{1,0:T(8,128)(2,1)S(1)}, u32[]{:S(2)}, u32[]{:S(2)}) collective-permute-start(bf16[272,128]{1,0:T(8,128)(2,1)S(1)} %get-tuple-element.54.refs_12_), channel_id=1, source_target_pairs={{0,4},{2,6},{4,0},{6,2},{8,12},{10,14},{12,8},{14,10},{16,20},{18,... | collective-permute-start | bytes 208904 | tf_op jit(solution)/shard_map/ppermute | solution.py:22
  11.3 5.0 %collective-permute-start.4 = (bf16[272,128]{1,0:T(8,128)(2,1)S(1)}, bf16[272,128]{1,0:T(8,128)(2,1)S(1)}, u32[]{:S(2)}, u32[]{:S(2)}) collective-permute-start(bf16[272,128]{1,0:T(8,128)(2,1)S(1)} %get-tuple-element.53.refs_10_), channel_id=1, source_target_pairs={{0,2},{2,0},{4,6},{6,4},{8,10},{10,8},{12,14},{14,12},{16,18},{18,... | collective-permute-start | bytes 208904 | tf_op jit(solution)/shard_map/ppermute | solution.py:22
  11.4 8.4 %collective-permute-start.11 = (bf16[256,128]{1,0:T(8,128)(2,1)S(1)}, bf16[256,128]{1,0:T(8,128)(2,1)S(1)}, u32[]{:S(2)}, u32[]{:S(2)}) collective-permute-start(bf16[256,128]{1,0:T(8,128)(2,1)S(1)} %get-tuple-element.59.refs_15_), channel_id=1, source_target_pairs={{0,6},{2,4},{4,2},{6,0},{8,14},{10,12},{12,10},{14,8},{16,22},{18,... | collective-permute-start | bytes 196616 | tf_op jit(solution)/shard_map/ppermute | solution.py:22
  14.3 5.6 %collective-permute-start.10 = (bf16[256,128]{1,0:T(8,128)(2,1)S(1)}, bf16[256,128]{1,0:T(8,128)(2,1)S(1)}, u32[]{:S(2)}, u32[]{:S(2)}) collective-permute-start(bf16[256,128]{1,0:T(8,128)(2,1)S(1)} %get-tuple-element.58.refs_13_), channel_id=1, source_target_pairs={{0,4},{2,6},{4,0},{6,2},{8,12},{10,14},{12,8},{14,10},{16,20},{18,... | collective-permute-start | bytes 196616 | tf_op jit(solution)/shard_map/ppermute | solution.py:22
  14.8 5.1 %collective-permute-start.9 = (bf16[256,128]{1,0:T(8,128)(2,1)S(1)}, bf16[256,128]{1,0:T(8,128)(2,1)S(1)}, u32[]{:S(2)}, u32[]{:S(2)}) collective-permute-start(bf16[256,128]{1,0:T(8,128)(2,1)S(1)} %get-tuple-element.57.refs_11_), channel_id=1, source_target_pairs={{0,2},{2,0},{4,6},{6,4},{8,10},{10,8},{12,14},{14,12},{16,18},{18,... | collective-permute-start | bytes 196616 | tf_op jit(solution)/shard_map/ppermute | solution.py:22
  16.3 11.6 %collective-permute-start.7 = (bf16[1040,128]{1,0:T(8,128)(2,1)S(1)}, bf16[1040,128]{1,0:T(8,128)(2,1)S(1)}, u32[]{:S(2)}, u32[]{:S(2)}) collective-permute-start(bf16[1040,128]{1,0:T(8,128)(2,1)S(1)} %add_add_fusion.refs_4_.refs_0_), channel_id=1, source_target_pairs={{0,8},{2,10},{4,12},{6,14},{8,16},{10,18},{12,20},{14,22},{16,24},... | collective-permute-start | bytes 798728 | tf_op jit(solution)/shard_map/ppermute | solution.py:27
  19.9 14.0 %collective-permute-start.12 = (bf16[1024,128]{1,0:T(8,128)(2,1)S(1)}, bf16[1024,128]{1,0:T(8,128)(2,1)S(1)}, u32[]{:S(2)}, u32[]{:S(2)}) collective-permute-start(bf16[1024,128]{1,0:T(8,128)(2,1)S(1)} %bitcast.11), channel_id=1, source_target_pairs={{0,8},{2,10},{4,12},{6,14},{8,16},{10,18},{12,20},{14,22},{16,24},... | collective-permute-start | bytes 786440 | tf_op jit(solution)/shard_map/ppermute | solution.py:27
  24.3 7.0 %collective-permute-start.1 = (bf16[256,128]{1,0:T(8,128)(2,1)S(1)}, bf16[256,128]{1,0:T(8,128)(2,1)S(1)}, u32[]{:S(2)}, u32[]{:S(2)}) collective-permute-start(bf16[256,128]{1,0:T(8,128)(2,1)S(1)} %get-tuple-element.49), channel_id=1, source_target_pairs={{0,2},{2,0},{4,6},{6,4},{8,10},{10,8},{12,14},{14,12},{16,18},{18,... | collective-permute-start | bytes 196616 | tf_op jit(solution)/shard_map/ppermute | solution.py:22
  25.3 6.1 %collective-permute-start.2 = (bf16[256,128]{1,0:T(8,128)(2,1)S(1)}, bf16[256,128]{1,0:T(8,128)(2,1)S(1)}, u32[]{:S(2)}, u32[]{:S(2)}) collective-permute-start(bf16[256,128]{1,0:T(8,128)(2,1)S(1)} %get-tuple-element.50), channel_id=1, source_target_pairs={{0,4},{2,6},{4,0},{6,2},{8,12},{10,14},{12,8},{14,10},{16,20},{18,... | collective-permute-start | bytes 196616 | tf_op jit(solution)/shard_map/ppermute | solution.py:22
  26.5 5.2 %collective-permute-start.3 = (bf16[256,128]{1,0:T(8,128)(2,1)S(1)}, bf16[256,128]{1,0:T(8,128)(2,1)S(1)}, u32[]{:S(2)}, u32[]{:S(2)}) collective-permute-start(bf16[256,128]{1,0:T(8,128)(2,1)S(1)} %get-tuple-element.51), channel_id=1, source_target_pairs={{0,6},{2,4},{4,2},{6,0},{8,14},{10,12},{12,10},{14,8},{16,22},{18,... | collective-permute-start | bytes 196616 | tf_op jit(solution)/shard_map/ppermute | solution.py:22
  27.9 9.6 %collective-permute-start.8 = (bf16[1040,128]{1,0:T(8,128)(2,1)S(1)}, bf16[1040,128]{1,0:T(8,128)(2,1)S(1)}, u32[]{:S(2)}, u32[]{:S(2)}) collective-permute-start(bf16[1040,128]{1,0:T(8,128)(2,1)S(1)} %collective-permute-done.7.refs_5_.refs_1_), channel_id=1, source_target_pairs={{0,8},{2,10},{4,12},{6,14},{8,16},{10,18},{12,20},{14,22},{16,24},... | collective-permute-start | bytes 798728 | tf_op jit(solution)/shard_map/ppermute | solution.py:27
  33.9 7.6 %collective-permute-start.13 = (bf16[1024,128]{1,0:T(8,128)(2,1)S(1)}, bf16[1024,128]{1,0:T(8,128)(2,1)S(1)}, u32[]{:S(2)}, u32[]{:S(2)}) collective-permute-start(bf16[1024,128]{1,0:T(8,128)(2,1)S(1)} %collective-permute-done.12.refs_6_.refs_8_), channel_id=1, source_target_pairs={{0,8},{2,10},{4,12},{6,14},{8,16},{10,18},{12,20},{14,22},{16,24},... | collective-permute-start | bytes 786440 | tf_op jit(solution)/shard_map/ppermute | solution.py:27
  37.9 4.3 %collective-permute-start.14 = (bf16[256,128]{1,0:T(8,128)(2,1)S(1)}, bf16[256,128]{1,0:T(8,128)(2,1)S(1)}, u32[]{:S(2)}, u32[]{:S(2)}) collective-permute-start(bf16[256,128]{1,0:T(8,128)(2,1)S(1)} %get-tuple-element.70), channel_id=1, source_target_pairs={{0,2},{2,0},{4,6},{6,4},{8,10},{10,8},{12,14},{14,12},{16,18},{18,... | collective-permute-start | bytes 196616 | tf_op jit(solution)/shard_map/ppermute | solution.py:22
  39.1 4.7 %collective-permute-start.16 = (bf16[256,128]{1,0:T(8,128)(2,1)S(1)}, bf16[256,128]{1,0:T(8,128)(2,1)S(1)}, u32[]{:S(2)}, u32[]{:S(2)}) collective-permute-start(bf16[256,128]{1,0:T(8,128)(2,1)S(1)} %get-tuple-element.74), channel_id=1, source_target_pairs={{0,4},{2,6},{4,0},{6,2},{8,12},{10,14},{12,8},{14,10},{16,20},{18,... | collective-permute-start | bytes 196616 | tf_op jit(solution)/shard_map/ppermute | solution.py:22
  39.9 5.9 %collective-permute-start.18 = (bf16[256,128]{1,0:T(8,128)(2,1)S(1)}, bf16[256,128]{1,0:T(8,128)(2,1)S(1)}, u32[]{:S(2)}, u32[]{:S(2)}) collective-permute-start(bf16[256,128]{1,0:T(8,128)(2,1)S(1)} %get-tuple-element.79), channel_id=1, source_target_pairs={{0,6},{2,4},{4,2},{6,0},{8,14},{10,12},{12,10},{14,8},{16,22},{18,... | collective-permute-start | bytes 196616 | tf_op jit(solution)/shard_map/ppermute | solution.py:22
  42.2 6.0 %collective-permute-start.15 = (bf16[512,128]{1,0:T(8,128)(2,1)S(1)}, bf16[512,128]{1,0:T(8,128)(2,1)S(1)}, u32[]{:S(2)}, u32[]{:S(2)}) collective-permute-start(bf16[512,128]{1,0:T(8,128)(2,1)S(1)} %get-tuple-element.71), channel_id=1, source_target_pairs={{0,2},{2,0},{4,6},{6,4},{8,10},{10,8},{12,14},{14,12},{16,18},{18,... | collective-permute-start | bytes 393224 | tf_op jit(solution)/shard_map/ppermute | solution.py:22
  43.8 5.6 %collective-permute-start.17 = (bf16[512,128]{1,0:T(8,128)(2,1)S(1)}, bf16[512,128]{1,0:T(8,128)(2,1)S(1)}, u32[]{:S(2)}, u32[]{:S(2)}) collective-permute-start(bf16[512,128]{1,0:T(8,128)(2,1)S(1)} %get-tuple-element.75), channel_id=1, source_target_pairs={{0,4},{2,6},{4,0},{6,2},{8,12},{10,14},{12,8},{14,10},{16,20},{18,... | collective-permute-start | bytes 393224 | tf_op jit(solution)/shard_map/ppermute | solution.py:22
  45.8 5.9 %collective-permute-start.19 = (bf16[512,128]{1,0:T(8,128)(2,1)S(1)}, bf16[512,128]{1,0:T(8,128)(2,1)S(1)}, u32[]{:S(2)}, u32[]{:S(2)}) collective-permute-start(bf16[512,128]{1,0:T(8,128)(2,1)S(1)} %get-tuple-element.80), channel_id=1, source_target_pairs={{0,6},{2,4},{4,2},{6,0},{8,14},{10,12},{12,10},{14,8},{16,22},{18,... | collective-permute-start | bytes 393224 | tf_op jit(solution)/shard_map/ppermute | solution.py:22
